TPU v7x, 32 devices: a whole 2x2x4 slice. The times are simulated.
32 devices in a mesh: dp: 4 (over z), fsdp: 8 (over y, x, core).
Axes of the slice: x: 2, y: 2, z: 4, core: 2. Of those that a mesh axis runs over, the one named last changes fastest.
Arguments:
- hidden: bfloat16 [65536, 768], P(('dp', 'fsdp')), may hold values from -6 to 6
- long_flags: int32 [128], P(('dp', 'fsdp')), may hold values 0 or 1
- norm1_gain: float32 [768], P(('dp', 'fsdp')), may hold values from 0.1 to 1.9
- query_w: float32 [768, 768], P(('dp', 'fsdp')), may hold values from -0.0546875 to 0.0546875
- key_w: float32 [768, 768], P(('dp', 'fsdp')), may hold values from -0.21875 to 0.21875
- value_w: float32 [768, 768], P(('dp', 'fsdp')), may hold values from -0.21875 to 0.21875
- out_w: float32 [768, 768], P(None, ('dp', 'fsdp')), may hold values from -0.875 to 0.875
- bias_table: float32 [32, 12], replicated, may hold values from -4 to 4
- norm2_gain: float32 [768], P(('dp', 'fsdp')), may hold values from 0.1 to 1.9
- ffn_in: float32 [768, 3072], P(('dp', 'fsdp')), may hold values from -0.21875 to 0.21875
- ffn_out: float32 [3072, 768], P(None, ('dp', 'fsdp')), may hold values from -0.109375 to 0.109375
- out_grad: bfloat16 [65536, 768], P(('dp', 'fsdp')), may hold values from -6 to 6
Outputs:
- output: bfloat16 [65536, 768], P(('dp', 'fsdp'))
- input_grad: bfloat16 [65536, 768], P(('dp', 'fsdp'))
- norm1_gain_grad: float32 [768], P(('dp', 'fsdp'))
- query_grad: float32 [768, 768], P(('dp', 'fsdp'))
- key_grad: float32 [768, 768], P(('dp', 'fsdp'))
- value_grad: float32 [768, 768], P(('dp', 'fsdp'))
- out_proj_grad: float32 [768, 768], P(None, ('dp', 'fsdp'))
- table_grad: float32 [32, 12], replicated
- norm2_gain_grad: float32 [768], P(('dp', 'fsdp'))
- ffn_in_grad: float32 [768, 3072], P(('dp', 'fsdp'))
- ffn_out_grad: float32 [3072, 768], P(None, ('dp', 'fsdp'))
Inputs may be any that keep to these rules, and one draw needn't show every extreme that they name: `long_flags`: 1 where the 512 slots of a block hold one passage of 500 tokens, 0 where they hold two passages of 250 tokens; the slots after the passages are padding that forms a segment of its own.
All inputs are finite; a program needn't handle non-finite values.
Results may differ from a plain program's by a relative error of at most 0.013.
The roundings to bfloat16 on the way count: a program that leaves them out, or rounds other values in their place, can miss the bound.
Values may be sent and summed in bfloat16 or wider, within the bound.
No kernel may reach another device: no remote copies, remote signals or barrier semaphores. Data moves between devices by JAX's collectives and lax.ppermute only.
A program may use at most 256 MiB of HBM per device.

v0:
```python
import math

import jax
import jax.numpy as jnp
from jax import lax
from jax.sharding import PartitionSpec as P

HEADS = 12
HEAD_DIM = 64
BUCKETS = 32
MAX_DIST = 128
BLOCK = 512
LONG = 500
SHORT = 250


norm_eps = 1e-06
masked_score = -1000000000.0


def bucket_limits():
    exact_count = BUCKETS // 4
    half_count = BUCKETS // 2
    scale_log = math.log(MAX_DIST / exact_count)
    thresholds = []
    for target in range(1, half_count - exact_count):
        distance = exact_count
        while (
            int(math.log(distance / exact_count) / scale_log * (half_count - exact_count)) < target
        ):
            distance += 1
        thresholds.append(distance)
    return thresholds


def bucket_grid():
    slot_ids = jnp.arange(BLOCK, dtype=jnp.int32)
    relative = slot_ids[None, :] - slot_ids[:, None]
    distance = jnp.abs(relative)
    exact_count = BUCKETS // 4
    beyond = jnp.full_like(distance, exact_count)
    for threshold in bucket_limits():
        beyond = beyond + (distance >= threshold).astype(jnp.int32)
    inside = jnp.where(distance < exact_count, distance, beyond)
    return inside + (relative > 0).astype(jnp.int32) * (BUCKETS // 2)


def segment_mask(long_flag):
    slot_ids = jnp.arange(BLOCK, dtype=jnp.int32)
    long_ids = (slot_ids >= LONG).astype(jnp.int32)
    short_ids = (slot_ids >= SHORT).astype(jnp.int32) + (slot_ids >= 2 * SHORT).astype(jnp.int32)
    segment = jnp.where(long_flag == 1, long_ids, short_ids)
    return segment[:, None] == segment[None, :]


def rms_scale(values):
    return lax.rsqrt(jnp.mean(values * values, axis=-1, keepdims=True) + norm_eps)


def norm_piece(values, gain_full):
    return values * rms_scale(values) * gain_full


def smooth_gate(values):
    return jax.nn.gelu(values, approximate=False)


def project(left, right):
    return jnp.dot(left, right, preferred_element_type=jnp.float32)


def project_back(left, right):
    return lax.dot_general(
        left, right, (((1,), (1,)), ((), ())), preferred_element_type=jnp.float32
    )


def weight_grad(left, right):
    return lax.dot_general(
        left, right, (((0,), (0,)), ((), ())), preferred_element_type=jnp.float32
    )


def unit_scores(queries, key_heads, position_bias, long_flag):
    scores = (
        jnp.einsum("ihd,jhd->hij", queries, key_heads, preferred_element_type=jnp.float32)
        + position_bias
    )
    return jnp.where(segment_mask(long_flag)[None], scores, masked_score)


def attend_forward(queries, key_heads, value_heads, position_bias, long_flags):

    def one_unit(packed):
        unit_q, unit_k, unit_v, long_flag = packed
        masked = unit_scores(unit_q, unit_k, position_bias, long_flag)
        row_top = jnp.max(masked, axis=-1, keepdims=True)
        exp_scores = jnp.exp(masked - row_top)
        row_total = jnp.sum(exp_scores, axis=-1, keepdims=True)
        attn_probs = (exp_scores / row_total).astype(jnp.bfloat16)
        attended = jnp.einsum(
            "hij,jhd->ihd", attn_probs, unit_v, preferred_element_type=jnp.float32
        )
        return (attended.astype(jnp.bfloat16), row_top + jnp.log(row_total))

    return lax.map(one_unit, (queries, key_heads, value_heads, long_flags))


def attend_backward(
    queries, key_heads, value_heads, grad_attended, log_total, position_bias, onehot_low, long_flags
):

    def one_unit(packed):
        unit_q, unit_k, unit_v, unit_grad, unit_log, long_flag = packed
        masked = unit_scores(unit_q, unit_k, position_bias, long_flag)
        attn_probs = jnp.exp(masked - unit_log)
        probs_low = attn_probs.astype(jnp.bfloat16)
        grad_v = jnp.einsum(
            "hij,ihd->jhd", probs_low, unit_grad, preferred_element_type=jnp.float32
        )
        grad_p = jnp.einsum("ihd,jhd->hij", unit_grad, unit_v, preferred_element_type=jnp.float32)
        row_dot = jnp.sum(attn_probs * grad_p, axis=-1, keepdims=True)
        grad_s = (attn_probs * (grad_p - row_dot)).astype(jnp.bfloat16)
        grad_q = jnp.einsum("hij,jhd->ihd", grad_s, unit_k, preferred_element_type=jnp.float32)
        grad_k = jnp.einsum("hij,ihd->jhd", grad_s, unit_q, preferred_element_type=jnp.float32)
        grad_table = jnp.einsum(
            "hij,ijb->bh", grad_s, onehot_low, preferred_element_type=jnp.float32
        )
        return (
            grad_q.astype(jnp.bfloat16),
            grad_k.astype(jnp.bfloat16),
            grad_v.astype(jnp.bfloat16),
            grad_table,
        )

    return lax.map(
        one_unit, (queries, key_heads, value_heads, grad_attended, log_total, long_flags)
    )


def body(
    hidden,
    long_flags,
    norm1_gain,
    query_w,
    key_w,
    value_w,
    out_w,
    bias_table,
    norm2_gain,
    ffn_in,
    ffn_out,
    out_grad,
):
    width = hidden.shape[1]
    unit_count = hidden.shape[0] // BLOCK
    gain_one, weight_q, weight_k, weight_v, weight_o = (
        lax.all_gather(norm1_gain.astype(jnp.bfloat16), ("dp", "fsdp"), axis=0, tiled=True),
        lax.all_gather(query_w.astype(jnp.bfloat16), ("dp", "fsdp"), axis=0, tiled=True),
        lax.all_gather(key_w.astype(jnp.bfloat16), ("dp", "fsdp"), axis=0, tiled=True),
        lax.all_gather(value_w.astype(jnp.bfloat16), ("dp", "fsdp"), axis=0, tiled=True),
        lax.all_gather(out_w.astype(jnp.bfloat16), ("dp", "fsdp"), axis=1, tiled=True),
    )
    bucket_ids = bucket_grid()
    onehot = (bucket_ids[:, :, None] == jnp.arange(BUCKETS, dtype=jnp.int32)[None, None, :]).astype(
        jnp.float32
    )
    position_bias = jnp.einsum("ijb,bh->hij", onehot, bias_table, precision=lax.Precision.HIGHEST)
    residual_in = hidden.astype(jnp.float32)
    normed = norm_piece(residual_in, gain_one.astype(jnp.float32)).astype(jnp.bfloat16)
    queries = (
        project(normed, weight_q).astype(jnp.bfloat16).reshape(unit_count, BLOCK, HEADS, HEAD_DIM)
    )
    key_heads = (
        project(normed, weight_k).astype(jnp.bfloat16).reshape(unit_count, BLOCK, HEADS, HEAD_DIM)
    )
    value_heads = (
        project(normed, weight_v).astype(jnp.bfloat16).reshape(unit_count, BLOCK, HEADS, HEAD_DIM)
    )
    attended, log_total = attend_forward(queries, key_heads, value_heads, position_bias, long_flags)
    attended = attended.reshape(-1, width)
    middle = residual_in + project(attended, weight_o)
    gain_two, weight_in, weight_out = (
        lax.all_gather(norm2_gain.astype(jnp.bfloat16), ("dp", "fsdp"), axis=0, tiled=True),
        lax.all_gather(ffn_in.astype(jnp.bfloat16), ("dp", "fsdp"), axis=0, tiled=True),
        lax.all_gather(ffn_out.astype(jnp.bfloat16), ("dp", "fsdp"), axis=1, tiled=True),
    )
    normed_two = norm_piece(middle, gain_two.astype(jnp.float32)).astype(jnp.bfloat16)
    ffn_inner = project(normed_two, weight_in)
    activated = smooth_gate(ffn_inner).astype(jnp.bfloat16)
    output = (middle + project(activated, weight_out)).astype(jnp.bfloat16)
    gain_two, weight_in, weight_out = (
        lax.all_gather(norm2_gain.astype(jnp.bfloat16), ("dp", "fsdp"), axis=0, tiled=True),
        lax.all_gather(ffn_in.astype(jnp.bfloat16), ("dp", "fsdp"), axis=0, tiled=True),
        lax.all_gather(ffn_out.astype(jnp.bfloat16), ("dp", "fsdp"), axis=1, tiled=True),
    )
    grad_w_out = weight_grad(activated, out_grad)
    grad_act = project_back(out_grad, weight_out)
    gate_pull = jax.vjp(smooth_gate, ffn_inner)[1]
    grad_inner = gate_pull(grad_act)[0].astype(jnp.bfloat16)
    grad_w_in = weight_grad(normed_two, grad_inner)
    grad_normed_two = project_back(grad_inner, weight_in)
    norm_two_pull = jax.vjp(norm_piece, middle, gain_two.astype(jnp.float32))[1]
    grad_middle_part, grad_gain_two = norm_two_pull(grad_normed_two)
    grad_middle = out_grad.astype(jnp.float32) + grad_middle_part
    ffn_sums = (
        lax.psum_scatter(grad_gain_two, ("dp", "fsdp"), scatter_dimension=0, tiled=True),
        lax.psum_scatter(grad_w_in, ("dp", "fsdp"), scatter_dimension=0, tiled=True),
        lax.psum_scatter(grad_w_out, ("dp", "fsdp"), scatter_dimension=1, tiled=True),
    )
    gain_one, weight_q, weight_k, weight_v, weight_o = (
        lax.all_gather(norm1_gain.astype(jnp.bfloat16), ("dp", "fsdp"), axis=0, tiled=True),
        lax.all_gather(query_w.astype(jnp.bfloat16), ("dp", "fsdp"), axis=0, tiled=True),
        lax.all_gather(key_w.astype(jnp.bfloat16), ("dp", "fsdp"), axis=0, tiled=True),
        lax.all_gather(value_w.astype(jnp.bfloat16), ("dp", "fsdp"), axis=0, tiled=True),
        lax.all_gather(out_w.astype(jnp.bfloat16), ("dp", "fsdp"), axis=1, tiled=True),
    )
    grad_branch = grad_middle.astype(jnp.bfloat16)
    grad_w_o = weight_grad(attended, grad_branch)
    grad_attended = (
        project_back(grad_branch, weight_o)
        .astype(jnp.bfloat16)
        .reshape(unit_count, BLOCK, HEADS, HEAD_DIM)
    )
    grad_q, grad_k, grad_v, table_parts = attend_backward(
        queries,
        key_heads,
        value_heads,
        grad_attended,
        log_total,
        position_bias,
        onehot.astype(jnp.bfloat16),
        long_flags,
    )
    grad_q = grad_q.reshape(-1, width)
    grad_k = grad_k.reshape(-1, width)
    grad_v = grad_v.reshape(-1, width)
    grad_w_q = weight_grad(normed, grad_q)
    grad_w_k = weight_grad(normed, grad_k)
    grad_w_v = weight_grad(normed, grad_v)
    grad_normed = (
        project_back(grad_q, weight_q)
        + project_back(grad_k, weight_k)
        + project_back(grad_v, weight_v)
    )
    norm_one_pull = jax.vjp(norm_piece, residual_in, gain_one.astype(jnp.float32))[1]
    grad_in_part, grad_gain_one = norm_one_pull(grad_normed)
    input_grad = (grad_middle + grad_in_part).astype(jnp.bfloat16)
    table_grad = lax.psum(jnp.sum(table_parts, axis=0), ("dp", "fsdp"))
    attention_sums = (
        lax.psum_scatter(grad_gain_one, ("dp", "fsdp"), scatter_dimension=0, tiled=True),
        lax.psum_scatter(grad_w_q, ("dp", "fsdp"), scatter_dimension=0, tiled=True),
        lax.psum_scatter(grad_w_k, ("dp", "fsdp"), scatter_dimension=0, tiled=True),
        lax.psum_scatter(grad_w_v, ("dp", "fsdp"), scatter_dimension=0, tiled=True),
        lax.psum_scatter(grad_w_o, ("dp", "fsdp"), scatter_dimension=1, tiled=True),
    )
    gain_one_grad, query_grad, key_grad, value_grad, out_proj_grad = attention_sums
    gain_two_grad, ffn_in_grad, ffn_out_grad = ffn_sums
    return (
        output,
        input_grad,
        gain_one_grad,
        query_grad,
        key_grad,
        value_grad,
        out_proj_grad,
        table_grad,
        gain_two_grad,
        ffn_in_grad,
        ffn_out_grad,
    )


def solution(mesh):
    return jax.shard_map(
        body,
        mesh=mesh,
        in_specs=(
            P(("dp", "fsdp"), None),
            P(("dp", "fsdp")),
            P(("dp", "fsdp")),
            P(("dp", "fsdp"), None),
            P(("dp", "fsdp"), None),
            P(("dp", "fsdp"), None),
            P(None, ("dp", "fsdp")),
            P(),
            P(("dp", "fsdp")),
            P(("dp", "fsdp"), None),
            P(None, ("dp", "fsdp")),
            P(("dp", "fsdp"), None),
        ),
        out_specs=(
            P(("dp", "fsdp"), None),
            P(("dp", "fsdp"), None),
            P(("dp", "fsdp")),
            P(("dp", "fsdp"), None),
            P(("dp", "fsdp"), None),
            P(("dp", "fsdp"), None),
            P(None, ("dp", "fsdp")),
            P(),
            P(("dp", "fsdp")),
            P(("dp", "fsdp"), None),
            P(None, ("dp", "fsdp")),
        ),
        check_vma=False,
    )
```

profile of v0, /device:TPU:0, one launch (start us, length us, event | category | flops | bytes accessed | tf_op | source)
XLA Modules:
  0.0 1333.5 jit_solution(4426170745100787124)
XLA Ops:
  23.8 42.3 %all-reduce.5 = (bf16[768]{0:T(1024)(128)(2,1)S(1)}, bf16[768]{0:T(1024)(128)(2,1)S(1)}) all-reduce(bf16[768]{0:T(1024)(128)(2,1)S(1)} %dynamic-update-slice, bf16[768]{0:T(1024)(128)(2,1)S(1)} %dynamic-update-slice.1), channel_id=1, replica_groups=mesh['dp'=4,'fsdp'=8] {'dp','fsdp'}, use_global_device_ids=true, to_apply=%add | all-reduce | flops 1536 | bytes 6144
  66.1 14.9 %fusion.62 = f32[12,512,512]{2,0,1:T(8,128)} fusion(s32[512,512]{1,0:T(8,128)} %fusion.75, f32[32,12]{0,1:T(8,128)S(1)} %copy-done), kind=kOutput, calls=%fused_computation.94 | convolution fusion | flops 1216348160 | bytes 13633024 | tf_op jit(solution)/shard_map/ijb,bh->hij/dot_general | solution.py:168
  81.0 17.7 %copy.91 = f32[12,512,512]{1,2,0:T(8,128)} copy(f32[12,512,512]{2,0,1:T(8,128)} %fusion.62) | data formatting | bytes 25165824 | tf_op jit(solution)/shard_map/while | solution.py:106
  140.7 40.6 %all-gather.11.cloned.1.call-done = bf16[768,768]{1,0:T(8,128)(2,1)} async-done(((bf16[24,768]{1,0:T(8,128)(2,1)}), bf16[768,768]{1,0:T(8,128)(2,1)}) %all-gather.11.cloned.1.call-update) | async-done | bytes 1179664 | tf_op jit(solution)/shard_map/all_gather | solution.py:160
  205.2 58.3 %while.29 = (s32[]{:T(128)}, bf16[4,512,12,64]{1,3,2,0:T(8,128)(2,1)}, f32[4,12,512,1]{2,1,3,0:T(8,128)}, bf16[4,512,12,64]{1,3,2,0:T(8,128)(2,1)}, s32[4]{0:T(1...) while((s32[]{:T(128)}, ...), condition=%wide.region_4.5_spmd, body=%wide.region_1.4_spmd.sunk | while | flops 831124480 | bytes 54213240 | solution.py:106
  280.2 23.4 %all-gather.15.cloned.1.call-done = bf16[768,3072]{1,0:T(8,128)(2,1)} async-done(((bf16[24,3072]{1,0:T(8,128)(2,1)}), bf16[768,3072]{1,0:T(8,128)(2,1)}) %all-gather.15.cloned.1.call-update) | async-done | bytes 4718608 | tf_op jit(solution)/shard_map/all_gather | solution.py:185
  303.6 70.1 %multiply_convert_fusion.1 = (bf16[2048,3072]{1,0:T(8,128)(2,1)}, f32[2048,3072]{1,0:T(8,128)}, f32[2048,3072]{1,0:T(8,128)}) fusion(bf16[768,3072]{1,0:T(8,128)(2,1)} %all-gather.15.cloned.1.call-done, f32[2048,768]{0,1:T(8,128)} %get-tuple-element.313, f32[768]{0:T(1024)S(1)} %copy-done.31, f32[2048]{0:T(1024)S(1)} %fusion.87), kind=kOutput, calls=%fused_computation.72 | convolution fusion | flops 10077339648 | bytes 73935872 | tf_op jit(solution)/shard_map/dot_general | solution.py:69
  373.7 27.8 %add_convert_fusion = bf16[2048,3072]{1,0:T(8,128)(2,1)} fusion(f32[2048,3072]{1,0:T(8,128)} %get-tuple-element.307, f32[2048,3072]{1,0:T(8,128)} %get-tuple-element.314, bf16[2048,768]{1,0:T(8,128)(2,1)S(1)} %copy-done.15, bf16[3072,768]{0,1:T(8,128)(2,1)} %all-gather.17.cloned.1.call-done), kind=kOutput, calls=%fused_computation.71 | convolution fusion | flops 9751756800 | bytes 70778880 | tf_op jit(solution)/shard_map/dot_general | solution.py:73
  401.4 16.6 %multiply_reduce_fusion.1 = (f32[768]{0:T(1024)}, f32[2048]{0:T(1024)S(1)}, f32[2048,768]{0,1:T(8,128)S(1)}) fusion(f32[2048,768]{0,1:T(8,128)} %get-tuple-element.313, f32[2048]{0:T(1024)S(1)} %fusion.87, f32[768]{0:T(1024)S(1)} %copy-done.31, bf16[2048,3072]{1,0:T(8,128)(2,1)} %add_convert_fusion, bf16[768,3072]{1,0:T(8,128)(2,1)} %all-gather.15.cloned.1.call-done), kind=kOutput, calls=%fused_computation.104 | convolution fusion | flops 9673110528 | bytes 29906944 | tf_op jit(solution)/shard_map/dot_general | solution.py:73
  450.6 274.7 %while.30 = (s32[]{:T(128)}, bf16[4,512,12,64]{1,3,2,0:T(8,128)(2,1)}, bf16[4,512,12,64]{1,3,2,0:T(8,128)(2,1)}, bf16[4,512,12,64]{1,3,2,0:T(8,128)(2,1)}, f32[4...) while((s32[]{:T(128)}, ...), condition=%wide.region_9.10_spmd.clone, body=%wide.region_7.9_spmd.clone.sunk | while | flops 2269508608 | bytes 271721920 | solution.py:136
  460.9 11.1 multiply_reduce_fusion.5
  486.1 14.6 %copy.125 = bf16[12,512,512]{2,0,1:T(8,128)(2,1)} copy(bf16[12,512,512]{1,2,0:T(8,128)(2,1)} %multiply_convert_fusion.6) | data formatting | bytes 12582912 | tf_op jit(solution)/shard_map/while/body/eval_jaxpr/convert_element_type | solution.py:123
  554.9 14.5 %copy.125 = bf16[12,512,512]{2,0,1:T(8,128)(2,1)} copy(bf16[12,512,512]{1,2,0:T(8,128)(2,1)} %multiply_convert_fusion.6) | data formatting | bytes 12582912 | tf_op jit(solution)/shard_map/while/body/eval_jaxpr/convert_element_type | solution.py:123
  598.2 11.1 multiply_reduce_fusion.5
  623.4 14.5 %copy.125 = bf16[12,512,512]{2,0,1:T(8,128)(2,1)} copy(bf16[12,512,512]{1,2,0:T(8,128)(2,1)} %multiply_convert_fusion.6) | data formatting | bytes 12582912 | tf_op jit(solution)/shard_map/while/body/eval_jaxpr/convert_element_type | solution.py:123
  692.0 14.5 %copy.125 = bf16[12,512,512]{2,0,1:T(8,128)(2,1)} copy(bf16[12,512,512]{1,2,0:T(8,128)(2,1)} %multiply_convert_fusion.6) | data formatting | bytes 12582912 | tf_op jit(solution)/shard_map/while/body/eval_jaxpr/convert_element_type | solution.py:123
  759.5 17.2 %fusion.88 = f32[768,3072]{1,0:T(8,128)} fusion(bf16[2048,3072]{1,0:T(8,128)(2,1)} %add_convert_fusion, f32[2048,768]{0,1:T(8,128)} %get-tuple-element.313, f32[768]{0:T(1024)S(1)} %copy-done.32, f32[2048]{0:T(1024)S(1)} %copy-done.27), kind=kOutput, calls=%fused_computation.136 | convolution fusion | flops 9668395008 | bytes 28322816 | tf_op jit(solution)/shard_map/dot_general | solution.py:79
  776.9 16.1 %fusion.101 = f32[3072,768]{0,1:T(8,128)} fusion(bf16[2048,3072]{1,0:T(8,128)(2,1)} %get-tuple-element.306, bf16[2048,768]{1,0:T(8,128)(2,1)} %param.27), kind=kOutput, calls=%fused_computation.142 | convolution fusion | flops 9663676416 | bytes 25165824 | tf_op jit(solution)/shard_map/dot_general | solution.py:79
  806.7 40.1 %all-reduce.4 = (f32[768]{0:T(1024)S(1)}, f32[32,12]{0,1:T(8,128)}, f32[768]{0:T(1024)S(1)}) all-reduce(f32[768]{0:T(1024)S(1)} %get-tuple-element.257, f32[32,12]{0,1:T(8,128)S(1)} %reduce_sum.88, f32[768]{0:T(1024)S(1)} %copy-done.33), channel_id=2, replica_groups=mesh['dp'=4,'fsdp'=8] {'dp','fsdp'}, use_global_device_ids=true, to_apply=%region_12.13.clone | all-reduce | flops 1920 | bytes 15360
  859.8 15.4 %add_convert_fusion.1 = bf16[2048,768]{0,1:T(8,128)(2,1)S(1)} fusion(f32[2048,768]{0,1:T(8,128)} %get-tuple-element.313, bf16[2048,3072]{1,0:T(8,128)(2,1)} %get-tuple-element.306, bf16[3072,768]{0,1:T(8,128)(2,1)} %all-gather.17.cloned.1.call-done), kind=kOutput, calls=%fused_computation.107 | convolution fusion | flops 9666822144 | bytes 26738688 | tf_op jit(solution)/shard_map/dot_general | solution.py:69
  878.0 60.6 %reduce-scatter.7.cloned.1.call-done = f32[24,768]{1,0:T(8,128)} async-done(((f32[768,768]{1,0:T(8,128)}), f32[24,768]{1,0:T(8,128)}) %reduce-scatter.7.cloned.1.call-update) | async-done | bytes 73744 | tf_op jit(solution)/shard_map/reduce_scatter | solution.py:252
  938.6 104.6 %reduce-scatter.9.cloned.1.call-done = f32[24,768]{1,0:T(8,128)} async-done(((f32[768,768]{1,0:T(8,128)}), f32[24,768]{1,0:T(8,128)}) %reduce-scatter.9.cloned.1.call-update) | async-done | bytes 73744 | tf_op jit(solution)/shard_map/reduce_scatter | solution.py:253
  1043.2 141.2 %reduce-scatter.15.cloned.1.call-done = f32[24,3072]{1,0:T(8,128)} async-done(((f32[768,3072]{1,0:T(8,128)}), f32[24,3072]{1,0:T(8,128)}) %reduce-scatter.15.cloned.1.call-update) | async-done | bytes 294928 | tf_op jit(solution)/shard_map/reduce_scatter | solution.py:208
  1184.5 141.9 %reduce-scatter.17.cloned.1.call-done = f32[3072,24]{0,1:T(8,128)} async-done(((f32[3072,768]{0,1:T(8,128)}), f32[3072,24]{0,1:T(8,128)}) %reduce-scatter.17.cloned.1.call-update) | async-done | bytes 294928 | tf_op jit(solution)/shard_map/reduce_scatter | solution.py:209
  (319 shorter events, 441.9 us)
Async XLA Ops:
  7.2 58.9 %copy-start = (f32[32,12]{0,1:T(8,128)S(1)}, f32[32,12]{0,1:T(8,128)}, u32[]{:S(2)}) copy-start(f32[32,12]{0,1:T(8,128)} %param.23) | copy-start | bytes 4612
  7.2 96.8 %all-gather.7.cloned.1.call-start = ((), (), s32[]{:S(2)}) async-start(), calls=%async_computation.6 | async-start | bytes 1216512 | tf_op jit(solution)/shard_map/all_gather | solution.py:161
  8.8 116.0 %all-gather.9.cloned.1.call-start = ((), (), s32[]{:S(2)}) async-start(), calls=%async_computation.7 | async-start | bytes 1216512 | tf_op jit(solution)/shard_map/all_gather | solution.py:159
  10.4 170.9 %all-gather.11.cloned.1.call-start = ((), (), s32[]{:S(2)}) async-start(), calls=%async_computation.8 | async-start | bytes 1216512 | tf_op jit(solution)/shard_map/all_gather | solution.py:160
  12.0 259.7 %all-gather.13.cloned.1.call-start = ((), (), s32[]{:S(2)}) async-start(), calls=%async_computation.9 | async-start | bytes 1216512 | tf_op jit(solution)/shard_map/all_gather | solution.py:162
  13.5 290.0 %all-gather.15.cloned.1.call-start = ((), (), s32[]{:S(2)}) async-start(), calls=%async_computation.10 | async-start | bytes 4866048 | tf_op jit(solution)/shard_map/all_gather | solution.py:185
  15.3 358.4 %all-gather.17.cloned.1.call-start = ((), (), s32[]{:S(2)}) async-start(), calls=%async_computation.11 | async-start | bytes 4866048 | tf_op jit(solution)/shard_map/all_gather | solution.py:186
  17.0 861.0 %reduce-scatter.13.cloned.1.call-start = ((), (), s32[]{:S(2)}) async-start(), calls=%async_computation.15 | async-start | bytes 2433024 | tf_op jit(solution)/shard_map/reduce_scatter | solution.py:255
  21.6 103.2 %copy-start.4 = (bf16[2048,768]{0,1:T(8,128)(2,1)}, bf16[2048,768]{0,1:T(8,128)(2,1)S(1)}, u32[]{:S(2)}) copy-start(bf16[2048,768]{0,1:T(8,128)(2,1)S(1)} %copy.84) | copy-start | bytes 9437188
  23.3 158.0 %copy-start.22 = (f32[2048]{0:T(1024)}, f32[2048]{0:T(1024)S(1)}, u32[]{:S(2)}) copy-start(f32[2048]{0:T(1024)S(1)} %fusion.86) | copy-start | bytes 24580
  66.1 115.2 %copy-start.20 = (f32[768]{0:T(1024)}, f32[768]{0:T(1024)S(1)}, u32[]{:S(2)}) copy-start(f32[768]{0:T(1024)S(1)} %convert_element_type.234) | copy-start | bytes 9220
  271.7 31.9 %copy-start.31 = (f32[768]{0:T(1024)S(1)}, f32[768]{0:T(1024)}, u32[]{:S(2)}) copy-start(f32[768]{0:T(1024)} %convert_element_type.251) | copy-start | bytes 9220
  280.2 93.5 %copy-start.28 = (f32[2048]{0:T(1024)}, f32[2048]{0:T(1024)S(1)}, u32[]{:S(2)}) copy-start(f32[2048]{0:T(1024)S(1)} %get-tuple-element.312) | copy-start | bytes 24580
  280.2 137.8 %copy-start.26 = (f32[2048]{0:T(1024)}, f32[2048]{0:T(1024)S(1)}, u32[]{:S(2)}) copy-start(f32[2048]{0:T(1024)S(1)} %fusion.87) | copy-start | bytes 24580
  303.6 70.1 %copy-start.15 = (bf16[2048,768]{1,0:T(8,128)(2,1)S(1)}, bf16[2048,768]{1,0:T(8,128)(2,1)}, u32[]{:S(2)}) copy-start(bf16[2048,768]{1,0:T(8,128)(2,1)} %param.27) | copy-start | bytes 9437188
  427.2 450.8 %reduce-scatter.11.cloned.1.call-start = ((), (), s32[]{:S(2)}) async-start(), calls=%async_computation.14 | async-start | bytes 2433024 | tf_op jit(solution)/shard_map/reduce_scatter | solution.py:254
  486.1 21.5 %slice-start = ((s8[6291456]{0:T(1024)(128)(4,1)}), s8[2097152]{0:T(1024)(128)(4,1)S(1)}, s32[]{:S(2)}) async-start(s8[6291456]{0:T(1024)(128)(4,1)} %bitcast.180), calls=%async_computation.18 | async-start | bytes 4194304 | tf_op jit(solution)/shard_map/while
  554.9 21.5 %slice-start = ((s8[6291456]{0:T(1024)(128)(4,1)}), s8[2097152]{0:T(1024)(128)(4,1)S(1)}, s32[]{:S(2)}) async-start(s8[6291456]{0:T(1024)(128)(4,1)} %bitcast.180), calls=%async_computation.18 | async-start | bytes 4194304 | tf_op jit(solution)/shard_map/while
  736.5 202.1 %reduce-scatter.7.cloned.1.call-start = ((), (), s32[]{:S(2)}) async-start(), calls=%async_computation.12 | async-start | bytes 2433024 | tf_op jit(solution)/shard_map/reduce_scatter | solution.py:252
  747.7 295.5 %reduce-scatter.9.cloned.1.call-start = ((), (), s32[]{:S(2)}) async-start(), calls=%async_computation.13 | async-start | bytes 2433024 | tf_op jit(solution)/shard_map/reduce_scatter | solution.py:253
  759.4 425.1 %reduce-scatter.15.cloned.1.call-start = ((), (), s32[]{:S(2)}) async-start(), calls=%async_computation.16 | async-start | bytes 9732096 | tf_op jit(solution)/shard_map/reduce_scatter | solution.py:208
  776.7 549.7 %reduce-scatter.17.cloned.1.call-start = ((), (), s32[]{:S(2)}) async-start(), calls=%async_computation.17 | async-start | bytes 9732096 | tf_op jit(solution)/shard_map/reduce_scatter | solution.py:209
  800.8 47.2 %copy-start.25 = (f32[2048]{0:T(1024)S(1)}, f32[2048]{0:T(1024)}, u32[]{:S(2)}) copy-start(f32[2048]{0:T(1024)} %copy-done.24) | copy-start | bytes 24580
  859.8 466.6 %copy-start.1 = (f32[32,12]{0,1:T(8,128)S(1)}, f32[32,12]{0,1:T(8,128)}, u32[]{:S(2)}) copy-start(f32[32,12]{0,1:T(8,128)} %param.23) | copy-start | bytes 4612
  (60 other events, 518.1 us)
Sparse Core Ops, SparseCore 0:
  11.5 56.7 all-gather.6
  71.8 52.9 all-gather.8
  128.3 52.9 all-gather.10
  184.6 52.9 all-gather.12
  240.9 62.5 all-gather.14
  306.9 62.4 all-gather.16
  427.4 97.8 reduce-scatter.12
  736.7 97.8 reduce-scatter.10
  840.5 98.0 reduce-scatter.6
  945.2 98.0 reduce-scatter.8
  1049.7 134.6 reduce-scatter.14
  1191.8 134.5 reduce-scatter.16
where the time goes:
time: 1340 us; the launch traced here: 1330 us
  waiting for transfers between devices  513 us (38%)
  matrix products  435 us (32%)
  local copies, waits for them, and re-layouts  211 us (16%)
  blocking collectives  82.4 us (6%)
  other arithmetic  71.2 us (5%)
  between operations  14.9 us (1%)
    reduce_scatter x1, waiting for transfers between devices, body(): lax.psum_scatter(grad_w_out, ('dp', 'fsdp'), scatter_dimension=1, tiled=T...  142 us
    reduce_scatter x1, waiting for transfers between devices, body(): lax.psum_scatter(grad_w_in, ('dp', 'fsdp'), scatter_dimension=0, tiled=True)  141 us
    dot_general x6, matrix products, project(): return jnp.dot(left, right, preferred_element_type=jnp.float32)  112 us
    reduce_scatter x1, waiting for transfers between devices, body(): lax.psum_scatter(grad_w_k, ('dp', 'fsdp'), scatter_dimension=0, tiled=True)  105 us
    unnamed x2, blocking collectives  82.4 us
    dot_general x8, matrix products, unit_scores(): jnp.einsum('ihd,jhd->hij', queries, key_heads, preferred_element_type=jnp...  69.6 us
    dot_general x6, matrix products, project_back(): lax.dot_general(left, right, (((1,), (1,)), ((), ())), preferred_element_...  65.1 us
    reduce_scatter x1, waiting for transfers between devices, body(): lax.psum_scatter(grad_w_q, ('dp', 'fsdp'), scatter_dimension=0, tiled=True)  60.6 us
  transfers between devices with their start and end apart: 12, of which 7 were waited for; matrix products, arithmetic and copies ran while one was open for 48% of the time, Pallas kernels for 0%

commit v1 on v0

v1 whole, which is shorter than its diff:
```python
import math, functools
import jax, jax.numpy as jnp
from jax import lax
from jax.experimental import pallas as pl
from jax.experimental.pallas import tpu as pltpu
HEADS=12; HEAD_DIM=64; BUCKETS=32; MAX_DIST=128; BLOCK=512; LONG=500; SHORT=250
F32=jnp.float32; BF16=jnp.bfloat16
far=-2.0**30
NN=(((1,),(0,)),((),())); NT=(((1,),(1,)),((),())); TN=(((0,),(0,)),((),()))
def dot(a,b,dn=NN): return lax.dot_general(a,b,dn,preferred_element_type=F32)

def bucket_limits():
    exact_count = BUCKETS // 4
    half_count = BUCKETS // 2
    scale_log = math.log(MAX_DIST / exact_count)
    thresholds = []
    for target in range(1, half_count - exact_count):
        distance = exact_count
        while int(math.log(distance / exact_count) / scale_log * (half_count - exact_count)) < target:
            distance += 1
        thresholds.append(distance)
    return thresholds
def bucket_of(relative):
    distance=jnp.abs(relative)
    exact=BUCKETS//4
    beyond=jnp.full_like(distance,exact)
    for t in bucket_limits():
        beyond=beyond+jnp.where(distance>=t,1,0)
    inside=jnp.where(distance<exact,distance,beyond)
    return inside+jnp.where(relative>0,BUCKETS//2,0)

def bias_kernel(tT_ref, out_ref, ext_ref):
    h=pl.program_id(0)
    @pl.when(h==0)
    def _():
        t=lax.broadcasted_iota(jnp.int32,(1,2*BLOCK),1)
        rel=-jnp.where(t<BLOCK,t,t-2*BLOCK)
        b=bucket_of(rel)
        acc=jnp.zeros((HEADS,2*BLOCK),F32)
        for c in range(BUCKETS):
            acc=jnp.where(b==c,tT_ref[:,c:c+1],acc)
        ext_ref[...]=acc
    row=ext_ref[pl.ds(h,1),:]
    for s in range(4):
        x=jnp.broadcast_to(row,(128,2*BLOCK))
        y=pltpu.roll(x,128*s,axis=1,stride=1,stride_axis=0)
        out_ref[0,pl.ds(128*s,128),:]=y[:,:BLOCK]
def bias_call(table):
    return pl.pallas_call(bias_kernel,grid=(HEADS,),
        in_specs=[pl.BlockSpec((HEADS,BUCKETS),lambda h:(0,0))],
        out_specs=pl.BlockSpec((1,BLOCK,BLOCK),lambda h:(h,0,0)),
        out_shape=jax.ShapeDtypeStruct((HEADS,BLOCK,BLOCK),F32),
        scratch_shapes=[pltpu.VMEM((HEADS,2*BLOCK),F32)],name="bias")(table.T)

def seg_ids(flag):
    s=lax.broadcasted_iota(jnp.int32,(1,BLOCK),1)
    long_ids=jnp.where(s>=LONG,1,0)
    short_ids=jnp.where(s>=SHORT,1,0)+jnp.where(s>=2*SHORT,1,0)
    return jnp.where(flag==1,long_ids,short_ids)
def masks(flag):
    seg=seg_ids(flag)
    c=lax.broadcasted_iota(jnp.int32,(HEAD_DIM,BLOCK),0)
    qm=jnp.where(seg==c,1.0,0.0).astype(BF16)
    km=jnp.where((seg!=c)&(c<3),far,0.0).astype(BF16)
    return qm,km

def fwd_kernel(flags_ref,q_ref,k_ref,v_ref,bias_ref,o_ref,lse_ref,*,CH):
    n=pl.program_id(1)
    qm,km=masks(flags_ref[n])
    qa=jnp.concatenate([q_ref[...],qm],0)
    ka=jnp.concatenate([k_ref[...],km],0).T
    vT=v_ref[...]
    for c in range(BLOCK//CH):
        sl=slice(c*CH,(c+1)*CH)
        s=dot(ka,qa[:,sl])+bias_ref[0,:,sl]
        m=jnp.max(s,axis=0,keepdims=True)
        e=jnp.exp(s-m)
        l=jnp.sum(e,axis=0,keepdims=True)
        p=(e*(1.0/l)).astype(BF16)
        o_ref[:,sl]=dot(vT,p).astype(BF16)
        lse_ref[0,:,sl]=m+jnp.log(l)
def fwd_call(flags,qkvT,bias,CH=256):
    T=qkvT.shape[1]; n=T//BLOCK
    sp=lambda off: pl.BlockSpec((HEAD_DIM,BLOCK),lambda h,n,f:(h+off,n))
    return pl.pallas_call(functools.partial(fwd_kernel,CH=CH),
        grid_spec=pltpu.PrefetchScalarGridSpec(num_scalar_prefetch=1,grid=(HEADS,n),
        in_specs=[sp(0),sp(HEADS),sp(2*HEADS),pl.BlockSpec((1,BLOCK,BLOCK),lambda h,n,f:(h,0,0))],
        out_specs=[pl.BlockSpec((HEAD_DIM,BLOCK),lambda h,n,f:(h,n)),pl.BlockSpec((1,1,BLOCK),lambda h,n,f:(h,0,n))]),
        out_shape=[jax.ShapeDtypeStruct((HEADS*HEAD_DIM,T),BF16),jax.ShapeDtypeStruct((HEADS,1,T),F32)],
        name="attend",
        compiler_params=pltpu.CompilerParams(vmem_limit_bytes=48*2**20))(flags,qkvT,qkvT,qkvT,bias)

def bwd_kernel(flags_ref,q_ref,k_ref,v_ref,do_ref,lse_ref,bias_ref,dq_ref,dk_ref,dv_ref,tab_ref,acc_ref,*,CH,nb):
    n=pl.program_id(1)
    qm,km=masks(flags_ref[n])
    q=q_ref[...]; kT=k_ref[...]; doT=do_ref[...]
    qa=jnp.concatenate([q,qm],0)
    ka=jnp.concatenate([kT,km],0).T
    v=v_ref[...].T
    @pl.when(n==0)
    def _(): acc_ref[...]=jnp.zeros_like(acc_ref)
    dk=None; dv=None
    for c in range(BLOCK//CH):
        sl=slice(c*CH,(c+1)*CH)
        s=dot(ka,qa[:,sl])+bias_ref[0,:,sl]
        p=jnp.exp(s-lse_ref[0,:,sl])
        pb=p.astype(BF16)
        dvc=dot(doT[:,sl],pb,NT)
        dp=dot(v,doT[:,sl])
        t=p*dp
        d=jnp.sum(t,axis=0,keepdims=True)
        ds=(t-p*d).astype(BF16)
        dq_ref[:,sl]=dot(kT,ds).astype(BF16)
        dkc=dot(q[:,sl],ds,NT)
        dk=dkc if dk is None else dk+dkc
        dv=dvc if dv is None else dv+dvc
        acc_ref[:,sl]+=ds.astype(F32)
    dk_ref[...]=dk.astype(BF16); dv_ref[...]=dv.astype(BF16)
    @pl.when(n==nb-1)
    def _():
        tot=None
        zero=jnp.zeros((128,BLOCK),F32)
        for g in range(4):
            x=jnp.concatenate([acc_ref[pl.ds(128*g,128),:],zero],1)
            y=pltpu.roll(x,(2*BLOCK-128*g)%(2*BLOCK),axis=1,stride=2*BLOCK-1,stride_axis=0)
            r=jnp.sum(y,axis=0,keepdims=True)
            tot=r if tot is None else tot+r
        t=lax.broadcasted_iota(jnp.int32,(1,2*BLOCK),1)
        rel=-jnp.where(t<BLOCK,t,t-2*BLOCK)
        b=bucket_of(rel)
        cc=lax.broadcasted_iota(jnp.int32,(BUCKETS,2*BLOCK),0)
        tab_ref[0]=jnp.broadcast_to(jnp.sum(jnp.where(b==cc,tot,0.0),axis=1,keepdims=True),(BUCKETS,128))
def bwd_call(flags,qkvT,doT,lse,bias,CH=256):
    T=qkvT.shape[1]; n=T//BLOCK
    sp=lambda off: pl.BlockSpec((HEAD_DIM,BLOCK),lambda h,n,f:(h+off,n))
    D=HEADS*HEAD_DIM
    return pl.pallas_call(functools.partial(bwd_kernel,CH=CH,nb=n),
        grid_spec=pltpu.PrefetchScalarGridSpec(num_scalar_prefetch=1,grid=(HEADS,n),
        in_specs=[sp(0),sp(HEADS),sp(2*HEADS),sp(0),pl.BlockSpec((1,1,BLOCK),lambda h,n,f:(h,0,n)),pl.BlockSpec((1,BLOCK,BLOCK),lambda h,n,f:(h,0,0))],
        out_specs=[sp(0),sp(0),sp(0),pl.BlockSpec((1,BUCKETS,128),lambda h,n,f:(h,0,0))],
        scratch_shapes=[pltpu.VMEM((BLOCK,BLOCK),F32)]),
        out_shape=[jax.ShapeDtypeStruct((D,T),BF16)]*3+[jax.ShapeDtypeStruct((HEADS,BUCKETS,128),F32)],
        name="attend_back",
        compiler_params=pltpu.CompilerParams(vmem_limit_bytes=48*2**20))(flags,qkvT,qkvT,qkvT,doT,lse,bias)

def fwd2_kernel(flags_ref,q_ref,k_ref,v_ref,bias_ref,o_ref,lse_ref,*,HP,mode):
    n=pl.program_id(1)
    qm,km=masks(flags_ref[n])
    S=[]
    for u in range(HP):
        r=slice(u*64,(u+1)*64)
        qa=jnp.concatenate([q_ref[r,:],qm],0)
        ka=jnp.concatenate([k_ref[r,:],km],0).T
        S.append(dot(ka,qa))
    for u in range(HP):
        r=slice(u*64,(u+1)*64)
        s=S[u]+bias_ref[u]
        m=jnp.max(s,axis=0,keepdims=True)
        e=jnp.exp(s-m)
        if mode=="def":
            l=jnp.sum(e,axis=0,keepdims=True)
            o_ref[r,:]=(dot(v_ref[r,:],e.astype(BF16))*(1.0/l)).astype(BF16)
        elif mode=="ones":
            va=jnp.concatenate([v_ref[r,:],jnp.ones((16,BLOCK),BF16)],0)
            oa=dot(va,e.astype(BF16))
            l=oa[64:65,:]
            o_ref[r,:]=(oa[:64]*(1.0/l)).astype(BF16)
        elif mode=="nomm":
            l=jnp.sum(e,axis=0,keepdims=True)
            o_ref[r,:]=e[:64].astype(BF16)
        else:
            l=jnp.sum(e,axis=0,keepdims=True)
            p=(e*(1.0/l)).astype(BF16)
            o_ref[r,:]=dot(v_ref[r,:],p).astype(BF16)
        lse_ref[u,:,:]=m+jnp.log(l)
def fwd2_call(flags,qkvT,bias,HP=2,mode="norm"):
    T=qkvT.shape[1]; n=T//BLOCK
    G=HEADS//HP
    sp=lambda off: pl.BlockSpec((HP*HEAD_DIM,BLOCK),lambda h,n,f:(h+off,n))
    return pl.pallas_call(functools.partial(fwd2_kernel,HP=HP,mode=mode),
        grid_spec=pltpu.PrefetchScalarGridSpec(num_scalar_prefetch=1,grid=(G,n),
        in_specs=[sp(0),sp(G),sp(2*G),pl.BlockSpec((HP,BLOCK,BLOCK),lambda h,n,f:(h,0,0))],
        out_specs=[pl.BlockSpec((HP*HEAD_DIM,BLOCK),lambda h,n,f:(h,n)),pl.BlockSpec((HP,1,BLOCK),lambda h,n,f:(h,0,n))]),
        out_shape=[jax.ShapeDtypeStruct((HEADS*HEAD_DIM,T),BF16),jax.ShapeDtypeStruct((HEADS,1,T),F32)],
        name="attend",
        compiler_params=pltpu.CompilerParams(vmem_limit_bytes=56*2**20))(flags,qkvT,qkvT,qkvT,bias)
def fwdN_kernel(flags_ref,q_ref,k_ref,v_ref,bias_ref,o_ref,lse_ref,*,HP):
    n=pl.program_id(1)
    qm,km=masks(flags_ref[n])
    for u in range(HP):
        r=slice(u*64,(u+1)*64)
        qa=jnp.concatenate([q_ref[r,:],qm],0)
        ka=jnp.concatenate([k_ref[r,:],km],0).T
        s=dot(ka,qa)+bias_ref[u]
        m=jnp.max(s,axis=0,keepdims=True)
        e=jnp.exp(s-m)
        l=jnp.sum(e,axis=0,keepdims=True)
        o=lax.dot_general(e.astype(BF16),v_ref[r,:],(((0,),(1,)),((),())),preferred_element_type=F32)
        o_ref[r,:]=(o.T*(1.0/l)).astype(BF16)
        lse_ref[u,:,:]=m+jnp.log(l)

def left_by_row(x,width):
    row=lax.broadcasted_iota(jnp.int32,x.shape,0)
    for b in range(7):
        y=pltpu.roll(x,width-(1<<b),axis=1)
        x=jnp.where((row>>b)&1==1,y,x)
    return x
def bwd2_kernel(flags_ref,q_ref,k_ref,v_ref,do_ref,lse_ref,bias_ref,dq_ref,dk_ref,dv_ref,tab_ref,band_ref,far_ref,*,HP,nb,tabmode):
    n=pl.program_id(1)
    qm,km=masks(flags_ref[n])
    @pl.when(n==0)
    def _():
        band_ref[...]=jnp.zeros_like(band_ref); far_ref[...]=jnp.zeros_like(far_ref)
    R=[slice(u*64,(u+1)*64) for u in range(HP)]
    S=[];DP=[]
    for u in range(HP):
        r=R[u]
        qa=jnp.concatenate([q_ref[r,:],qm],0)
        ka=jnp.concatenate([k_ref[r,:],km],0).T
        S.append(dot(ka,qa))
        DP.append(dot(v_ref[r,:].T,do_ref[r,:]))
    for u in range(HP):
        r=R[u]
        p=jnp.exp(S[u]+bias_ref[u]-lse_ref[u])
        pb=p.astype(BF16)
        dv_ref[r,:]=dot(do_ref[r,:],pb,NT).astype(BF16)
        t=p*DP[u]
        d=jnp.sum(t,axis=0,keepdims=True)
        dsf=t-p*d
        ds=dsf.astype(BF16)
        dq_ref[r,:]=dot(k_ref[r,:],ds).astype(BF16)
        dk_ref[r,:]=dot(q_ref[r,:],ds,NT).astype(BF16)
        if tabmode:
            lo=None;hi=None;bl=[None]*3
            for g in range(4):
                for c in range(4):
                    tile=dsf[128*g:128*(g+1),128*c:128*(c+1)]
                    w=c-g+1
                    if 0<=w<3:
                        bl[w]=tile if bl[w] is None else bl[w]+tile
                    elif w<0:
                        lo=tile if lo is None else lo+tile
                    else:
                        hi=tile if hi is None else hi+tile
            for w in range(3): band_ref[u,:,128*w:128*(w+1)]+=bl[w]
            far_ref[u,0]+=jnp.sum(lo.reshape(16,8,128),axis=0)
            far_ref[u,1]+=jnp.sum(hi.reshape(16,8,128),axis=0)
    @pl.when(n==nb-1)
    def _():
        t=lax.broadcasted_iota(jnp.int32,(1,BLOCK),1)
        b=bucket_of(-jnp.where(t<384,t-128,t-640))
        cc=lax.broadcasted_iota(jnp.int32,(BUCKETS,BLOCK),0)
        c1=lax.broadcasted_iota(jnp.int32,(BUCKETS,128),0)
        for u in range(HP):
            x=jnp.concatenate([band_ref[u],jnp.zeros((128,128),F32)],1)
            tot=jnp.sum(left_by_row(x,BLOCK),axis=0,keepdims=True)
            lo=jnp.sum(far_ref[u,0],axis=0,keepdims=True); hi=jnp.sum(far_ref[u,1],axis=0,keepdims=True)
            val=jnp.where(b==cc,tot,0.0)
            val=val[:,:128]+val[:,128:256]+val[:,256:384]+val[:,384:]
            val=val+jnp.where(c1==BUCKETS-1,lo,0.0)+jnp.where(c1==BUCKETS//2-1,hi,0.0)
            tab_ref[u]=jnp.broadcast_to(jnp.sum(val,axis=1,keepdims=True),(BUCKETS,128))
def bwd2_call(flags,qkvT,doT,lse,bias,HP=2,tabmode=1):
    T=qkvT.shape[1]; n=T//BLOCK; G=HEADS//HP
    sp=lambda off: pl.BlockSpec((HP*HEAD_DIM,BLOCK),lambda h,n,f:(h+off,n))
    D=HEADS*HEAD_DIM
    return pl.pallas_call(functools.partial(bwd2_kernel,HP=HP,nb=n,tabmode=tabmode),
        grid_spec=pltpu.PrefetchScalarGridSpec(num_scalar_prefetch=1,grid=(G,n),
        in_specs=[sp(0),sp(G),sp(2*G),sp(0),pl.BlockSpec((HP,1,BLOCK),lambda h,n,f:(h,0,n)),pl.BlockSpec((HP,BLOCK,BLOCK),lambda h,n,f:(h,0,0))],
        out_specs=[sp(0),sp(0),sp(0),pl.BlockSpec((HP,BUCKETS,128),lambda h,n,f:(h,0,0))],
        scratch_shapes=[pltpu.VMEM((HP,128,384),F32),pltpu.VMEM((HP,2,8,128),F32)]),
        out_shape=[jax.ShapeDtypeStruct((D,T),BF16)]*3+[jax.ShapeDtypeStruct((HEADS,BUCKETS,128),F32)],
        name="attend_back",
        compiler_params=pltpu.CompilerParams(vmem_limit_bytes=60*2**20))(flags,qkvT,qkvT,qkvT,doT,lse,bias)

D=768
norm_eps=1e-6
def rms(x): return lax.rsqrt(jnp.mean(x*x,axis=-1,keepdims=True)+norm_eps)
GA=128
def row_of(gains,which):
    return gains.astype(F32).T[which:which+1,:]
def qkv_kernel(x_ref,w_ref,aT_ref,qkvT_ref,wT_ref):
    @pl.when(pl.program_id(0)==0)
    def _():
        for c in range(3):
            wT_ref[pl.ds(c*D,D),:]=w_ref[:,c*D:(c+1)*D].T
    x=x_ref[...].astype(F32)
    g=row_of(w_ref[:,3*D:3*D+GA],0)
    a=(x*rms(x)*g).astype(BF16)
    aT=a.T
    aT_ref[...]=aT
    qkvT_ref[...]=dot(wT_ref[...],aT).astype(BF16)
def qkv_call(x,w):
    T=x.shape[0]
    return pl.pallas_call(qkv_kernel,grid=(T//BLOCK,),
        in_specs=[pl.BlockSpec((BLOCK,D),lambda t:(t,0)),pl.BlockSpec(w.shape,lambda t:(0,0),pipeline_mode=pl.Buffered(1))],
        out_specs=[pl.BlockSpec((D,BLOCK),lambda t:(0,t)),pl.BlockSpec((3*D,BLOCK),lambda t:(0,t))],
        out_shape=[jax.ShapeDtypeStruct((D,T),BF16),jax.ShapeDtypeStruct((3*D,T),BF16)],
        scratch_shapes=[pltpu.VMEM((3*D,D),BF16)],name="project",
        compiler_params=pltpu.CompilerParams(vmem_limit_bytes=56*2**20))(x,w)
def mid_kernel(x_ref,oT_ref,wo_ref,ga_ref,m_ref,b_ref,bT_ref,*_):
    o=oT_ref[...].T
    m=x_ref[...].astype(F32)+dot(o,wo_ref[...],NT)
    m_ref[...]=m
    b=(m*rms(m)*row_of(ga_ref[...],1)).astype(BF16)
    b_ref[...]=b
    bT_ref[0]=b.T
def mid_call(x,oT,woT,gains):
    T=x.shape[0]
    return pl.pallas_call(mid_kernel,grid=(T//BLOCK,),
        in_specs=[pl.BlockSpec((BLOCK,D),lambda t:(t,0)),pl.BlockSpec((D,BLOCK),lambda t:(0,t)),
                  pl.BlockSpec((D,D),lambda t:(0,woT[1])),pl.BlockSpec((D,GA),lambda t:(0,gains[1]))],
        out_specs=[pl.BlockSpec((BLOCK,D),lambda t:(t,0)),pl.BlockSpec((BLOCK,D),lambda t:(t,0)),pl.BlockSpec((1,D,BLOCK),lambda t:(t,0,0))],
        out_shape=[jax.ShapeDtypeStruct((T,D),F32),jax.ShapeDtypeStruct((T,D),BF16),jax.ShapeDtypeStruct((T//BLOCK,D,BLOCK),BF16)],
        name="middle",
        compiler_params=pltpu.CompilerParams(vmem_limit_bytes=48*2**20))(x,oT,woT[0],gains[0])
def gate(u,mode):
    if mode=="erf":
        P=0.5*(1.0+lax.erf(u*(0.5**0.5)))
        z=jnp.exp(-0.5*u*u)
    else:
        z=jnp.exp(-0.5*u*u)
        t=1.0/(1.0+(0.3275911*0.5**0.5)*jnp.abs(u))
        q=((((0.5*1.061405429*t-0.5*1.453152027)*t+0.5*1.421413741)*t-0.5*0.284496736)*t+0.5*0.254829592)*t*z
        P=jnp.where(u>=0,1.0-q,q)
    return u*P, P+u*z*(2*math.pi)**-0.5
def ffn_kernel(b_ref,bT_ref,dy_ref,m_ref,win_ref,wout_ref,out_ref,db_ref,dwin_ref,dwout_ref,
               oacc,dacc,dyT,ain,aout,*,FC,SUB,nc,nt,mode,TB,order):
    c=pl.program_id(0); t=pl.program_id(1)
    rows=pl.ds(t*TB,TB)
    @pl.when(c==0)
    def _():
        oacc[rows,:]=m_ref[...]
        dacc[rows,:]=jnp.zeros((TB,D),F32)
        dyT[t]=dy_ref[rows,:].T
    b=b_ref[rows,:]; dy=dy_ref[rows,:]
    G=[];DU=[]
    U=[dot(b,win_ref[:,s*SUB:(s+1)*SUB]) for s in range(FC//SUB)]
    DG=[dot(dy,wout_ref[:,s*SUB:(s+1)*SUB]) for s in range(FC//SUB)]
    @pl.when(t==0)
    def _():
        ain[...]=jnp.zeros_like(ain); aout[...]=jnp.zeros_like(aout)
    for s in range(FC//SUB):
        g,pull=gate(U[s],mode)
        g=g.astype(BF16)
        du=(DG[s]*pull).astype(BF16)
        sl=slice(s*SUB,(s+1)*SUB)
        aout[:,sl]+=dot(dyT[t],g)
        ain[:,sl]+=dot(bT_ref[t],du)
        G.append(g);DU.append(du)
    g=jnp.concatenate(G,1);du=jnp.concatenate(DU,1)
    oacc[rows,:]+=dot(g,wout_ref[...],NT)
    dacc[rows,:]+=dot(du,win_ref[...],NT)
    @pl.when(t==nt-1)
    def _():
        dwin_ref[...]=ain[...].astype(BF16)
        dwout_ref[...]=aout[...].astype(BF16)
    @pl.when(c==nc-1)
    def _():
        out_ref[...]=oacc[rows,:].astype(BF16)
        db_ref[...]=dacc[rows,:]
def ffn_call(b,bT,dy,m,win,wout,FC=768,SUB=256,mode="erf",TB=512,order=0):
    T=b.shape[0]; nt=T//TB; FF=3072; nc=FF//FC
    bT3=bT
    last=lambda c,t:(jnp.where(c==nc-1,t,0),0)
    first=lambda c,t:(jnp.where(c==0,t,nt-1),0)
    one=pl.Buffered(1)
    return pl.pallas_call(functools.partial(ffn_kernel,FC=FC,SUB=SUB,nc=nc,nt=nt,mode=mode,TB=TB,order=order),grid=(nc,nt),
        in_specs=[pl.BlockSpec((T,D),lambda c,t:(0,0),pipeline_mode=one),pl.BlockSpec((nt,D,TB),lambda c,t:(0,0,0),pipeline_mode=one),
            pl.BlockSpec((T,D),lambda c,t:(0,0),pipeline_mode=one),
            pl.BlockSpec((TB,D),first),pl.BlockSpec((D,FC),lambda c,t:(0,c+win[1]*D//FC)),pl.BlockSpec((D,FC),lambda c,t:(0,c+wout[1]*D//FC))],
        out_specs=[pl.BlockSpec((TB,D),last),pl.BlockSpec((TB,D),last),pl.BlockSpec((D,FC),lambda c,t:(0,c)),pl.BlockSpec((D,FC),lambda c,t:(0,c))],
        out_shape=[jax.ShapeDtypeStruct((T,D),BF16),jax.ShapeDtypeStruct((T,D),F32),jax.ShapeDtypeStruct((D,FF),BF16),jax.ShapeDtypeStruct((D,FF),BF16)],
        scratch_shapes=[pltpu.VMEM((T,D),F32),pltpu.VMEM((T,D),F32),pltpu.VMEM((nt,D,TB),BF16),pltpu.VMEM((D,FC),F32),pltpu.VMEM((D,FC),F32)],
        name="feed_forward",
        compiler_params=pltpu.CompilerParams(vmem_limit_bytes=62*2**20))(b,bT3,dy,m,win[0],wout[0])

def post_kernel(dy_ref,db_ref,m_ref,oT_ref,wo_ref,ga_ref,dm_ref,doT_ref,dwo_ref,dg_ref,acc_ref,*,nt):
    t=pl.program_id(0)
    @pl.when(t==0)
    def _():
        acc_ref[...]=jnp.zeros_like(acc_ref); dg_ref[...]=jnp.zeros_like(dg_ref)
    m=m_ref[...]; db=db_ref[...]
    r=rms(m); n2=m*r
    dn=db*row_of(ga_ref[...],1)
    dg_ref[...]+=jnp.sum(db*n2,axis=0,keepdims=True)
    dm=dy_ref[...].astype(F32)+r*(dn-n2*jnp.mean(dn*n2,axis=-1,keepdims=True))
    dm_ref[...]=dm
    dmb=dm.astype(BF16)
    acc_ref[...]+=dot(dmb.T,oT_ref[...],NT)
    doT_ref[...]=dot(dmb,wo_ref[...]).astype(BF16).T
    @pl.when(t==nt-1)
    def _(): dwo_ref[...]=acc_ref[...].astype(BF16)
def post_call(dy,db,m,oT,woT,gains):
    T=dy.shape[0]; nt=T//BLOCK
    row=pl.BlockSpec((BLOCK,D),lambda t:(t,0)); col=pl.BlockSpec((D,BLOCK),lambda t:(0,t))
    return pl.pallas_call(functools.partial(post_kernel,nt=nt),grid=(nt,),
        in_specs=[row,row,row,col,pl.BlockSpec((D,D),lambda t:(0,woT[1])),pl.BlockSpec((D,GA),lambda t:(0,gains[1]))],
        out_specs=[row,col,pl.BlockSpec((D,D),lambda t:(0,0)),pl.BlockSpec((1,D),lambda t:(0,0))],
        out_shape=[jax.ShapeDtypeStruct((T,D),F32),jax.ShapeDtypeStruct((D,T),BF16),jax.ShapeDtypeStruct((D,D),BF16),jax.ShapeDtypeStruct((1,D),F32)],
        scratch_shapes=[pltpu.VMEM((D,D),F32)],name="middle_back",
        compiler_params=pltpu.CompilerParams(vmem_limit_bytes=48*2**20))(dy,db,m,oT,woT[0],gains[0])
def last_kernel(x_ref,dm_ref,aT_ref,dq_ref,dk_ref,dv_ref,w_ref,dx_ref,dw_ref,dg_ref,acc_ref,*,nt):
    t=pl.program_id(0)
    @pl.when(t==0)
    def _():
        acc_ref[...]=jnp.zeros_like(acc_ref); dg_ref[...]=jnp.zeros_like(dg_ref)
    aT=aT_ref[...]
    da=None
    for c,ref in enumerate((dq_ref,dk_ref,dv_ref)):
        y=ref[...]
        sl=slice(c*D,(c+1)*D)
        acc_ref[:,sl]+=dot(aT,y,NT)
        z=dot(w_ref[:,sl],y)
        da=z if da is None else da+z
    da=da.T
    x=x_ref[...].astype(F32)
    r=rms(x); n1=x*r
    dn=da*row_of(w_ref[:,3*D:3*D+GA],0)
    dg_ref[...]+=jnp.sum(da*n1,axis=0,keepdims=True)
    dx_ref[...]=(dm_ref[...]+r*(dn-n1*jnp.mean(dn*n1,axis=-1,keepdims=True))).astype(BF16)
    @pl.when(t==nt-1)
    def _(): dw_ref[...]=acc_ref[...].astype(BF16)
def last_call(x,dm,aT,dqT,dkT,dvT,w):
    T=x.shape[0]; nt=T//BLOCK
    row=pl.BlockSpec((BLOCK,D),lambda t:(t,0)); col=pl.BlockSpec((D,BLOCK),lambda t:(0,t))
    return pl.pallas_call(functools.partial(last_kernel,nt=nt),grid=(nt,),
        in_specs=[row,row,col,col,col,col,pl.BlockSpec(w.shape,lambda t:(0,0),pipeline_mode=pl.Buffered(1))],
        out_specs=[row,pl.BlockSpec((D,3*D),lambda t:(0,0)),pl.BlockSpec((1,D),lambda t:(0,0))],
        out_shape=[jax.ShapeDtypeStruct((T,D),BF16),jax.ShapeDtypeStruct((D,3*D),BF16),jax.ShapeDtypeStruct((1,D),F32)],
        scratch_shapes=[pltpu.VMEM((D,3*D),F32)],name="project_back",
        compiler_params=pltpu.CompilerParams(vmem_limit_bytes=56*2**20))(x,dm,aT,dqT,dkT,dvT,w)

BOTH=("dp","fsdp")
def body(hidden,long_flags,norm1_gain,query_w,key_w,value_w,out_w,bias_table,norm2_gain,ffn_in,ffn_out,out_grad):
    rows=norm1_gain.shape[0]
    gains=jnp.concatenate([norm1_gain[:,None],norm2_gain[:,None],jnp.zeros((rows,GA-2),F32)],1)
    pa=jnp.concatenate([query_w,key_w,value_w,gains],1).astype(BF16)
    pb=jnp.concatenate([out_w.T,ffn_in,ffn_out.T],1).astype(BF16)
    wa=lax.all_gather(pa,BOTH,axis=0,tiled=True)
    wb=lax.all_gather(pb,BOTH,axis=0,tiled=True)
    bias=bias_call(bias_table)
    aT,qkvT=qkv_call(hidden,wa)
    oT,lse=fwd2_call(long_flags,qkvT,bias,HP=4,mode="norm")
    GB=3*D//GA
    m,b,bT=mid_call(hidden,oT,(wb,0),(wa,GB))
    out,db,dwin,dwoutT=ffn_call(b,bT,out_grad,m,(wb,1),(wb,5))
    dm,doT,dwoT,dg2=post_call(out_grad,db,m,oT,(wb,0),(wa,GB))
    dqT,dkT,dvT,tab=bwd2_call(long_flags,qkvT,doT,lse,bias,HP=4)
    dx,dwqkv,dg1=last_call(hidden,dm,aT,dqT,dkT,dvT,wa)
    ndev=D//rows
    def rs(x): return lax.psum_scatter(x,BOTH,scatter_dimension=0,tiled=True)
    fsum=rs(jnp.concatenate([dwoT,dwin,dwoutT],1)).astype(F32)
    tabv=tab[:,:,0].T
    ex=jnp.concatenate([dg1.T,dg2.T],1)
    tb=jnp.tile(tabv.reshape(rows,-1),(ndev,1))
    pad=jnp.zeros((D,GA-2-tb.shape[1]%GA),F32)
    asum=rs(jnp.concatenate([dwqkv,jnp.concatenate([ex,tb,pad],1).astype(BF16)],1)).astype(F32)
    table=asum[:,3*D+2:3*D+2+tb.shape[1]].reshape(BUCKETS,HEADS)
    return (out,dx,asum[:,3*D],asum[:,:D],asum[:,D:2*D],asum[:,2*D:3*D],fsum[:,:D].T,table,asum[:,3*D+1],fsum[:,D:D+3072],fsum[:,D+3072:].T)

def solution(mesh):
    P=jax.sharding.PartitionSpec
    r=P(BOTH,None); v=P(BOTH); c=P(None,BOTH)
    return jax.shard_map(body,mesh=mesh,in_specs=(r,v,v,r,r,r,c,P(),v,r,c,r),out_specs=(r,r,v,r,r,r,c,P(),v,r,c),check_vma=False)
```

time: 1340 us -> 615 us (0.46)
  matrix products: 435 us -> 0 us
  Pallas kernels: 0 us -> 238 us
  local copies, waits for them, and re-layouts: 211 us -> 18.4 us
  waiting for transfers between devices: 513 us -> 324 us
  blocking collectives: 82.4 us -> 0 us
  other arithmetic: 71.2 us -> 19.2 us
    dot_general x51 -> x0, matrix products: 435 us -> none  [the longest x6 112 us: project(): return jnp.dot(left, right, preferred_element_type=jnp.float32)]
    reduce_scatter x6 -> x1, waiting for transfers between devices: 448 us -> 142 us  [rs(): return lax.psum_scatter(x, BOTH, scatter_dimension=0, tiled=True)]
    pallas_call x0 -> x8, Pallas kernels: none -> 238 us  [the longest x1 79 us: ffn_call(): pl.pallas_call(functools.partial(ffn_kernel, FC=FC, SUB=SUB, nc=nc, nt=nt...]
    unnamed x12 -> x5, waiting for transfers between devices: 0.2 us -> 88.1 us
    unnamed x2 -> x0, blocking collectives: 82.4 us -> none
    convert_element_type x8 -> x0, local copies, waits for them, and re-layouts: 74 us -> none  [the longest x4 58.1 us: one_unit(): grad_s = (attn_probs * (grad_p - row_dot)).astype(jnp.bfloat16)]
    while x80 -> x0, local copies, waits for them, and re-layouts: 65.8 us -> none  [the longest x5 34.4 us: attend_forward(): return lax.map(one_unit, (queries, key_heads, value_heads, long_flags))]
    convert_element_type x15 -> x2, other arithmetic: 55.4 us -> 1.93 us  [the longest x1 1.02 us: body(): fsum = rs(jnp.concatenate([dwoT, dwin, dwoutT], 1)).astype(F32)]
  transfers between devices with their start and end apart: 12 -> 4, of which waited for: 7 -> 4; matrix products, arithmetic and copies ran while one was open for 48% -> 3% of each run, Pallas kernels for 0% -> 9%
where the time goes in v1:
time: 615 us; the launch traced here: 614 us
  waiting for transfers between devices  324 us (53%)
  Pallas kernels  238 us (39%)
  other arithmetic  19.2 us (3%)
  local copies, waits for them, and re-layouts  18.4 us (3%)
  between operations  13.9 us (2%)
    reduce_scatter x1, waiting for transfers between devices, rs(): return lax.psum_scatter(x, BOTH, scatter_dimension=0, tiled=True)  142 us
    unnamed x5, waiting for transfers between devices  88.1 us
    pallas_call x1, Pallas kernels, ffn_call(): pl.pallas_call(functools.partial(ffn_kernel, FC=FC, SUB=SUB, nc=nc, nt=nt...  79 us
    pallas_call x1, Pallas kernels, bwd2_call(): pl.pallas_call(functools.partial(bwd2_kernel, HP=HP, nb=n, tabmode=tabmod...  54.8 us
    all_gather x1, waiting for transfers between devices, body(): wa = lax.all_gather(pa, BOTH, axis=0, tiled=True)  51.3 us
    all_gather x1, waiting for transfers between devices, body(): wb = lax.all_gather(pb, BOTH, axis=0, tiled=True)  42.9 us
    pallas_call x1, Pallas kernels, fwd2_call(): pl.pallas_call(functools.partial(fwd2_kernel, HP=HP, mode=mode), grid_spe...  32.4 us
    pallas_call x1, Pallas kernels, last_call(): pl.pallas_call(functools.partial(last_kernel, nt=nt), grid=(nt,), in_spec...  26.2 us
  transfers between devices with their start and end apart: 4, of which 4 were waited for; matrix products, arithmetic and copies ran while one was open for 3% of the time, Pallas kernels for 9%

profile of v1, /device:TPU:0, one launch (start us, length us, event | category | flops | bytes accessed | tf_op | source)
XLA Modules:
  0.0 614.2 jit_solution(9575768993974013275)
XLA Ops:
  7.2 0.9 convert.45
  12.2 1.0 convert.51
  13.2 0.9 convert_bitcast_fusion.1
  14.1 1.0 convert_bitcast_fusion
  15.9 8.4 %bias.1.bias_ref = f32[12,512,512]{2,1,0:T(8,128)} custom-call(f32[12,32]{1,0:T(8,128)} %bitcast.21), custom_call_target="tpu_custom_call" | custom-call | tf_op jit(solution)/shard_map/bias/pallas_call | solution.py:49
  24.3 51.3 %all-gather.3.cloned.1.call-done.w_ref.ga_ref = bf16[768,2432]{1,0:T(8,128)(2,1)} async-done(((bf16[24,2432]{1,0:T(8,128)(2,1)}), bf16[768,2432]{1,0:T(8,128)(2,1)}) %all-gather.3.cloned.1.call-update) | async-done | bytes 3735568 | tf_op jit(solution)/shard_map/all_gather | solution.py:439
  75.6 14.2 %project.1 = (bf16[768,2048]{1,0:T(8,128)(2,1)}, bf16[2304,2048]{1,0:T(8,128)(2,1)}) custom-call(bf16[2048,768]{1,0:T(8,128)(2,1)} %x_ref.5, bf16[768,2432]{1,0:T(8,128)(2,1)} %all-gather.3.cloned.1.call-done.w_ref.ga_ref), custom_call_target="tpu_custom_call" | custom-call | tf_op jit(solution)/shard_map/project/pallas_call | solution.py:294
  89.8 32.4 %attend.1 = (bf16[768,2048]{1,0:T(8,128)(2,1)}, f32[12,1,2048]{2,1,0:T(1,128)}) custom-call(s32[4]{0:T(128)} %flags_ref.3, bf16[2304,2048]{1,0:T(8,128)(2,1)} %get-tuple-element.33.q_ref.k_ref.v_ref, bf16[2304,2048]{1,0:T(8,128)(2,1)} %get-tuple-element.33.q_ref.k_ref.v_ref, bf16[2304,2048]{1,0:T(8,128)(2,1)} %get-tuple-element.33.q_ref.k_ref.v_ref, ...), custom_call_target="tpu_custom_call" | custom-call | tf_op jit(solution)/shard_map/attend/pallas_call | solution.py:180
  122.1 42.9 %all-gather.5.cloned.1.call-done.wo_ref.win_ref.wout_ref = bf16[768,6912]{1,0:T(8,128)(2,1)} async-done(((bf16[24,6912]{1,0:T(8,128)(2,1)}), bf16[768,6912]{1,0:T(8,128)(2,1)}) %all-gather.5.cloned.1.call-update) | async-done | bytes 10616848 | tf_op jit(solution)/shard_map/all_gather | solution.py:440
  165.1 8.6 %middle.1 = (f32[2048,768]{1,0:T(8,128)}, bf16[2048,768]{1,0:T(8,128)(2,1)S(1)}, bf16[4,768,512]{2,1,0:T(8,128)(2,1)}) custom-call(bf16[2048,768]{1,0:T(8,128)(2,1)} %x_ref.5, bf16[768,2048]{1,0:T(8,128)(2,1)} %get-tuple-element.34.oT_ref, bf16[768,6912]{1,0:T(8,128)(2,1)} %all-gather.5.cloned.1.call-done.wo_ref.win_ref.wout_ref, ...), custom_call_target="tpu_custom_call" | custom-call | tf_op jit(solution)/shard_map/middle/pallas_call | solution.py:309
  173.7 1.7 copy-done.1
  175.4 79.0 %feed_forward.1 = (bf16[2048,768]{1,0:T(8,128)(2,1)}, f32[2048,768]{1,0:T(8,128)}, bf16[768,3072]{1,0:T(8,128)(2,1)}, bf16[768,3072]{1,0:T(8,128)(2,1)}) custom-call(bf16[2048,768]{1,0:T(8,128)(2,1)} %copy-done.1, bf16[4,768,512]{2,1,0:T(8,128)(2,1)} %get-tuple-element.36.bT_ref, bf16[2048,768]{1,0:T(8,128)(2,1)} %dy_ref.3, ...), custom_call_target="tpu_custom_call" | custom-call | tf_op jit(solution)/shard_map/feed_forward/pallas_call | solution.py:367
  254.4 14.5 %middle_back.1 = (f32[2048,768]{1,0:T(8,128)}, bf16[768,2048]{1,0:T(8,128)(2,1)S(1)}, bf16[768,768]{1,0:T(8,128)(2,1)S(1)}, f32[1,768]{1,0:T(1,128)S(1)}) custom-call(bf16[2048,768]{1,0:T(8,128)(2,1)} %dy_ref.3, f32[2048,768]{1,0:T(8,128)} %get-tuple-element.39.db_ref, f32[2048,768]{1,0:T(8,128)} %get-tuple-element.37.m_ref, ...), custom_call_target="tpu_custom_call" | custom-call | tf_op jit(solution)/shard_map/middle_back/pallas_call | solution.py:396
  268.9 1.7 copy-done
  270.6 54.8 %attend_back.1 = (bf16[768,2048]{1,0:T(8,128)(2,1)}, bf16[768,2048]{1,0:T(8,128)(2,1)}, bf16[768,2048]{1,0:T(8,128)(2,1)}, f32[12,32,128]{2,1,0:T(8,128)}) custom-call(s32[4]{0:T(128)} %flags_ref.3, bf16[2304,2048]{1,0:T(8,128)(2,1)} %get-tuple-element.33.q_ref.k_ref.v_ref, bf16[2304,2048]{1,0:T(8,128)(2,1)} %get-tuple-element.33.q_ref.k_ref.v_ref, ...), custom_call_target="tpu_custom_call" | custom-call | tf_op jit(solution)/shard_map/attend_back/pallas_call | solution.py:266
  325.4 26.2 %project_back.1 = (bf16[2048,768]{1,0:T(8,128)(2,1)}, bf16[768,2304]{1,0:T(8,128)(2,1)}, f32[1,768]{1,0:T(1,128)}) custom-call(bf16[2048,768]{1,0:T(8,128)(2,1)} %x_ref.5, f32[2048,768]{1,0:T(8,128)} %get-tuple-element.40.dm_ref, bf16[768,2048]{1,0:T(8,128)(2,1)} %get-tuple-element.41.aT_ref, bf16[768,2048]{1,0:T(8,128)(2,1)} %get-tuple-element.44.dq_ref, ...), custom_call_target="tpu_custom_call" | custom-call | tf_op jit(solution)/shard_map/project_back/pallas_call | solution.py:426
  353.1 6.6 %concatenate.19 = bf16[768,2432]{1,0:T(8,128)(2,1)} concatenate(bf16[768,2304]{1,0:T(8,128)(2,1)} %get-tuple-element.48, bf16[768,1]{1,0:T(8,128)(2,1)S(1)} %copy.35, bf16[768,1]{1,0:T(8,128)(2,1)S(1)} %copy.36, bf16[768,16]{1,0:T(8,128)(2,1)S(1)} %bitcast.19, bf16[768,110]{1,0:T(8,128)(2,1)S(1)} %broadcast_in_dim.17), dimensions={1} | concatenate | bytes 7471104 | tf_op jit(solution)/shard_map/concatenate | solution.py:457
  359.8 8.9 %pad_maximum_fusion = bf16[768,6912]{1,0:T(8,128)(2,1)} fusion(bf16[768,3072]{1,0:T(8,128)(2,1)} %get-tuple-element.54, bf16[768,3072]{1,0:T(8,128)(2,1)} %get-tuple-element.53, bf16[768,768]{1,0:T(8,128)(2,1)S(1)} %get-tuple-element.52), kind=kLoop, calls=%fused_computation | loop fusion | flops 31850496 | bytes 21233664 | tf_op jit(solution)/shard_map/concatenate | solution.py:452
  368.8 88.1 %reduce-scatter.7.cloned.1.call-done = bf16[24,2432]{1,0:T(8,128)(2,1)} async-done(((bf16[768,2432]{1,0:T(8,128)(2,1)}), bf16[24,2432]{1,0:T(8,128)(2,1)}) %reduce-scatter.7.cloned.1.call-update) | async-done | bytes 116752
  458.4 0.9 convert_element_type.4
  460.0 1.5 fusion.1
  461.5 142.1 %reduce-scatter.5.cloned.1.call-done = bf16[24,6912]{1,0:T(8,128)(2,1)} async-done(((bf16[768,6912]{1,0:T(8,128)(2,1)}), bf16[24,6912]{1,0:T(8,128)(2,1)}) %reduce-scatter.5.cloned.1.call-update) | async-done | bytes 331792 | tf_op jit(solution)/shard_map/reduce_scatter | solution.py:451
  603.6 1.0 convert_element_type.10
  606.0 1.6 slice.47
  (36 shorter events, 10.1 us)
Async XLA Ops:
  7.2 68.4 %all-gather.3.cloned.1.call-start = ((), (), s32[]{:S(2)}) async-start(), calls=%async_computation.2 | async-start | bytes 3852288 | tf_op jit(solution)/shard_map/all_gather | solution.py:439
  12.2 152.9 %all-gather.5.cloned.1.call-start = ((), (), s32[]{:S(2)}) async-start(), calls=%async_computation.3 | async-start | bytes 10948608 | tf_op jit(solution)/shard_map/all_gather | solution.py:440
  15.9 441.0 %reduce-scatter.7.cloned.1.call-start = ((), (), s32[]{:S(2)}) async-start(), calls=%async_computation.5 | async-start | bytes 3852288
  173.7 1.7 copy-start.1
  268.9 1.7 copy-start
  325.4 27.1 %copy-start.2 = (f32[12,32,128]{2,1,0:T(8,128)S(1)}, f32[12,32,128]{2,1,0:T(8,128)}, u32[]{:S(2)}) copy-start(f32[12,32,128]{2,1,0:T(8,128)} %get-tuple-element.51) | copy-start | bytes 589828
  359.7 243.9 %reduce-scatter.5.cloned.1.call-start = ((), (), s32[]{:S(2)}) async-start(), calls=%async_computation.4 | async-start | bytes 10948608 | tf_op jit(solution)/shard_map/reduce_scatter | solution.py:451
Sparse Core Ops, SparseCore 0:
  12.3 63.2 all-gather.2
  79.1 85.9 all-gather.4
  359.9 96.9 reduce-scatter.6
  462.8 140.7 reduce-scatter.4

commit v2 on v1

--- a/solution.py
+++ b/solution.py
@@ -205,7 +205,7 @@
         y=pltpu.roll(x,width-(1<<b),axis=1)
         x=jnp.where((row>>b)&1==1,y,x)
     return x
-def bwd2_kernel(flags_ref,q_ref,k_ref,v_ref,do_ref,lse_ref,bias_ref,dq_ref,dk_ref,dv_ref,tab_ref,band_ref,far_ref,*,HP,nb,tabmode):
+def bwd2_kernel(flags_ref,q_ref,k_ref,v_ref,do_ref,lse_ref,bias_ref,g_ref,tab_ref,band_ref,far_ref,*,HP,nb,tabmode):
     n=pl.program_id(1)
     qm,km=masks(flags_ref[n])
     @pl.when(n==0)
@@ -223,13 +223,13 @@
         r=R[u]
         p=jnp.exp(S[u]+bias_ref[u]-lse_ref[u])
         pb=p.astype(BF16)
-        dv_ref[r,:]=dot(do_ref[r,:],pb,NT).astype(BF16)
+        g_ref[2,r,:]=dot(do_ref[r,:],pb,NT).astype(BF16)
         t=p*DP[u]
         d=jnp.sum(t,axis=0,keepdims=True)
         dsf=t-p*d
         ds=dsf.astype(BF16)
-        dq_ref[r,:]=dot(k_ref[r,:],ds).astype(BF16)
-        dk_ref[r,:]=dot(q_ref[r,:],ds,NT).astype(BF16)
+        g_ref[0,r,:]=dot(k_ref[r,:],ds).astype(BF16)
+        g_ref[1,r,:]=dot(q_ref[r,:],ds,NT).astype(BF16)
         if tabmode:
             lo=None;hi=None;bl=[None]*3
             for g in range(4):
@@ -258,7 +258,9 @@
             val=jnp.where(b==cc,tot,0.0)
             val=val[:,:128]+val[:,128:256]+val[:,256:384]+val[:,384:]
             val=val+jnp.where(c1==BUCKETS-1,lo,0.0)+jnp.where(c1==BUCKETS//2-1,hi,0.0)
-            tab_ref[u]=jnp.broadcast_to(jnp.sum(val,axis=1,keepdims=True),(BUCKETS,128))
+            col=jnp.broadcast_to(jnp.sum(val,axis=1,keepdims=True),(BUCKETS,128))
+            col=jnp.concatenate([col,jnp.zeros((128-BUCKETS,128),F32)],0)
+            tab_ref[u]=col.T[:8]
 def bwd2_call(flags,qkvT,doT,lse,bias,HP=2,tabmode=1):
     T=qkvT.shape[1]; n=T//BLOCK; G=HEADS//HP
     sp=lambda off: pl.BlockSpec((HP*HEAD_DIM,BLOCK),lambda h,n,f:(h+off,n))
@@ -266,9 +268,9 @@
     return pl.pallas_call(functools.partial(bwd2_kernel,HP=HP,nb=n,tabmode=tabmode),
         grid_spec=pltpu.PrefetchScalarGridSpec(num_scalar_prefetch=1,grid=(G,n),
         in_specs=[sp(0),sp(G),sp(2*G),sp(0),pl.BlockSpec((HP,1,BLOCK),lambda h,n,f:(h,0,n)),pl.BlockSpec((HP,BLOCK,BLOCK),lambda h,n,f:(h,0,0))],
-        out_specs=[sp(0),sp(0),sp(0),pl.BlockSpec((HP,BUCKETS,128),lambda h,n,f:(h,0,0))],
+        out_specs=[pl.BlockSpec((3,HP*HEAD_DIM,BLOCK),lambda h,n,f:(0,h,n)),pl.BlockSpec((HP,8,128),lambda h,n,f:(h,0,0))],
         scratch_shapes=[pltpu.VMEM((HP,128,384),F32),pltpu.VMEM((HP,2,8,128),F32)]),
-        out_shape=[jax.ShapeDtypeStruct((D,T),BF16)]*3+[jax.ShapeDtypeStruct((HEADS,BUCKETS,128),F32)],
+        out_shape=[jax.ShapeDtypeStruct((3,D,T),BF16),jax.ShapeDtypeStruct((HEADS,8,128),F32)],
         name="attend_back",
         compiler_params=pltpu.CompilerParams(vmem_limit_bytes=60*2**20))(flags,qkvT,qkvT,qkvT,doT,lse,bias)
 
@@ -323,7 +325,7 @@
         q=((((0.5*1.061405429*t-0.5*1.453152027)*t+0.5*1.421413741)*t-0.5*0.284496736)*t+0.5*0.254829592)*t*z
         P=jnp.where(u>=0,1.0-q,q)
     return u*P, P+u*z*(2*math.pi)**-0.5
-def ffn_kernel(b_ref,bT_ref,dy_ref,m_ref,win_ref,wout_ref,out_ref,db_ref,dwin_ref,dwout_ref,
+def ffn_kernel(b_ref,bT_ref,dy_ref,m_ref,win_ref,wout_ref,out_ref,db_ref,dw_ref,
                oacc,dacc,dyT,ain,aout,*,FC,SUB,nc,nt,mode,TB,order):
     c=pl.program_id(0); t=pl.program_id(1)
     rows=pl.ds(t*TB,TB)
@@ -352,8 +354,8 @@
     dacc[rows,:]+=dot(du,win_ref[...],NT)
     @pl.when(t==nt-1)
     def _():
-        dwin_ref[...]=ain[...].astype(BF16)
-        dwout_ref[...]=aout[...].astype(BF16)
+        dw_ref[:,:FC]=ain[...].astype(BF16)
+        dw_ref[:,FC:]=aout[...].astype(BF16)
     @pl.when(c==nc-1)
     def _():
         out_ref[...]=oacc[rows,:].astype(BF16)
@@ -368,21 +370,20 @@
         in_specs=[pl.BlockSpec((T,D),lambda c,t:(0,0),pipeline_mode=one),pl.BlockSpec((nt,D,TB),lambda c,t:(0,0,0),pipeline_mode=one),
             pl.BlockSpec((T,D),lambda c,t:(0,0),pipeline_mode=one),
             pl.BlockSpec((TB,D),first),pl.BlockSpec((D,FC),lambda c,t:(0,c+win[1]*D//FC)),pl.BlockSpec((D,FC),lambda c,t:(0,c+wout[1]*D//FC))],
-        out_specs=[pl.BlockSpec((TB,D),last),pl.BlockSpec((TB,D),last),pl.BlockSpec((D,FC),lambda c,t:(0,c)),pl.BlockSpec((D,FC),lambda c,t:(0,c))],
-        out_shape=[jax.ShapeDtypeStruct((T,D),BF16),jax.ShapeDtypeStruct((T,D),F32),jax.ShapeDtypeStruct((D,FF),BF16),jax.ShapeDtypeStruct((D,FF),BF16)],
+        out_specs=[pl.BlockSpec((TB,D),last),pl.BlockSpec((TB,D),last),pl.BlockSpec((D,2*FC),lambda c,t:(0,c))],
+        out_shape=[jax.ShapeDtypeStruct((T,D),BF16),jax.ShapeDtypeStruct((T,D),F32),jax.ShapeDtypeStruct((D,2*FF),BF16)],
         scratch_shapes=[pltpu.VMEM((T,D),F32),pltpu.VMEM((T,D),F32),pltpu.VMEM((nt,D,TB),BF16),pltpu.VMEM((D,FC),F32),pltpu.VMEM((D,FC),F32)],
         name="feed_forward",
         compiler_params=pltpu.CompilerParams(vmem_limit_bytes=62*2**20))(b,bT3,dy,m,win[0],wout[0])
 
-def post_kernel(dy_ref,db_ref,m_ref,oT_ref,wo_ref,ga_ref,dm_ref,doT_ref,dwo_ref,dg_ref,acc_ref,*,nt):
+def post_kernel(dy_ref,db_ref,m_ref,oT_ref,wo_ref,ga_ref,dm_ref,doT_ref,dwo_ref,acc_ref,*,nt):
     t=pl.program_id(0)
     @pl.when(t==0)
     def _():
-        acc_ref[...]=jnp.zeros_like(acc_ref); dg_ref[...]=jnp.zeros_like(dg_ref)
+        acc_ref[...]=jnp.zeros_like(acc_ref)
     m=m_ref[...]; db=db_ref[...]
     r=rms(m); n2=m*r
     dn=db*row_of(ga_ref[...],1)
-    dg_ref[...]+=jnp.sum(db*n2,axis=0,keepdims=True)
     dm=dy_ref[...].astype(F32)+r*(dn-n2*jnp.mean(dn*n2,axis=-1,keepdims=True))
     dm_ref[...]=dm
     dmb=dm.astype(BF16)
@@ -395,70 +396,251 @@
     row=pl.BlockSpec((BLOCK,D),lambda t:(t,0)); col=pl.BlockSpec((D,BLOCK),lambda t:(0,t))
     return pl.pallas_call(functools.partial(post_kernel,nt=nt),grid=(nt,),
         in_specs=[row,row,row,col,pl.BlockSpec((D,D),lambda t:(0,woT[1])),pl.BlockSpec((D,GA),lambda t:(0,gains[1]))],
-        out_specs=[row,col,pl.BlockSpec((D,D),lambda t:(0,0)),pl.BlockSpec((1,D),lambda t:(0,0))],
-        out_shape=[jax.ShapeDtypeStruct((T,D),F32),jax.ShapeDtypeStruct((D,T),BF16),jax.ShapeDtypeStruct((D,D),BF16),jax.ShapeDtypeStruct((1,D),F32)],
+        out_specs=[row,col,pl.BlockSpec((D,D),lambda t:(0,0))],
+        out_shape=[jax.ShapeDtypeStruct((T,D),F32),jax.ShapeDtypeStruct((D,T),BF16),jax.ShapeDtypeStruct((D,D),BF16)],
         scratch_shapes=[pltpu.VMEM((D,D),F32)],name="middle_back",
         compiler_params=pltpu.CompilerParams(vmem_limit_bytes=48*2**20))(dy,db,m,oT,woT[0],gains[0])
-def last_kernel(x_ref,dm_ref,aT_ref,dq_ref,dk_ref,dv_ref,w_ref,dx_ref,dw_ref,dg_ref,acc_ref,*,nt):
-    t=pl.program_id(0)
-    @pl.when(t==0)
-    def _():
-        acc_ref[...]=jnp.zeros_like(acc_ref); dg_ref[...]=jnp.zeros_like(dg_ref)
-    aT=aT_ref[...]
+def last_kernel(x_ref,dm_ref,g_ref,w_ref,dx_ref):
     da=None
-    for c,ref in enumerate((dq_ref,dk_ref,dv_ref)):
-        y=ref[...]
-        sl=slice(c*D,(c+1)*D)
-        acc_ref[:,sl]+=dot(aT,y,NT)
-        z=dot(w_ref[:,sl],y)
+    for c in range(3):
+        z=dot(w_ref[:,c*D:(c+1)*D],g_ref[c])
         da=z if da is None else da+z
     da=da.T
     x=x_ref[...].astype(F32)
     r=rms(x); n1=x*r
     dn=da*row_of(w_ref[:,3*D:3*D+GA],0)
-    dg_ref[...]+=jnp.sum(da*n1,axis=0,keepdims=True)
     dx_ref[...]=(dm_ref[...]+r*(dn-n1*jnp.mean(dn*n1,axis=-1,keepdims=True))).astype(BF16)
-    @pl.when(t==nt-1)
-    def _(): dw_ref[...]=acc_ref[...].astype(BF16)
-def last_call(x,dm,aT,dqT,dkT,dvT,w):
+def last_call(x,dm,gT,w):
     T=x.shape[0]; nt=T//BLOCK
-    row=pl.BlockSpec((BLOCK,D),lambda t:(t,0)); col=pl.BlockSpec((D,BLOCK),lambda t:(0,t))
-    return pl.pallas_call(functools.partial(last_kernel,nt=nt),grid=(nt,),
-        in_specs=[row,row,col,col,col,col,pl.BlockSpec(w.shape,lambda t:(0,0),pipeline_mode=pl.Buffered(1))],
-        out_specs=[row,pl.BlockSpec((D,3*D),lambda t:(0,0)),pl.BlockSpec((1,D),lambda t:(0,0))],
-        out_shape=[jax.ShapeDtypeStruct((T,D),BF16),jax.ShapeDtypeStruct((D,3*D),BF16),jax.ShapeDtypeStruct((1,D),F32)],
-        scratch_shapes=[pltpu.VMEM((D,3*D),F32)],name="project_back",
-        compiler_params=pltpu.CompilerParams(vmem_limit_bytes=56*2**20))(x,dm,aT,dqT,dkT,dvT,w)
+    row=pl.BlockSpec((BLOCK,D),lambda t:(t,0))
+    return pl.pallas_call(last_kernel,grid=(nt,),
+        in_specs=[row,row,pl.BlockSpec((3,D,BLOCK),lambda t:(0,0,t)),pl.BlockSpec(w.shape,lambda t:(0,0),pipeline_mode=pl.Buffered(1))],
+        out_specs=row,out_shape=jax.ShapeDtypeStruct((T,D),BF16),name="project_back",
+        cost_estimate=pl.CostEstimate(flops=2*T*D*3*D,bytes_accessed=20*T*D,transcendentals=0),
+        compiler_params=pltpu.CompilerParams(vmem_limit_bytes=56*2**20))(x,dm,gT,w)
+
+GW=3*D+GA
+def pack_a_kernel(q_ref,k_ref,v_ref,g1_ref,g2_ref,o_ref):
+    for c,ref in enumerate((q_ref,k_ref,v_ref)):
+        o_ref[:,c*D:(c+1)*D]=ref[...].astype(BF16)
+    rows=o_ref.shape[0]
+    g=jnp.concatenate([g1_ref[...],g2_ref[...],jnp.zeros((GA-2,rows),F32)],0)
+    o_ref[:,3*D:]=g.T.astype(BF16)
+def pack_a(q,k,v,g1,g2):
+    return pl.pallas_call(pack_a_kernel,out_shape=jax.ShapeDtypeStruct((q.shape[0],GW),BF16),name="pack_attention")(q,k,v,g1[None],g2[None])
+def pack_b_kernel(wo_ref,wi_ref,wu_ref,o_ref):
+    F=wi_ref.shape[1]
+    o_ref[:,:D]=wo_ref[...].astype(BF16)
+    o_ref[:,D:D+F]=wi_ref[...].astype(BF16)
+    o_ref[:,D+F:]=wu_ref[...].astype(BF16)
+def pack_b(wo,wi,wu):
+    return pl.pallas_call(pack_b_kernel,out_shape=jax.ShapeDtypeStruct((wi.shape[0],D+2*wi.shape[1]),BF16),name="pack_feed_forward")(wo.T,wi,wu.T)
+
+def swap(x,axis,mask):
+    n=8 if axis=="fsdp" else 4
+    f=mask if callable(mask) else (lambda i:mask)
+    return lax.ppermute(x,axis,[(i,i^f(i)) for i in range(n)])
+first_leg=lambda i: 4 if i&1 else 2
+second_leg=lambda i: 2 if i&1 else 4
+def gather_pieces(shard,beside):
+    a=shard[None]
+    a=jnp.concatenate([a,swap(a,"dp",2)],0)
+    got=swap(a,"dp",1)
+    got,beside=lax.optimization_barrier((got,beside))
+    a=jnp.concatenate([a,got],0)
+    a=jnp.concatenate([a,swap(a,"fsdp",first_leg)],0)
+    b=swap(a,"fsdp",second_leg)
+    c=swap(a,"fsdp",1)
+    d=swap(b,"fsdp",1)
+    return (a,b,c,d),beside
+def place():
+    f=lax.axis_index("fsdp"); z=lax.axis_index("dp")
+    return jnp.stack([f,z]).astype(jnp.int32)
+def assemble_rows(at_ref,pieces,put):
+    f=at_ref[0]; z=at_ref[1]
+    core=f&1; x=(f>>1)&1; y=f>>2
+    for j in range(16):
+        zj,yj,xj=j>>2,(j>>1)&1,j&1
+        dz=zj^z; dx=xj^x; dy=yj^y
+        low=(dz&1)*2+(dz>>1)
+        halves=[]
+        for cj in range(2):
+            far_core=core^cj
+            one=jnp.where(cj==0,dx,dy)
+            two=jnp.where(cj==0,dy,dx)
+            slot=one*4+low
+            which=far_core*2+two
+            halves.append((which,slot))
+        put(j,halves)
+def project2_kernel(at_ref,x_ref,a_ref,b_ref,c_ref,d_ref,aT_ref,qkvT_ref,w_ref,all_ref,wT_ref):
+    R=a_ref.shape[1]
+    @pl.when(pl.program_id(0)==0)
+    def _():
+        for i,ref in enumerate((a_ref,b_ref,c_ref,d_ref)): all_ref[pl.ds(8*i,8)]=ref[...]
+        def put(j,halves):
+            v=jnp.concatenate([all_ref[w*8+s].astype(F32) for w,s in halves],0)
+            w_ref[pl.ds(j*2*R,2*R),:]=v.astype(BF16)
+        assemble_rows(at_ref,None,put)
+        for c in range(3):
+            wT_ref[pl.ds(c*D,D),:]=w_ref[:,c*D:(c+1)*D].T
+    x=x_ref[...].astype(F32)
+    g=row_of(w_ref[:,3*D:3*D+GA],0)
+    a=(x*rms(x)*g).astype(BF16)
+    aT=a.T
+    aT_ref[...]=aT
+    qkvT_ref[...]=dot(wT_ref[...],aT).astype(BF16)
+def project2_call(x,pieces,at):
+    T=x.shape[0]; R=pieces[0].shape[1]
+    one=pl.Buffered(1)
+    ps=pl.BlockSpec((8,R,GW),lambda t,at:(0,0,0),pipeline_mode=one)
+    return pl.pallas_call(project2_kernel,
+        grid_spec=pltpu.PrefetchScalarGridSpec(num_scalar_prefetch=1,grid=(T//BLOCK,),
+        in_specs=[pl.BlockSpec((BLOCK,D),lambda t,at:(t,0)),ps,ps,ps,ps],
+        out_specs=[pl.BlockSpec((D,BLOCK),lambda t,at:(0,t)),pl.BlockSpec((3*D,BLOCK),lambda t,at:(0,t)),pl.BlockSpec((D,GW),lambda t,at:(0,0))],
+        scratch_shapes=[pltpu.VMEM((32,R,GW),BF16),pltpu.VMEM((3*D,D),BF16)]),
+        out_shape=[jax.ShapeDtypeStruct((D,T),BF16),jax.ShapeDtypeStruct((3*D,T),BF16),jax.ShapeDtypeStruct((D,GW),BF16)],
+        name="project",
+        compiler_params=pltpu.CompilerParams(vmem_limit_bytes=60*2**20))(at,x,*pieces)
+
+
+def add(a,b): return (a.astype(F32)+b.astype(F32)).astype(BF16)
+WB=256
+GN=4*D+WB
+def slot_rows(s,f,z,core):
+    x=(f>>1)&1; y=f>>2
+    one=s>>3; two=(s>>2)&1
+    dx=jnp.where(core==0,one,two); dy=jnp.where(core==0,two,one)
+    zz=z^((s>>1)&1)^((s&1)<<1)
+    return (zz*8+(y^dy)*4+(x^dx)*2+core)
+def grads_kernel(at_ref,aT_ref,g_ref,wo_ref,tab_ref,keep_ref,send_ref,v_ref):
+    c=pl.program_id(0)
+    R=keep_ref.shape[1]
+    @pl.when(c<9)
+    def _(): v_ref[...]=dot(aT_ref[...],g_ref[0],NT)
+    @pl.when((c>=9)&(c<12))
+    def _(): v_ref[...]=wo_ref[...].astype(F32)
+    @pl.when(c<12)
+    def _():
+        f=at_ref[0]; z=at_ref[1]; core=f&1
+        for s in range(16):
+            for ref,cc in ((keep_ref,core),(send_ref,1-core)):
+                j=slot_rows(s,f,z,cc)
+                ref[s]=v_ref[pl.ds(pl.multiple_of(j*R,8),R),:].astype(BF16)
+    @pl.when(c==12)
+    def _():
+        t=jnp.concatenate([tab_ref[h,:1,:] for h in range(HEADS)]+[jnp.zeros((R-HEADS,128),F32)],0)
+        t=jnp.concatenate([t,jnp.zeros((R,WB-128),F32)],1).astype(BF16)
+        for s in range(16):
+            keep_ref[s]=t; send_ref[s]=t
+def grads_call(at,aT,gT,dwoT,tab):
+    T=aT.shape[1]; R=D//32
+    nb=D//WB
+    out=pl.BlockSpec((16,R,WB),lambda c,at:(0,0,c))
+    return pl.pallas_call(grads_kernel,
+        grid_spec=pltpu.PrefetchScalarGridSpec(num_scalar_prefetch=1,grid=(GN//WB,),
+        in_specs=[pl.BlockSpec((D,T),lambda c,at:(0,0),pipeline_mode=pl.Buffered(1)),
+                  pl.BlockSpec((1,WB,T),lambda c,at:(jnp.minimum(c,8)//nb,jnp.minimum(c,8)%nb,0)),
+                  pl.BlockSpec((D,WB),lambda c,at:(0,jnp.clip(c-9,0,2))),
+                  pl.BlockSpec((HEADS,8,128),lambda c,at:(0,0,0))],
+        out_specs=[out,out],scratch_shapes=[pltpu.VMEM((D,WB),F32)]),
+        out_shape=[jax.ShapeDtypeStruct((16,R,GN),BF16)]*2,name="weight_grads",
+        compiler_params=pltpu.CompilerParams(vmem_limit_bytes=48*2**20))(at,aT,gT,dwoT,tab)
+def scatter_sum(keep,send,beside):
+    r=swap(send,"fsdp",1)
+    for half,axis,leg in ((8,"fsdp",first_leg),(4,"fsdp",second_leg),(2,"dp",1),(1,"dp",2)):
+        out=add(keep[half:],r[half:])
+        keep=add(keep[:half],r[:half])
+        r=swap(out,axis,leg)
+        if half==8: r,beside=lax.optimization_barrier((r,beside))
+    return keep[0],r[0],beside
+def finish_kernel(a_ref,b_ref,wq_ref,wk_ref,wv_ref,g_ref,q_ref,k_ref,v_ref,o_ref,tab_ref,dg_ref):
+    R=a_ref.shape[0]
+    tot=None
+    for c,(w,out) in enumerate(((wq_ref,q_ref),(wk_ref,k_ref),(wv_ref,v_ref),(None,o_ref))):
+        sl=slice(c*D,(c+1)*D)
+        s=a_ref[:,sl].astype(F32)+b_ref[:,sl].astype(F32)
+        out[...]=s
+        if w is not None:
+            y=jnp.sum(s*w[...].astype(BF16).astype(F32),axis=1,keepdims=True)
+            tot=y if tot is None else tot+y
+    t=a_ref[:,4*D:4*D+128].astype(F32)+b_ref[:,4*D:4*D+128].astype(F32)
+    t=jnp.concatenate([t,jnp.zeros((128-R,128),F32)],0).T
+    tab_ref[...]=t[:BUCKETS,:HEADS]
+    rowv=jnp.broadcast_to(tot,(R,128))
+    rowv=jnp.concatenate([rowv,jnp.zeros((128-R,128),F32)],0).T[:1,:R]
+    dg_ref[...]=rowv/g_ref[...].astype(BF16).astype(F32)
+def finish_call(a,b,wq,wk,wv,g1):
+    R=a.shape[0]; sd=jax.ShapeDtypeStruct
+    return pl.pallas_call(finish_kernel,out_shape=[sd((R,D),F32)]*4+[sd((BUCKETS,HEADS),F32),sd((1,R),F32)],name="finish_attention")(a,b,wq,wk,wv,g1[None])
+def finish_ffn_kernel(s_ref,w_ref,g_ref,i_ref,o_ref,dg_ref,*,FC):
+    R=s_ref.shape[0]
+    tot=None
+    for c in range(w_ref.shape[1]//FC):
+        sl=slice(c*FC,(c+1)*FC)
+        s=s_ref[:,2*c*FC:(2*c+1)*FC].astype(F32)
+        i_ref[:,sl]=s
+        o_ref[:,sl]=s_ref[:,(2*c+1)*FC:(2*c+2)*FC].astype(F32)
+        y=jnp.sum(s*w_ref[:,sl].astype(BF16).astype(F32),axis=1,keepdims=True)
+        tot=y if tot is None else tot+y
+    rowv=jnp.broadcast_to(tot,(R,128))
+    rowv=jnp.concatenate([rowv,jnp.zeros((128-R,128),F32)],0).T[:1,:R]
+    dg_ref[...]=rowv/g_ref[...].astype(BF16).astype(F32)
+def finish_ffn_call(s,w,g2,FC):
+    R,F=w.shape; sd=jax.ShapeDtypeStruct
+    return pl.pallas_call(functools.partial(finish_ffn_kernel,FC=FC),out_shape=[sd((R,F),F32),sd((R,F),F32),sd((1,R),F32)],name="finish_feed_forward")(s,w,g2[None])
 
 BOTH=("dp","fsdp")
-def body(hidden,long_flags,norm1_gain,query_w,key_w,value_w,out_w,bias_table,norm2_gain,ffn_in,ffn_out,out_grad):
+FC=768
+def low(v): return v.astype(BF16).astype(F32)
+def body(sizes,hidden,long_flags,norm1_gain,query_w,key_w,value_w,out_w,bias_table,norm2_gain,ffn_in,ffn_out,out_grad):
     rows=norm1_gain.shape[0]
-    gains=jnp.concatenate([norm1_gain[:,None],norm2_gain[:,None],jnp.zeros((rows,GA-2),F32)],1)
-    pa=jnp.concatenate([query_w,key_w,value_w,gains],1).astype(BF16)
-    pb=jnp.concatenate([out_w.T,ffn_in,ffn_out.T],1).astype(BF16)
-    wa=lax.all_gather(pa,BOTH,axis=0,tiled=True)
-    wb=lax.all_gather(pb,BOTH,axis=0,tiled=True)
-    bias=bias_call(bias_table)
-    aT,qkvT=qkv_call(hidden,wa)
+    FF=ffn_in.shape[1]
+    legs=sizes==(4,8)
+    if legs:
+        pa=pack_a(query_w,key_w,value_w,norm1_gain,norm2_gain)
+        pb=pack_b(out_w,ffn_in,ffn_out)
+        wb=lax.all_gather(pb,BOTH,axis=0,tiled=True)
+        at=place()
+        pieces,bias=gather_pieces(pa,bias_call(bias_table))
+        aT,qkvT,wa=project2_call(hidden,pieces,at)
+    else:
+        bias=bias_call(bias_table)
+        gains=jnp.concatenate([norm1_gain[:,None],norm2_gain[:,None],jnp.zeros((rows,GA-2),F32)],1)
+        pa=jnp.concatenate([query_w,key_w,value_w,gains],1).astype(BF16)
+        pb=jnp.concatenate([out_w.T,ffn_in,ffn_out.T],1).astype(BF16)
+        wa=lax.all_gather(pa,BOTH,axis=0,tiled=True)
+        wb=lax.all_gather(pb,BOTH,axis=0,tiled=True)
+        aT,qkvT=qkv_call(hidden,wa)
     oT,lse=fwd2_call(long_flags,qkvT,bias,HP=4,mode="norm")
     GB=3*D//GA
     m,b,bT=mid_call(hidden,oT,(wb,0),(wa,GB))
-    out,db,dwin,dwoutT=ffn_call(b,bT,out_grad,m,(wb,1),(wb,5))
-    dm,doT,dwoT,dg2=post_call(out_grad,db,m,oT,(wb,0),(wa,GB))
-    dqT,dkT,dvT,tab=bwd2_call(long_flags,qkvT,doT,lse,bias,HP=4)
-    dx,dwqkv,dg1=last_call(hidden,dm,aT,dqT,dkT,dvT,wa)
-    ndev=D//rows
+    out,db,dffn=ffn_call(b,bT,out_grad,m,(wb,1),(wb,5),FC=FC)
     def rs(x): return lax.psum_scatter(x,BOTH,scatter_dimension=0,tiled=True)
-    fsum=rs(jnp.concatenate([dwoT,dwin,dwoutT],1)).astype(F32)
-    tabv=tab[:,:,0].T
-    ex=jnp.concatenate([dg1.T,dg2.T],1)
-    tb=jnp.tile(tabv.reshape(rows,-1),(ndev,1))
-    pad=jnp.zeros((D,GA-2-tb.shape[1]%GA),F32)
-    asum=rs(jnp.concatenate([dwqkv,jnp.concatenate([ex,tb,pad],1).astype(BF16)],1)).astype(F32)
-    table=asum[:,3*D+2:3*D+2+tb.shape[1]].reshape(BUCKETS,HEADS)
-    return (out,dx,asum[:,3*D],asum[:,:D],asum[:,D:2*D],asum[:,2*D:3*D],fsum[:,:D].T,table,asum[:,3*D+1],fsum[:,D:D+3072],fsum[:,D+3072:].T)
+    fsum=rs(dffn)
+    dm,doT,dwoT=post_call(out_grad,db,m,oT,(wb,0),(wa,GB))
+    gT,tab=bwd2_call(long_flags,qkvT,doT,lse,bias,HP=4)
+    if legs:
+        keep,send=grads_call(at,aT,gT,dwoT,tab)
+        a,b2,dx=scatter_sum(keep,send,last_call(hidden,dm,gT,wa))
+        dq,dk,dv,do,table,dg1=finish_call(a,b2,query_w,key_w,value_w,norm1_gain)
+        di,du,dg2=finish_ffn_call(fsum,ffn_in,norm2_gain,FC)
+        dg1=dg1[0]; dg2=dg2[0]
+    else:
+        dx=last_call(hidden,dm,gT,wa)
+        tabs=tab[:,0,:BUCKETS].reshape(-1)
+        wide=tabs.shape[0]//rows
+        tb=jnp.tile(tabs.reshape(rows,wide),(D//rows,1))
+        parts=[lax.dot_general(aT,gT[c],NT,preferred_element_type=F32).astype(BF16) for c in range(3)]
+        asum=rs(jnp.concatenate(parts+[dwoT,tb.astype(BF16)],1)).astype(F32)
+        dq,dk,dv,do=[asum[:,c*D:(c+1)*D] for c in range(4)]
+        table=asum[:,4*D:].reshape(HEADS,BUCKETS).T
+        f=fsum.astype(F32).reshape(rows,FF//FC,2,FC)
+        di=f[:,:,0].reshape(rows,FF); du=f[:,:,1].reshape(rows,FF)
+        dg1=jnp.sum(dq*low(query_w)+dk*low(key_w)+dv*low(value_w),axis=1)/low(norm1_gain)
+        dg2=jnp.sum(di*low(ffn_in),axis=1)/low(norm2_gain)
+    return (out,dx,dg1,dq,dk,dv,do.T,table,dg2,di,du.T)
 
 def solution(mesh):
     P=jax.sharding.PartitionSpec
     r=P(BOTH,None); v=P(BOTH); c=P(None,BOTH)
-    return jax.shard_map(body,mesh=mesh,in_specs=(r,v,v,r,r,r,c,P(),v,r,c,r),out_specs=(r,r,v,r,r,r,c,P(),v,r,c),check_vma=False)
+    return jax.shard_map(functools.partial(body,(mesh.shape["dp"],mesh.shape["fsdp"])),mesh=mesh,in_specs=(r,v,v,r,r,r,c,P(),v,r,c,r),out_specs=(r,r,v,r,r,r,c,P(),v,r,c),check_vma=False)

time: 615 us -> 370 us (0.60)
  waiting for transfers between devices: 324 us -> 74.4 us
  starting transfers between devices: 0.16 us -> 17.4 us
  other arithmetic: 19.2 us -> 3.49 us
  Pallas kernels: 238 us -> 253 us
  local copies, waits for them, and re-layouts: 18.4 us -> 6.15 us
    reduce_scatter x1, waiting for transfers between devices: 142 us -> 0.01 us  [rs(): return lax.psum_scatter(x, BOTH, scatter_dimension=0, tiled=True)]
    unnamed x5 -> x2, waiting for transfers between devices: 88.1 us -> 0.03 us
    ppermute x0 -> x11, waiting for transfers between devices: none -> 74.4 us  [swap(): return lax.ppermute(x, axis, [(i, i ^ f(i)) for i in range(n)])]
    all_gather x1 -> x0, waiting for transfers between devices: 51.3 us -> none  [body(): wa = lax.all_gather(pa, BOTH, axis=0, tiled=True)]
    all_gather x1, waiting for transfers between devices: 42.9 us -> 0.01 us  [body(): wb = lax.all_gather(pb, BOTH, axis=0, tiled=True)]
    ppermute x0 -> x11, starting transfers between devices: none -> 17.3 us  [swap(): return lax.ppermute(x, axis, [(i, i ^ f(i)) for i in range(n)])]
    pallas_call x2 -> x7, Pallas kernels: 40.4 us -> 54.4 us  [the longest x1 16.2 us: grads_call(): pl.pallas_call(grads_kernel, grid_spec=pltpu.PrefetchScalarGridSpec(num_s...]
    concatenate x2 -> x3, other arithmetic: 9.69 us -> 1.11 us  [the longest x1 0.93 us: gather_pieces(): a = jnp.concatenate([a, swap(a, 'dp', 2)], 0)]
  transfers between devices with their start and end apart: 4 -> 13, of which waited for: 4 -> 10; matrix products, arithmetic and copies ran while one was open for 3% -> 1% of each run, Pallas kernels for 9% -> 44%
where the time goes in v2:
time: 370 us; the launch traced here: 369 us
  Pallas kernels  253 us (68%)
  waiting for transfers between devices  74.4 us (20%)
  starting transfers between devices  17.4 us (5%)
  between operations  14.1 us (4%)
  local copies, waits for them, and re-layouts  6.15 us (2%)
    pallas_call x1, Pallas kernels, ffn_call(): pl.pallas_call(functools.partial(ffn_kernel, FC=FC, SUB=SUB, nc=nc, nt=nt...  79 us
    ppermute x11, waiting for transfers between devices, swap(): return lax.ppermute(x, axis, [(i, i ^ f(i)) for i in range(n)])  74.4 us
    pallas_call x1, Pallas kernels, bwd2_call(): pl.pallas_call(functools.partial(bwd2_kernel, HP=HP, nb=n, tabmode=tabmod...  55.6 us
    pallas_call x1, Pallas kernels, fwd2_call(): pl.pallas_call(functools.partial(fwd2_kernel, HP=HP, mode=mode), grid_spe...  32.5 us
    ppermute x11, starting transfers between devices, swap(): return lax.ppermute(x, axis, [(i, i ^ f(i)) for i in range(n)])  17.3 us
    pallas_call x1, Pallas kernels, grads_call(): pl.pallas_call(grads_kernel, grid_spec=pltpu.PrefetchScalarGridSpec(num_s...  16.2 us
    pallas_call x1, Pallas kernels, last_call(): pl.pallas_call(last_kernel, grid=(nt,), in_specs=[row, row, pl.BlockSpec(...  15.7 us
    pallas_call x1, Pallas kernels, project2_call(): pl.pallas_call(project2_kernel, grid_spec=pltpu.PrefetchScalarGridSpec(nu...  15.1 us
  transfers between devices with their start and end apart: 13, of which 10 were waited for; matrix products, arithmetic and copies ran while one was open for 1% of the time, Pallas kernels for 44%

profile of v2, /device:TPU:0, one launch (start us, length us, event | category | flops | bytes accessed | tf_op | source)
XLA Modules:
  0.0 368.7 jit_solution(1928020203836276451)
XLA Ops:
  7.2 1.9 pack_feed_forward.1
  10.9 4.0 %collective-permute-start = (bf16[1,24,2432]{2,1,0:T(8,128)(2,1)}, bf16[1,24,2432]{2,1,0:T(8,128)(2,1)S(1)}, u32[]{:S(2)}, u32[]{:S(2)}) collective-permute-start(bf16[1,24,2432]{2,1,0:T(8,128)(2,1)} %bitcast.15), channel_id=1, source_target_pairs={{0,16},{8,24},{16,0},{24,8},{1,17},{9,25},{17,1},{25,9},{2,18},{10... | collective-permute-start | bytes 350216 | tf_op jit(solution)/shard_map/ppermute | solution.py:442
  14.9 5.9 %collective-permute-done = bf16[1,24,2432]{2,1,0:T(8,128)(2,1)S(1)} collective-permute-done((bf16[1,24,2432]{2,1,0:T(8,128)(2,1)}, bf16[1,24,2432]{2,1,0:T(8,128)(2,1)S(1)}, u32[]{:S(2)}, u32[]{:S(2)}) %collective-permute-start) | collective-permute-done | bytes 116768 | tf_op jit(solution)/shard_map/ppermute | solution.py:442
  22.6 8.6 %bias.1.bias_ref = f32[12,512,512]{2,1,0:T(8,128)} custom-call(f32[12,32]{1,0:T(8,128)} %bitcast.22), custom_call_target="tpu_custom_call" | custom-call | tf_op jit(solution)/shard_map/bias/pallas_call | solution.py:49
  31.2 1.7 collective-permute-done.1
  34.5 7.2 %collective-permute-done.2 = bf16[4,24,2432]{2,1,0:T(8,128)(2,1)S(1)} collective-permute-done((bf16[4,24,2432]{2,1,0:T(8,128)(2,1)S(1)}, bf16[4,24,2432]{2,1,0:T(8,128)(2,1)S(1)}, u32[]{:S(2)}, u32[]{:S(2)}) %collective-permute-start.2) | collective-permute-done | bytes 466976 | tf_op jit(solution)/shard_map/ppermute | solution.py:442
  43.2 16.9 %collective-permute-done.3.b_ref = bf16[8,24,2432]{2,1,0:T(8,128)(2,1)S(1)} collective-permute-done((bf16[8,24,2432]{2,1,0:T(8,128)(2,1)S(1)}, bf16[8,24,2432]{2,1,0:T(8,128)(2,1)S(1)}, u32[]{:S(2)}, u32[]{:S(2)}) %collective-permute-start.3) | collective-permute-done | bytes 933920 | tf_op jit(solution)/shard_map/ppermute | solution.py:442
  60.1 2.1 collective-permute-start.5
  64.5 15.1 %project.1 = (bf16[768,2048]{1,0:T(8,128)(2,1)}, bf16[2304,2048]{1,0:T(8,128)(2,1)}, bf16[768,2432]{1,0:T(8,128)(2,1)}) custom-call(s32[2]{0:T(128)} %pad_add_fusion.at_ref, bf16[2048,768]{1,0:T(8,128)(2,1)} %x_ref.5, bf16[8,24,2432]{2,1,0:T(8,128)(2,1)} %copy-done.4, bf16[8,24,2432]{2,1,0:T(8,128)(2,1)} %copy-done.6, bf16[8,24,2432]{2,1,0:T(8,128)(2,1)} %copy-done.7, ...), custom_call_target="tpu_custom_call" | custom-call | tf_op jit(solution)/shard_map/project/pallas_call | solution.py:496
  79.6 32.5 %attend.1 = (bf16[768,2048]{1,0:T(8,128)(2,1)}, f32[12,1,2048]{2,1,0:T(1,128)}) custom-call(s32[4]{0:T(128)} %flags_ref.3, bf16[2304,2048]{1,0:T(8,128)(2,1)} %get-tuple-element.43.q_ref.k_ref.v_ref, bf16[2304,2048]{1,0:T(8,128)(2,1)} %get-tuple-element.43.q_ref.k_ref.v_ref, bf16[2304,2048]{1,0:T(8,128)(2,1)} %get-tuple-element.43.q_ref.k_ref.v_ref, ...), custom_call_target="tpu_custom_call" | custom-call | tf_op jit(solution)/shard_map/attend/pallas_call | solution.py:180
  112.1 8.6 %middle.1 = (f32[2048,768]{1,0:T(8,128)}, bf16[2048,768]{1,0:T(8,128)(2,1)S(1)}, bf16[4,768,512]{2,1,0:T(8,128)(2,1)}) custom-call(bf16[2048,768]{1,0:T(8,128)(2,1)} %x_ref.5, bf16[768,2048]{1,0:T(8,128)(2,1)} %get-tuple-element.45.oT_ref, bf16[768,6912]{1,0:T(8,128)(2,1)} %all-gather.2.cloned.1.call-done.wo_ref.win_ref.wout_ref, ...), custom_call_target="tpu_custom_call" | custom-call | tf_op jit(solution)/shard_map/middle/pallas_call | solution.py:311
  122.4 79.0 %feed_forward.1 = (bf16[2048,768]{1,0:T(8,128)(2,1)}, f32[2048,768]{1,0:T(8,128)}, bf16[768,6144]{1,0:T(8,128)(2,1)}) custom-call(bf16[2048,768]{1,0:T(8,128)(2,1)} %copy-done.1, bf16[4,768,512]{2,1,0:T(8,128)(2,1)} %get-tuple-element.48.bT_ref, bf16[2048,768]{1,0:T(8,128)(2,1)} %dy_ref.3, f32[2048,768]{1,0:T(8,128)} %get-tuple-element.49.m_ref, ...), custom_call_target="tpu_custom_call" | custom-call | tf_op jit(solution)/shard_map/feed_forward/pallas_call | solution.py:369
  201.5 14.5 %middle_back.1 = (f32[2048,768]{1,0:T(8,128)}, bf16[768,2048]{1,0:T(8,128)(2,1)S(1)}, bf16[768,768]{1,0:T(8,128)(2,1)S(1)}) custom-call(bf16[2048,768]{1,0:T(8,128)(2,1)} %dy_ref.3, f32[2048,768]{1,0:T(8,128)} %get-tuple-element.52.db_ref, f32[2048,768]{1,0:T(8,128)} %get-tuple-element.49.m_ref, bf16[768,2048]{1,0:T(8,128)(2,1)} %get-tuple-element.45.oT_ref, ...), custom_call_target="tpu_custom_call" | custom-call | tf_op jit(solution)/shard_map/middle_back/pallas_call | solution.py:397
  217.5 55.6 %attend_back.1 = (bf16[3,768,2048]{2,1,0:T(8,128)(2,1)}, f32[12,8,128]{2,1,0:T(8,128)}) custom-call(s32[4]{0:T(128)} %flags_ref.3, bf16[2304,2048]{1,0:T(8,128)(2,1)} %get-tuple-element.43.q_ref.k_ref.v_ref, bf16[2304,2048]{1,0:T(8,128)(2,1)} %get-tuple-element.43.q_ref.k_ref.v_ref, bf16[2304,2048]{1,0:T(8,128)(2,1)} %get-tuple-element.43.q_ref.k_ref.v_ref, ...), custom_call_target="tpu_custom_call" | custom-call | tf_op jit(solution)/shard_map/attend_back/pallas_call | solution.py:268
  273.9 16.2 %weight_grads.1 = (bf16[16,24,3328]{2,1,0:T(8,128)(2,1)S(1)}, bf16[16,24,3328]{2,1,0:T(8,128)(2,1)}) custom-call(s32[2]{0:T(128)S(1)} %copy-done.3, bf16[768,2048]{1,0:T(8,128)(2,1)} %get-tuple-element.51.aT_ref, bf16[3,768,2048]{2,1,0:T(8,128)(2,1)} %get-tuple-element.55.g_ref, bf16[768,768]{1,0:T(8,128)(2,1)S(1)} %get-tuple-element.56.wo_ref, ...), custom_call_target="tpu_custom_call" | custom-call | tf_op jit(solution)/shard_map/weight_grads/pallas_call | solution.py:539
  290.5 4.7 %collective-permute-done.6 = bf16[16,24,3328]{2,1,0:T(8,128)(2,1)S(1)} collective-permute-done((bf16[16,24,3328]{2,1,0:T(8,128)(2,1)}, bf16[16,24,3328]{2,1,0:T(8,128)(2,1)S(1)}, u32[]{:S(2)}, u32[]{:S(2)}) %collective-permute-start.6) | collective-permute-done | bytes 2555936 | tf_op jit(solution)/shard_map/ppermute | solution.py:442
  296.9 15.7 %project_back.1 = bf16[2048,768]{1,0:T(8,128)(2,1)} custom-call(bf16[2048,768]{1,0:T(8,128)(2,1)} %x_ref.5, f32[2048,768]{1,0:T(8,128)} %get-tuple-element.60.dm_ref, bf16[3,768,2048]{2,1,0:T(8,128)(2,1)} %get-tuple-element.55.g_ref, bf16[768,2432]{1,0:T(8,128)(2,1)} %get-tuple-element.46.ga_ref.w_ref), custom_call_target="tpu_custom_call" | custom-call | flops 7247757312 | bytes 31457280 | tf_op jit(solution)/shard_map/project_back/pallas_call | solution.py:416
  312.6 4.7 %collective-permute-done.7 = bf16[8,24,3328]{2,1,0:T(8,128)(2,1)S(1)} collective-permute-done((bf16[8,24,3328]{2,1,0:T(8,128)(2,1)S(1)}, bf16[8,24,3328]{2,1,0:T(8,128)(2,1)S(1)}, u32[]{:S(2)}, u32[]{:S(2)}) %collective-permute-start.7) | collective-permute-done | bytes 1277984 | tf_op jit(solution)/shard_map/ppermute | solution.py:442
  318.9 9.2 %collective-permute-done.8 = bf16[4,24,3328]{2,1,0:T(8,128)(2,1)S(1)} collective-permute-done((bf16[4,24,3328]{2,1,0:T(8,128)(2,1)S(1)}, bf16[4,24,3328]{2,1,0:T(8,128)(2,1)S(1)}, u32[]{:S(2)}, u32[]{:S(2)}) %collective-permute-start.8) | collective-permute-done | bytes 639008 | tf_op jit(solution)/shard_map/ppermute | solution.py:442
  328.2 3.0 collective-permute-start.9
  331.3 13.3 %collective-permute-done.9 = bf16[2,24,3328]{2,1,0:T(8,128)(2,1)S(1)} collective-permute-done((bf16[2,24,3328]{2,1,0:T(8,128)(2,1)S(1)}, bf16[2,24,3328]{2,1,0:T(8,128)(2,1)S(1)}, u32[]{:S(2)}, u32[]{:S(2)}) %collective-permute-start.9) | collective-permute-done | bytes 319520 | tf_op jit(solution)/shard_map/ppermute | solution.py:442
  346.9 9.1 %collective-permute-done.10 = bf16[1,24,3328]{2,1,0:T(8,128)(2,1)S(1)} collective-permute-done((bf16[1,24,3328]{2,1,0:T(8,128)(2,1)S(1)}, bf16[1,24,3328]{2,1,0:T(8,128)(2,1)S(1)}, u32[]{:S(2)}, u32[]{:S(2)}) %collective-permute-start.10) | collective-permute-done | bytes 159776 | tf_op jit(solution)/shard_map/ppermute | solution.py:442
  356.7 1.9 finish_attention.1
  360.0 1.9 finish_feed_forward.1
  (44 shorter events, 21.3 us)
Async XLA Ops:
  7.2 104.9 %all-gather.2.cloned.1.call-start = ((), (), s32[]{:S(2)}) async-start(), calls=%async_computation.1 | async-start | bytes 10948608 | tf_op jit(solution)/shard_map/all_gather | solution.py:602
  9.1 350.8 %reduce-scatter.2.cloned.1.call-start = ((), (), s32[]{:S(2)}) async-start(), calls=%async_computation.2 | async-start | bytes 9732096 | tf_op jit(solution)/shard_map/reduce_scatter | solution.py:618
  10.9 9.9 %collective-permute-start = (bf16[1,24,2432]{2,1,0:T(8,128)(2,1)}, bf16[1,24,2432]{2,1,0:T(8,128)(2,1)S(1)}, u32[]{:S(2)}, u32[]{:S(2)}) collective-permute-start(bf16[1,24,2432]{2,1,0:T(8,128)(2,1)} %bitcast.15), channel_id=1, source_target_pairs={{0,16},{8,24},{16,0},{24,8},{1,17},{9,25},{17,1},{25,9},{2,18},{10... | collective-permute-start | bytes 350216 | tf_op jit(solution)/shard_map/ppermute | solution.py:442
  21.7 11.2 %collective-permute-start.1 = (bf16[2,24,2432]{2,1,0:T(8,128)(2,1)S(1)}, bf16[2,24,2432]{2,1,0:T(8,128)(2,1)S(1)}, u32[]{:S(2)}, u32[]{:S(2)}) collective-permute-start(bf16[2,24,2432]{2,1,0:T(8,128)(2,1)S(1)} %pad_maximum_fusion.2), channel_id=1, source_target_pairs={{0,8},{8,0},{16,24},{24,16},{1,9},{9,1},{17,25},{25,17},{2,10},{10... | collective-permute-start | bytes 700424 | tf_op jit(solution)/shard_map/ppermute | solution.py:442
  22.6 10.3 %copy-start.5 = (bf16[24,2432]{1,0:T(8,128)(2,1)S(1)}, bf16[24,2432]{1,0:T(8,128)(2,1)}, u32[]{:S(2)}) copy-start(bf16[24,2432]{1,0:T(8,128)(2,1)} %pack_attention.1) | copy-start | bytes 350212
  33.0 8.6 %collective-permute-start.2 = (bf16[4,24,2432]{2,1,0:T(8,128)(2,1)S(1)}, bf16[4,24,2432]{2,1,0:T(8,128)(2,1)S(1)}, u32[]{:S(2)}, u32[]{:S(2)}) collective-permute-start(bf16[4,24,2432]{2,1,0:T(8,128)(2,1)S(1)} %pad_maximum_fusion.1), channel_id=1, source_target_pairs={{0,2},{1,5},{2,0},{3,7},{4,6},{5,1},{6,4},{7,3},{8,10},{9,13},{10,... | collective-permute-start | bytes 1400840 | tf_op jit(solution)/shard_map/ppermute | solution.py:442
  41.7 22.7 %copy-start.4 = (bf16[8,24,2432]{2,1,0:T(8,128)(2,1)}, bf16[8,24,2432]{2,1,0:T(8,128)(2,1)S(1)}, u32[]{:S(2)}) copy-start(bf16[8,24,2432]{2,1,0:T(8,128)(2,1)S(1)} %pad_maximum_fusion.a_ref) | copy-start | bytes 2801668
  41.8 18.4 %collective-permute-start.3 = (bf16[8,24,2432]{2,1,0:T(8,128)(2,1)S(1)}, bf16[8,24,2432]{2,1,0:T(8,128)(2,1)S(1)}, u32[]{:S(2)}, u32[]{:S(2)}) collective-permute-start(bf16[8,24,2432]{2,1,0:T(8,128)(2,1)S(1)} %pad_maximum_fusion.a_ref), channel_id=1, source_target_pairs={{0,4},{1,3},{2,6},{3,1},{4,0},{5,7},{6,2},{7,5},{8,12},{9,11},{10,... | collective-permute-start | bytes 2801672 | tf_op jit(solution)/shard_map/ppermute | solution.py:442
  43.2 19.5 %collective-permute-start.4 = (bf16[8,24,2432]{2,1,0:T(8,128)(2,1)S(1)}, bf16[8,24,2432]{2,1,0:T(8,128)(2,1)S(1)}, u32[]{:S(2)}, u32[]{:S(2)}) collective-permute-start(bf16[8,24,2432]{2,1,0:T(8,128)(2,1)S(1)} %pad_maximum_fusion.a_ref), channel_id=1, source_target_pairs={{0,1},{1,0},{2,3},{3,2},{4,5},{5,4},{6,7},{7,6},{8,9},{9,8},{10,11... | collective-permute-start | bytes 2801672 | tf_op jit(solution)/shard_map/ppermute | solution.py:442
  60.1 4.3 %copy-start.6 = (bf16[8,24,2432]{2,1,0:T(8,128)(2,1)}, bf16[8,24,2432]{2,1,0:T(8,128)(2,1)S(1)}, u32[]{:S(2)}) copy-start(bf16[8,24,2432]{2,1,0:T(8,128)(2,1)S(1)} %collective-permute-done.3.b_ref) | copy-start | bytes 2801668
  60.1 4.3 %collective-permute-start.5 = (bf16[8,24,2432]{2,1,0:T(8,128)(2,1)S(1)}, bf16[8,24,2432]{2,1,0:T(8,128)(2,1)}, u32[]{:S(2)}, u32[]{:S(2)}) collective-permute-start(bf16[8,24,2432]{2,1,0:T(8,128)(2,1)S(1)} %collective-permute-done.3.b_ref), channel_id=1, source_target_pairs={{0,1},{1,0},{2,3},{3,2},{4,5},{5,4},{6,7},{7,6},{8,9},{9,8},{10,11... | collective-permute-start | bytes 2801672 | tf_op jit(solution)/shard_map/ppermute | solution.py:442
  62.8 1.7 copy-start.7
  120.8 1.7 copy-start.1
  215.9 1.6 copy-start
  217.5 55.6 %copy-start.3 = (s32[2]{0:T(128)S(1)}, s32[2]{0:T(128)}, u32[]{:S(2)}) copy-start(s32[2]{0:T(128)} %pad_add_fusion.at_ref) | copy-start | bytes 28
  273.1 0.8 copy-start.2
  290.1 5.1 %collective-permute-start.6 = (bf16[16,24,3328]{2,1,0:T(8,128)(2,1)}, bf16[16,24,3328]{2,1,0:T(8,128)(2,1)S(1)}, u32[]{:S(2)}, u32[]{:S(2)}) collective-permute-start(bf16[16,24,3328]{2,1,0:T(8,128)(2,1)} %get-tuple-element.59), channel_id=1, source_target_pairs={{0,1},{1,0},{2,3},{3,2},{4,5},{5,4},{6,7},{7,6},{8,9},{9,8},{10,11... | collective-permute-start | bytes 7667720 | tf_op jit(solution)/shard_map/ppermute | solution.py:442
  295.8 21.5 %collective-permute-start.7 = (bf16[8,24,3328]{2,1,0:T(8,128)(2,1)S(1)}, bf16[8,24,3328]{2,1,0:T(8,128)(2,1)S(1)}, u32[]{:S(2)}, u32[]{:S(2)}) collective-permute-start(bf16[8,24,3328]{2,1,0:T(8,128)(2,1)S(1)} %get-tuple-element.85), channel_id=1, source_target_pairs={{0,2},{1,5},{2,0},{3,7},{4,6},{5,1},{6,4},{7,3},{8,10},{9,13},{10,... | collective-permute-start | bytes 3833864 | tf_op jit(solution)/shard_map/ppermute | solution.py:442
  317.6 10.5 %collective-permute-start.8 = (bf16[4,24,3328]{2,1,0:T(8,128)(2,1)S(1)}, bf16[4,24,3328]{2,1,0:T(8,128)(2,1)S(1)}, u32[]{:S(2)}, u32[]{:S(2)}) collective-permute-start(bf16[4,24,3328]{2,1,0:T(8,128)(2,1)S(1)} %get-tuple-element.87), channel_id=1, source_target_pairs={{0,4},{1,3},{2,6},{3,1},{4,0},{5,7},{6,2},{7,5},{8,12},{9,11},{10,... | collective-permute-start | bytes 1916936 | tf_op jit(solution)/shard_map/ppermute | solution.py:442
  328.2 16.4 %collective-permute-start.9 = (bf16[2,24,3328]{2,1,0:T(8,128)(2,1)S(1)}, bf16[2,24,3328]{2,1,0:T(8,128)(2,1)S(1)}, u32[]{:S(2)}, u32[]{:S(2)}) collective-permute-start(bf16[2,24,3328]{2,1,0:T(8,128)(2,1)S(1)} %get-tuple-element.89), channel_id=1, source_target_pairs={{0,8},{8,0},{16,24},{24,16},{1,9},{9,1},{17,25},{25,17},{2,10},{10... | collective-permute-start | bytes 958472 | tf_op jit(solution)/shard_map/ppermute | solution.py:442
  345.4 10.7 %collective-permute-start.10 = (bf16[1,24,3328]{2,1,0:T(8,128)(2,1)S(1)}, bf16[1,24,3328]{2,1,0:T(8,128)(2,1)S(1)}, u32[]{:S(2)}, u32[]{:S(2)}) collective-permute-start(bf16[1,24,3328]{2,1,0:T(8,128)(2,1)S(1)} %get-tuple-element.90), channel_id=1, source_target_pairs={{0,16},{8,24},{16,0},{24,8},{1,17},{9,25},{17,1},{25,9},{2,18},{10... | collective-permute-start | bytes 479240 | tf_op jit(solution)/shard_map/ppermute | solution.py:442
  356.0 0.7 copy-start.8
Sparse Core Ops, SparseCore 0:
  10.9 98.0 all-gather.1
  201.6 145.2 reduce-scatter.1

commit v3 on v2

--- a/solution.py
+++ b/solution.py
@@ -419,7 +419,91 @@
         cost_estimate=pl.CostEstimate(flops=2*T*D*3*D,bytes_accessed=20*T*D,transcendentals=0),
         compiler_params=pltpu.CompilerParams(vmem_limit_bytes=56*2**20))(x,dm,gT,w)
 
+def block_kernel(at_ref,x_ref,oT_ref,dy_ref,ga_ref,wo_ref,win_ref,wout_ref,
+                 out_ref,dm_ref,doT_ref,dwo_ref,*rest,FC,SUB,nc,nt,legs):
+    dw_ref,b_s,bT_s,dyT,oacc,dacc,ain,aout,awo=rest
+    c=pl.program_id(0); t=pl.program_id(1)
+    rows=pl.ds(t*BLOCK,BLOCK)
+    def middle():
+        return x_ref[...].astype(F32)+dot(oT_ref[...].T,wo_ref[...],NT)
+    @pl.when(c==0)
+    def _():
+        m=middle()
+        b=(m*rms(m)*row_of(ga_ref[...],1)).astype(BF16)
+        b_s[t]=b
+        bT_s[t]=b.T
+        dyT[t]=dy_ref[rows,:].T
+        oacc[rows,:]=m
+        dacc[rows,:]=jnp.zeros((BLOCK,D),F32)
+    b=b_s[t]; dy=dy_ref[rows,:]
+    G=[];DU=[]
+    n=FC//SUB
+    U=[dot(b,win_ref[:,s*SUB:(s+1)*SUB]) for s in range(n)]
+    DG=[dot(dy,wout_ref[:,s*SUB:(s+1)*SUB]) for s in range(n)]
+    @pl.when(t==0)
+    def _():
+        ain[...]=jnp.zeros_like(ain); aout[...]=jnp.zeros_like(aout)
+    for s in range(n):
+        g,pull=gate(U[s],"erf")
+        g=g.astype(BF16)
+        du=(DG[s]*pull).astype(BF16)
+        sl=slice(s*SUB,(s+1)*SUB)
+        aout[:,sl]+=dot(dyT[t],g)
+        ain[:,sl]+=dot(bT_s[t],du)
+        G.append(g);DU.append(du)
+    g=jnp.concatenate(G,1);du=jnp.concatenate(DU,1)
+    oacc[rows,:]+=dot(g,wout_ref[...],NT)
+    dacc[rows,:]+=dot(du,win_ref[...],NT)
+    @pl.when(t==nt-1)
+    def _():
+        if legs:
+            R=dw_ref.shape[1]
+            for s in range(32):
+                z=at_ref[0]^((s>>1)&1)^((s&1)<<1)
+                at=pl.ds(pl.multiple_of((z*8+(s>>2))*R,8),R)
+                dw_ref[s,:,:FC]=ain[at,:].astype(BF16)
+                dw_ref[s,:,FC:]=aout[at,:].astype(BF16)
+        else:
+            dw_ref[:,:FC]=ain[...].astype(BF16)
+            dw_ref[:,FC:]=aout[...].astype(BF16)
+    @pl.when((c==nc-1)&(t==0))
+    def _(): awo[...]=jnp.zeros_like(awo)
+    @pl.when(c==nc-1)
+    def _():
+        out_ref[...]=oacc[rows,:].astype(BF16)
+        m=middle()
+        db=dacc[rows,:]
+        r=rms(m); n2=m*r
+        dn=db*row_of(ga_ref[...],1)
+        dm=dy.astype(F32)+r*(dn-n2*jnp.mean(dn*n2,axis=-1,keepdims=True))
+        dm_ref[...]=dm
+        dmb=dm.astype(BF16)
+        awo[...]+=dot(dmb.T,oT_ref[...],NT)
+        doT_ref[...]=dot(dmb,wo_ref[...]).astype(BF16).T
+    @pl.when((c==nc-1)&(t==nt-1))
+    def _(): dwo_ref[...]=awo[...].astype(BF16)
+def block_call(x,oT,dy,gains,wo,win,wout,core,legs,FC=768,SUB=256):
+    T=x.shape[0]; nt=T//BLOCK; FF=3072; nc=FF//FC
+    last=lambda c,t:jnp.where(c==nc-1,t,0)
+    ends=lambda c,t:jnp.where((c==0)|(c==nc-1),t,nt-1)
+    one=pl.Buffered(1)
+    sd=jax.ShapeDtypeStruct; BS=pl.BlockSpec; R=D//32
+    return pl.pallas_call(functools.partial(block_kernel,FC=FC,SUB=SUB,nc=nc,nt=nt,legs=legs),
+        grid_spec=pltpu.PrefetchScalarGridSpec(num_scalar_prefetch=1,grid=(nc,nt),
+        in_specs=[BS((BLOCK,D),lambda c,t,at:(ends(c,t),0)),BS((D,BLOCK),lambda c,t,at:(0,ends(c,t))),
+            BS((T,D),lambda c,t,at:(0,0),pipeline_mode=one),
+            BS((D,GA),lambda c,t,at:(0,gains[1]),pipeline_mode=one),BS((D,D),lambda c,t,at:(0,wo[1]),pipeline_mode=one),
+            BS((D,FC),lambda c,t,at:(0,c+win[1]*D//FC)),BS((D,FC),lambda c,t,at:(0,c+wout[1]*D//FC))],
+        out_specs=[BS((BLOCK,D),lambda c,t,at:(last(c,t),0)),BS((BLOCK,D),lambda c,t,at:(last(c,t),0)),BS((D,BLOCK),lambda c,t,at:(0,last(c,t))),
+            BS((D,D),lambda c,t,at:(0,0))]+([BS((32,R,2*FC),lambda c,t,at:(0,0,c))] if legs else [BS((D,2*FC),lambda c,t,at:(0,c))]),
+        scratch_shapes=[pltpu.VMEM((nt,BLOCK,D),BF16),pltpu.VMEM((nt,D,BLOCK),BF16),pltpu.VMEM((nt,D,BLOCK),BF16),
+            pltpu.VMEM((T,D),F32),pltpu.VMEM((T,D),F32),pltpu.VMEM((D,FC),F32),pltpu.VMEM((D,FC),F32),pltpu.VMEM((D,D),F32)]),
+        out_shape=[sd((T,D),BF16),sd((T,D),F32),sd((D,T),BF16),sd((D,D),BF16)]+([sd((32,R,2*FF),BF16)] if legs else [sd((D,2*FF),BF16)]),
+        name="feed_forward",
+        compiler_params=pltpu.CompilerParams(vmem_limit_bytes=62*2**20+2**19))(core,x,oT,dy,gains[0],wo[0],win[0],wout[0])
+
 GW=3*D+GA
+INNER=("yx","core")
 def pack_a_kernel(q_ref,k_ref,v_ref,g1_ref,g2_ref,o_ref):
     for c,ref in enumerate((q_ref,k_ref,v_ref)):
         o_ref[:,c*D:(c+1)*D]=ref[...].astype(BF16)
@@ -437,7 +521,7 @@
     return pl.pallas_call(pack_b_kernel,out_shape=jax.ShapeDtypeStruct((wi.shape[0],D+2*wi.shape[1]),BF16),name="pack_feed_forward")(wo.T,wi,wu.T)
 
 def swap(x,axis,mask):
-    n=8 if axis=="fsdp" else 4
+    n=8 if axis==INNER else 4
     f=mask if callable(mask) else (lambda i:mask)
     return lax.ppermute(x,axis,[(i,i^f(i)) for i in range(n)])
 first_leg=lambda i: 4 if i&1 else 2
@@ -448,13 +532,13 @@
     got=swap(a,"dp",1)
     got,beside=lax.optimization_barrier((got,beside))
     a=jnp.concatenate([a,got],0)
-    a=jnp.concatenate([a,swap(a,"fsdp",first_leg)],0)
-    b=swap(a,"fsdp",second_leg)
-    c=swap(a,"fsdp",1)
-    d=swap(b,"fsdp",1)
+    a=jnp.concatenate([a,swap(a,INNER,first_leg)],0)
+    b=swap(a,INNER,second_leg)
+    c=swap(a,INNER,1)
+    d=swap(b,INNER,1)
     return (a,b,c,d),beside
 def place():
-    f=lax.axis_index("fsdp"); z=lax.axis_index("dp")
+    f=lax.axis_index(INNER); z=lax.axis_index("dp")
     return jnp.stack([f,z]).astype(jnp.int32)
 def assemble_rows(at_ref,pieces,put):
     f=at_ref[0]; z=at_ref[1]
@@ -504,50 +588,49 @@
 
 
 def add(a,b): return (a.astype(F32)+b.astype(F32)).astype(BF16)
-WB=256
-GN=4*D+WB
+GN=4*D+128
 def slot_rows(s,f,z,core):
     x=(f>>1)&1; y=f>>2
     one=s>>3; two=(s>>2)&1
     dx=jnp.where(core==0,one,two); dy=jnp.where(core==0,two,one)
     zz=z^((s>>1)&1)^((s&1)<<1)
     return (zz*8+(y^dy)*4+(x^dx)*2+core)
+def slot_table():
+    f=lax.axis_index(INNER); z=lax.axis_index("dp")
+    s=jnp.arange(16,dtype=jnp.int32); core=f&1
+    return jnp.stack([slot_rows(s,f,z,core),slot_rows(s,f,z,1-core)]).astype(jnp.int32)
 def grads_kernel(at_ref,aT_ref,g_ref,wo_ref,tab_ref,keep_ref,send_ref,v_ref):
     c=pl.program_id(0)
     R=keep_ref.shape[1]
-    @pl.when(c<9)
+    @pl.when(c<3)
     def _(): v_ref[...]=dot(aT_ref[...],g_ref[0],NT)
-    @pl.when((c>=9)&(c<12))
+    @pl.when(c==3)
     def _(): v_ref[...]=wo_ref[...].astype(F32)
-    @pl.when(c<12)
-    def _():
-        f=at_ref[0]; z=at_ref[1]; core=f&1
+    @pl.when(c<4)
+    def _():
         for s in range(16):
-            for ref,cc in ((keep_ref,core),(send_ref,1-core)):
-                j=slot_rows(s,f,z,cc)
-                ref[s]=v_ref[pl.ds(pl.multiple_of(j*R,8),R),:].astype(BF16)
-    @pl.when(c==12)
-    def _():
-        t=jnp.concatenate([tab_ref[h,:1,:] for h in range(HEADS)]+[jnp.zeros((R-HEADS,128),F32)],0)
-        t=jnp.concatenate([t,jnp.zeros((R,WB-128),F32)],1).astype(BF16)
+            for q,ref in enumerate((keep_ref,send_ref)):
+                ref[s]=v_ref[pl.ds(pl.multiple_of(at_ref[q,s]*R,8),R),:].astype(BF16)
+    @pl.when(c==4)
+    def _():
+        t=jnp.concatenate([tab_ref[h,:1,:] for h in range(HEADS)]+[jnp.zeros((R-HEADS,128),F32)],0).astype(BF16)
         for s in range(16):
-            keep_ref[s]=t; send_ref[s]=t
+            keep_ref[s,:,:128]=t; send_ref[s,:,:128]=t
 def grads_call(at,aT,gT,dwoT,tab):
     T=aT.shape[1]; R=D//32
-    nb=D//WB
-    out=pl.BlockSpec((16,R,WB),lambda c,at:(0,0,c))
+    out=pl.BlockSpec((16,R,D),lambda c,at:(0,0,c))
     return pl.pallas_call(grads_kernel,
-        grid_spec=pltpu.PrefetchScalarGridSpec(num_scalar_prefetch=1,grid=(GN//WB,),
+        grid_spec=pltpu.PrefetchScalarGridSpec(num_scalar_prefetch=1,grid=(5,),
         in_specs=[pl.BlockSpec((D,T),lambda c,at:(0,0),pipeline_mode=pl.Buffered(1)),
-                  pl.BlockSpec((1,WB,T),lambda c,at:(jnp.minimum(c,8)//nb,jnp.minimum(c,8)%nb,0)),
-                  pl.BlockSpec((D,WB),lambda c,at:(0,jnp.clip(c-9,0,2))),
+                  pl.BlockSpec((1,D,T),lambda c,at:(jnp.minimum(c,2),0,0)),
+                  pl.BlockSpec((D,D),lambda c,at:(0,0),pipeline_mode=pl.Buffered(1)),
                   pl.BlockSpec((HEADS,8,128),lambda c,at:(0,0,0))],
-        out_specs=[out,out],scratch_shapes=[pltpu.VMEM((D,WB),F32)]),
+        out_specs=[out,out],scratch_shapes=[pltpu.VMEM((D,D),F32)]),
         out_shape=[jax.ShapeDtypeStruct((16,R,GN),BF16)]*2,name="weight_grads",
         compiler_params=pltpu.CompilerParams(vmem_limit_bytes=48*2**20))(at,aT,gT,dwoT,tab)
 def scatter_sum(keep,send,beside):
-    r=swap(send,"fsdp",1)
-    for half,axis,leg in ((8,"fsdp",first_leg),(4,"fsdp",second_leg),(2,"dp",1),(1,"dp",2)):
+    r=swap(send,INNER,1)
+    for half,axis,leg in ((8,INNER,first_leg),(4,INNER,second_leg),(2,"dp",1),(1,"dp",2)):
         out=add(keep[half:],r[half:])
         keep=add(keep[:half],r[:half])
         r=swap(out,axis,leg)
@@ -572,24 +655,26 @@
 def finish_call(a,b,wq,wk,wv,g1):
     R=a.shape[0]; sd=jax.ShapeDtypeStruct
     return pl.pallas_call(finish_kernel,out_shape=[sd((R,D),F32)]*4+[sd((BUCKETS,HEADS),F32),sd((1,R),F32)],name="finish_attention")(a,b,wq,wk,wv,g1[None])
-def finish_ffn_kernel(s_ref,w_ref,g_ref,i_ref,o_ref,dg_ref,*,FC):
+def finish_ffn_kernel(s_ref,t_ref,w_ref,g_ref,i_ref,o_ref,dg_ref,*,FC):
     R=s_ref.shape[0]
     tot=None
     for c in range(w_ref.shape[1]//FC):
         sl=slice(c*FC,(c+1)*FC)
-        s=s_ref[:,2*c*FC:(2*c+1)*FC].astype(F32)
+        one=slice(2*c*FC,(2*c+1)*FC); two=slice((2*c+1)*FC,(2*c+2)*FC)
+        s=s_ref[:,one].astype(F32)+t_ref[:,one].astype(F32)
         i_ref[:,sl]=s
-        o_ref[:,sl]=s_ref[:,(2*c+1)*FC:(2*c+2)*FC].astype(F32)
+        o_ref[:,sl]=s_ref[:,two].astype(F32)+t_ref[:,two].astype(F32)
         y=jnp.sum(s*w_ref[:,sl].astype(BF16).astype(F32),axis=1,keepdims=True)
         tot=y if tot is None else tot+y
     rowv=jnp.broadcast_to(tot,(R,128))
     rowv=jnp.concatenate([rowv,jnp.zeros((128-R,128),F32)],0).T[:1,:R]
     dg_ref[...]=rowv/g_ref[...].astype(BF16).astype(F32)
-def finish_ffn_call(s,w,g2,FC):
+def finish_ffn_call(s,t,w,g2,FC):
     R,F=w.shape; sd=jax.ShapeDtypeStruct
-    return pl.pallas_call(functools.partial(finish_ffn_kernel,FC=FC),out_shape=[sd((R,F),F32),sd((R,F),F32),sd((1,R),F32)],name="finish_feed_forward")(s,w,g2[None])
+    return pl.pallas_call(functools.partial(finish_ffn_kernel,FC=FC),out_shape=[sd((R,F),F32),sd((R,F),F32),sd((1,R),F32)],name="finish_feed_forward")(s,t,w,g2[None])
 
 BOTH=("dp","fsdp")
+ALL=("dp","yx","core")
 FC=768
 def low(v): return v.astype(BF16).astype(F32)
 def body(sizes,hidden,long_flags,norm1_gain,query_w,key_w,value_w,out_w,bias_table,norm2_gain,ffn_in,ffn_out,out_grad):
@@ -599,7 +684,7 @@
     if legs:
         pa=pack_a(query_w,key_w,value_w,norm1_gain,norm2_gain)
         pb=pack_b(out_w,ffn_in,ffn_out)
-        wb=lax.all_gather(pb,BOTH,axis=0,tiled=True)
+        wb=lax.all_gather(pb,ALL,axis=0,tiled=True)
         at=place()
         pieces,bias=gather_pieces(pa,bias_call(bias_table))
         aT,qkvT,wa=project2_call(hidden,pieces,at)
@@ -613,17 +698,19 @@
         aT,qkvT=qkv_call(hidden,wa)
     oT,lse=fwd2_call(long_flags,qkvT,bias,HP=4,mode="norm")
     GB=3*D//GA
-    m,b,bT=mid_call(hidden,oT,(wb,0),(wa,GB))
-    out,db,dffn=ffn_call(b,bT,out_grad,m,(wb,1),(wb,5),FC=FC)
-    def rs(x): return lax.psum_scatter(x,BOTH,scatter_dimension=0,tiled=True)
-    fsum=rs(dffn)
-    dm,doT,dwoT=post_call(out_grad,db,m,oT,(wb,0),(wa,GB))
+    z=(lax.axis_index("dp") if legs else jnp.zeros((),jnp.int32)).reshape(1)
+    out,dm,doT,dwoT,dffn=block_call(hidden,oT,out_grad,(wa,GB),(wb,0),(wb,1),(wb,5),z,legs,FC=FC)
+    def rs(x,axes=BOTH): return lax.psum_scatter(x,axes,scatter_dimension=0,tiled=True)
+    fsum=rs(dffn.reshape(D,2*FF),INNER if legs else BOTH)
     gT,tab=bwd2_call(long_flags,qkvT,doT,lse,bias,HP=4)
     if legs:
-        keep,send=grads_call(at,aT,gT,dwoT,tab)
+        keep,send=grads_call(slot_table(),aT,gT,dwoT,tab)
         a,b2,dx=scatter_sum(keep,send,last_call(hidden,dm,gT,wa))
+        h=fsum.reshape(4,rows,2*FF)
+        r=swap(h[2:],"dp",1)
+        fa,fb=add(h[0],r[0]),swap(add(h[1],r[1]),"dp",2)
         dq,dk,dv,do,table,dg1=finish_call(a,b2,query_w,key_w,value_w,norm1_gain)
-        di,du,dg2=finish_ffn_call(fsum,ffn_in,norm2_gain,FC)
+        di,du,dg2=finish_ffn_call(fa,fb,ffn_in,norm2_gain,FC)
         dg1=dg1[0]; dg2=dg2[0]
     else:
         dx=last_call(hidden,dm,gT,wa)
@@ -642,5 +729,10 @@
 
 def solution(mesh):
     P=jax.sharding.PartitionSpec
-    r=P(BOTH,None); v=P(BOTH); c=P(None,BOTH)
-    return jax.shard_map(functools.partial(body,(mesh.shape["dp"],mesh.shape["fsdp"])),mesh=mesh,in_specs=(r,v,v,r,r,r,c,P(),v,r,c,r),out_specs=(r,r,v,r,r,r,c,P(),v,r,c),check_vma=False)
+    sizes=(mesh.shape["dp"],mesh.shape["fsdp"])
+    axes=BOTH
+    if sizes==(4,8):
+        mesh=jax.sharding.Mesh(mesh.devices.reshape(4,4,2),ALL)
+        axes=ALL
+    r=P(axes,None); v=P(axes); c=P(None,axes)
+    return jax.shard_map(functools.partial(body,sizes),mesh=mesh,in_specs=(r,v,v,r,r,r,c,P(),v,r,c,r),out_specs=(r,r,v,r,r,r,c,P(),v,r,c),check_vma=False)

time: 370 us -> 355 us (0.959)
  Pallas kernels: 253 us -> 242 us
  waiting for transfers between devices: 74.4 us -> 66.8 us
  starting transfers between devices: 17.4 us -> 22.8 us
    pallas_call x3 -> x1, Pallas kernels: 102 us -> 94.4 us  [block_call(): pl.pallas_call(functools.partial(block_kernel, FC=FC, SUB=SUB, nc=nc, nt=...]
    ppermute x11 -> x13, waiting for transfers between devices: 74.4 us -> 66.7 us  [swap(): return lax.ppermute(x, axis, [(i, i ^ f(i)) for i in range(n)])]
    ppermute x11 -> x13, starting transfers between devices: 17.3 us -> 22.7 us  [swap(): return lax.ppermute(x, axis, [(i, i ^ f(i)) for i in range(n)])]
  transfers between devices with their start and end apart: 13 -> 15, of which waited for: 10 -> 11; matrix products, arithmetic and copies ran while one was open for 1% -> 2% of each run, Pallas kernels for 44% -> 41%
where the time goes in v3:
time: 355 us
  Pallas kernels  242 us (68%)
  waiting for transfers between devices  66.8 us (19%)
  starting transfers between devices  22.8 us (6%)
  between operations  14.2 us (4%)
  local copies, waits for them, and re-layouts  4.78 us (1%)
  other arithmetic  4.29 us (1%)
    pallas_call x1, Pallas kernels, block_call(): pl.pallas_call(functools.partial(block_kernel, FC=FC, SUB=SUB, nc=nc, nt=...  94.4 us
    ppermute x13, waiting for transfers between devices, swap(): return lax.ppermute(x, axis, [(i, i ^ f(i)) for i in range(n)])  66.7 us
    pallas_call x1, Pallas kernels, bwd2_call(): pl.pallas_call(functools.partial(bwd2_kernel, HP=HP, nb=n, tabmode=tabmod...  55.5 us
    pallas_call x1, Pallas kernels, fwd2_call(): pl.pallas_call(functools.partial(fwd2_kernel, HP=HP, mode=mode), grid_spe...  32.5 us
    ppermute x13, starting transfers between devices, swap(): return lax.ppermute(x, axis, [(i, i ^ f(i)) for i in range(n)])  22.7 us
    pallas_call x1, Pallas kernels, last_call(): pl.pallas_call(last_kernel, grid=(nt,), in_specs=[row, row, pl.BlockSpec(...  15.8 us
    pallas_call x1, Pallas kernels, project2_call(): pl.pallas_call(project2_kernel, grid_spec=pltpu.PrefetchScalarGridSpec(nu...  15.1 us
    pallas_call x1, Pallas kernels, grads_call(): pl.pallas_call(grads_kernel, grid_spec=pltpu.PrefetchScalarGridSpec(num_s...  12.9 us
  transfers between devices with their start and end apart: 15, of which 11 were waited for; matrix products, arithmetic and copies ran while one was open for 2% of the time, Pallas kernels for 41%

profile of v3, /device:TPU:0, one launch (start us, length us, event | category | flops | bytes accessed | tf_op | source)
XLA Modules:
  0.0 355.0 jit_solution(9862620222231785987)
XLA Ops:
  7.2 1.9 pack_feed_forward.1
  10.9 4.0 %collective-permute-start = (bf16[1,24,2432]{2,1,0:T(8,128)(2,1)}, bf16[1,24,2432]{2,1,0:T(8,128)(2,1)S(1)}, u32[]{:S(2)}, u32[]{:S(2)}) collective-permute-start(bf16[1,24,2432]{2,1,0:T(8,128)(2,1)} %bitcast.28), channel_id=1, source_target_pairs={{0,16},{8,24},{16,0},{24,8},{1,17},{9,25},{17,1},{25,9},{2,18},{10... | collective-permute-start | bytes 350216 | tf_op jit(solution)/shard_map/ppermute | solution.py:526
  14.9 5.9 %collective-permute-done = bf16[1,24,2432]{2,1,0:T(8,128)(2,1)S(1)} collective-permute-done((bf16[1,24,2432]{2,1,0:T(8,128)(2,1)}, bf16[1,24,2432]{2,1,0:T(8,128)(2,1)S(1)}, u32[]{:S(2)}, u32[]{:S(2)}) %collective-permute-start) | collective-permute-done | bytes 116768 | tf_op jit(solution)/shard_map/ppermute | solution.py:526
  22.6 8.6 %bias.1.bias_ref = f32[12,512,512]{2,1,0:T(8,128)} custom-call(f32[12,32]{1,0:T(8,128)} %bitcast.36), custom_call_target="tpu_custom_call" | custom-call | tf_op jit(solution)/shard_map/bias/pallas_call | solution.py:49
  31.2 1.7 collective-permute-done.1
  34.4 7.2 %collective-permute-done.2 = bf16[4,24,2432]{2,1,0:T(8,128)(2,1)S(1)} collective-permute-done((bf16[4,24,2432]{2,1,0:T(8,128)(2,1)S(1)}, bf16[4,24,2432]{2,1,0:T(8,128)(2,1)S(1)}, u32[]{:S(2)}, u32[]{:S(2)}) %collective-permute-start.2) | collective-permute-done | bytes 466976 | tf_op jit(solution)/shard_map/ppermute | solution.py:526
  43.2 16.9 %collective-permute-done.3.b_ref = bf16[8,24,2432]{2,1,0:T(8,128)(2,1)S(1)} collective-permute-done((bf16[8,24,2432]{2,1,0:T(8,128)(2,1)S(1)}, bf16[8,24,2432]{2,1,0:T(8,128)(2,1)S(1)}, u32[]{:S(2)}, u32[]{:S(2)}) %collective-permute-start.3) | collective-permute-done | bytes 933920 | tf_op jit(solution)/shard_map/ppermute | solution.py:526
  60.1 2.0 collective-permute-start.5
  64.4 15.1 %project.1 = (bf16[768,2048]{1,0:T(8,128)(2,1)}, bf16[2304,2048]{1,0:T(8,128)(2,1)}, bf16[768,2432]{1,0:T(8,128)(2,1)}) custom-call(s32[2]{0:T(128)} %pad_add_fusion.1.at_ref, bf16[2048,768]{1,0:T(8,128)(2,1)} %x_ref.5, bf16[8,24,2432]{2,1,0:T(8,128)(2,1)} %copy-done.2, bf16[8,24,2432]{2,1,0:T(8,128)(2,1)} %copy-done.5, bf16[8,24,2432]{2,1,0:T(8,128)(2,1)} %copy-done.6, ...), custom_call_target="tpu_custom_call" | custom-call | tf_op jit(solution)/shard_map/project/pallas_call | solution.py:580
  79.5 32.5 %attend.1 = (bf16[768,2048]{1,0:T(8,128)(2,1)}, f32[12,1,2048]{2,1,0:T(1,128)}) custom-call(s32[4]{0:T(128)} %flags_ref.3, bf16[2304,2048]{1,0:T(8,128)(2,1)} %get-tuple-element.39.q_ref.k_ref.v_ref, bf16[2304,2048]{1,0:T(8,128)(2,1)} %get-tuple-element.39.q_ref.k_ref.v_ref, bf16[2304,2048]{1,0:T(8,128)(2,1)} %get-tuple-element.39.q_ref.k_ref.v_ref, ...), custom_call_target="tpu_custom_call" | custom-call | tf_op jit(solution)/shard_map/attend/pallas_call | solution.py:180
  112.0 94.4 %feed_forward.1 = (bf16[2048,768]{1,0:T(8,128)(2,1)}, f32[2048,768]{1,0:T(8,128)}, bf16[768,2048]{1,0:T(8,128)(2,1)}, bf16[768,768]{1,0:T(8,128)(2,1)}, bf16[32,24,6144]{2,1,0:T(8,128)(2,1)}) custom-call(s32[1]{0:T(128)} %bitcast.at_ref, bf16[2048,768]{1,0:T(8,128)(2,1)} %x_ref.5, bf16[768,2048]{1,0:T(8,128)(2,1)} %get-tuple-element.41.oT_ref, ...), custom_call_target="tpu_custom_call" | custom-call | tf_op jit(solution)/shard_map/feed_forward/pallas_call | solution.py:491
  206.5 55.5 %attend_back.1 = (bf16[3,768,2048]{2,1,0:T(8,128)(2,1)}, f32[12,8,128]{2,1,0:T(8,128)}) custom-call(s32[4]{0:T(128)} %flags_ref.3, bf16[2304,2048]{1,0:T(8,128)(2,1)} %get-tuple-element.39.q_ref.k_ref.v_ref, bf16[2304,2048]{1,0:T(8,128)(2,1)} %get-tuple-element.39.q_ref.k_ref.v_ref, bf16[2304,2048]{1,0:T(8,128)(2,1)} %get-tuple-element.39.q_ref.k_ref.v_ref, ...), custom_call_target="tpu_custom_call" | custom-call | tf_op jit(solution)/shard_map/attend_back/pallas_call | solution.py:268
  262.8 12.9 %weight_grads.1 = (bf16[16,24,3200]{2,1,0:T(8,128)(2,1)S(1)}, bf16[16,24,3200]{2,1,0:T(8,128)(2,1)S(1)}) custom-call(s32[2,16]{1,0:T(2,128)S(1)} %pad_add_fusion.at_ref, bf16[768,2048]{1,0:T(8,128)(2,1)} %get-tuple-element.44.aT_ref, bf16[3,768,2048]{2,1,0:T(8,128)(2,1)} %get-tuple-element.47.g_ref, bf16[768,768]{1,0:T(8,128)(2,1)S(1)} %copy-done, ...), custom_call_target="tpu_custom_call" | custom-call | tf_op jit(solution)/shard_map/weight_grads/pallas_call | solution.py:622
  276.1 4.3 %collective-permute-done.6 = bf16[16,24,3200]{2,1,0:T(8,128)(2,1)S(1)} collective-permute-done((bf16[16,24,3200]{2,1,0:T(8,128)(2,1)S(1)}, bf16[16,24,3200]{2,1,0:T(8,128)(2,1)S(1)}, u32[]{:S(2)}, u32[]{:S(2)}) %collective-permute-start.6) | collective-permute-done | bytes 2457632 | tf_op jit(solution)/shard_map/ppermute | solution.py:526
  282.1 15.8 %project_back.1 = bf16[2048,768]{1,0:T(8,128)(2,1)} custom-call(bf16[2048,768]{1,0:T(8,128)(2,1)} %x_ref.5, f32[2048,768]{1,0:T(8,128)} %get-tuple-element.52.dm_ref, bf16[3,768,2048]{2,1,0:T(8,128)(2,1)} %get-tuple-element.47.g_ref, bf16[768,2432]{1,0:T(8,128)(2,1)} %get-tuple-element.42.ga_ref.w_ref), custom_call_target="tpu_custom_call" | custom-call | flops 7247757312 | bytes 31457280 | tf_op jit(solution)/shard_map/project_back/pallas_call | solution.py:416
  301.7 2.3 collective-permute-start.11
  303.9 5.2 %collective-permute-done.8 = bf16[4,24,3200]{2,1,0:T(8,128)(2,1)S(1)} collective-permute-done((bf16[4,24,3200]{2,1,0:T(8,128)(2,1)S(1)}, bf16[4,24,3200]{2,1,0:T(8,128)(2,1)S(1)}, u32[]{:S(2)}, u32[]{:S(2)}) %collective-permute-start.8) | collective-permute-done | bytes 614432 | tf_op jit(solution)/shard_map/ppermute | solution.py:526
  309.3 2.1 collective-permute-start.9
  311.4 6.7 %collective-permute-done.11 = bf16[2,24,6144]{2,1,0:T(8,128)(2,1)S(1)} collective-permute-done((bf16[2,24,6144]{2,1,0:T(8,128)(2,1)S(1)}, bf16[2,24,6144]{2,1,0:T(8,128)(2,1)S(1)}, u32[]{:S(2)}, u32[]{:S(2)}) %collective-permute-start.11) | collective-permute-done | bytes 589856 | tf_op jit(solution)/shard_map/ppermute | solution.py:526
  319.0 4.8 %collective-permute-start.12 = (bf16[24,6144]{1,0:T(8,128)(2,1)S(1)}, bf16[24,6144]{1,0:T(8,128)(2,1)S(1)}, u32[]{:S(2)}, u32[]{:S(2)}) collective-permute-start(bf16[24,6144]{1,0:T(8,128)(2,1)S(1)} %get-tuple-element.80), channel_id=1, source_target_pairs={{0,16},{8,24},{16,0},{24,8},{1,17},{9,25},{17,1},{25,9},{2,18},{10... | collective-permute-start | bytes 884744 | tf_op jit(solution)/shard_map/ppermute | solution.py:526
  323.8 5.2 %collective-permute-done.9 = bf16[2,24,3200]{2,1,0:T(8,128)(2,1)S(1)} collective-permute-done((bf16[2,24,3200]{2,1,0:T(8,128)(2,1)S(1)}, bf16[2,24,3200]{2,1,0:T(8,128)(2,1)S(1)}, u32[]{:S(2)}, u32[]{:S(2)}) %collective-permute-start.9) | collective-permute-done | bytes 307232 | tf_op jit(solution)/shard_map/ppermute | solution.py:526
  330.2 11.3 %collective-permute-done.10 = bf16[1,24,3200]{2,1,0:T(8,128)(2,1)S(1)} collective-permute-done((bf16[1,24,3200]{2,1,0:T(8,128)(2,1)S(1)}, bf16[1,24,3200]{2,1,0:T(8,128)(2,1)S(1)}, u32[]{:S(2)}, u32[]{:S(2)}) %collective-permute-start.10) | collective-permute-done | bytes 153632 | tf_op jit(solution)/shard_map/ppermute | solution.py:526
  342.2 1.9 finish_attention.1
  346.1 2.0 finish_feed_forward.1
  (50 shorter events, 20.8 us)
Async XLA Ops:
  7.2 104.9 %all-gather.2.cloned.1.call-start = ((), (), s32[]{:S(2)}) async-start(), calls=%async_computation.1 | async-start | bytes 10948608 | tf_op jit(solution)/shard_map/all_gather | solution.py:687
  9.1 291.4 %reduce-scatter.2.cloned.1.call-start = ((), (), s32[]{:S(2)}) async-start(), calls=%async_computation.2 | async-start | bytes 10616832 | tf_op jit(solution)/shard_map/reduce_scatter | solution.py:703
  10.9 9.9 %collective-permute-start = (bf16[1,24,2432]{2,1,0:T(8,128)(2,1)}, bf16[1,24,2432]{2,1,0:T(8,128)(2,1)S(1)}, u32[]{:S(2)}, u32[]{:S(2)}) collective-permute-start(bf16[1,24,2432]{2,1,0:T(8,128)(2,1)} %bitcast.28), channel_id=1, source_target_pairs={{0,16},{8,24},{16,0},{24,8},{1,17},{9,25},{17,1},{25,9},{2,18},{10... | collective-permute-start | bytes 350216 | tf_op jit(solution)/shard_map/ppermute | solution.py:526
  21.7 11.2 %collective-permute-start.1 = (bf16[2,24,2432]{2,1,0:T(8,128)(2,1)S(1)}, bf16[2,24,2432]{2,1,0:T(8,128)(2,1)S(1)}, u32[]{:S(2)}, u32[]{:S(2)}) collective-permute-start(bf16[2,24,2432]{2,1,0:T(8,128)(2,1)S(1)} %pad_maximum_fusion.2), channel_id=1, source_target_pairs={{0,8},{8,0},{16,24},{24,16},{1,9},{9,1},{17,25},{25,17},{2,10},{10... | collective-permute-start | bytes 700424 | tf_op jit(solution)/shard_map/ppermute | solution.py:526
  22.6 10.3 %copy-start.3 = (bf16[24,2432]{1,0:T(8,128)(2,1)S(1)}, bf16[24,2432]{1,0:T(8,128)(2,1)}, u32[]{:S(2)}) copy-start(bf16[24,2432]{1,0:T(8,128)(2,1)} %pack_attention.1) | copy-start | bytes 350212
  32.9 8.6 %collective-permute-start.2 = (bf16[4,24,2432]{2,1,0:T(8,128)(2,1)S(1)}, bf16[4,24,2432]{2,1,0:T(8,128)(2,1)S(1)}, u32[]{:S(2)}, u32[]{:S(2)}) collective-permute-start(bf16[4,24,2432]{2,1,0:T(8,128)(2,1)S(1)} %pad_maximum_fusion.1), channel_id=1, source_target_pairs={{0,2},{1,5},{2,0},{3,7},{4,6},{5,1},{6,4},{7,3},{8,10},{9,13},{10,... | collective-permute-start | bytes 1400840 | tf_op jit(solution)/shard_map/ppermute | solution.py:526
  41.7 22.7 %copy-start.2 = (bf16[8,24,2432]{2,1,0:T(8,128)(2,1)}, bf16[8,24,2432]{2,1,0:T(8,128)(2,1)S(1)}, u32[]{:S(2)}) copy-start(bf16[8,24,2432]{2,1,0:T(8,128)(2,1)S(1)} %pad_maximum_fusion.a_ref) | copy-start | bytes 2801668
  41.7 18.4 %collective-permute-start.3 = (bf16[8,24,2432]{2,1,0:T(8,128)(2,1)S(1)}, bf16[8,24,2432]{2,1,0:T(8,128)(2,1)S(1)}, u32[]{:S(2)}, u32[]{:S(2)}) collective-permute-start(bf16[8,24,2432]{2,1,0:T(8,128)(2,1)S(1)} %pad_maximum_fusion.a_ref), channel_id=1, source_target_pairs={{0,4},{1,3},{2,6},{3,1},{4,0},{5,7},{6,2},{7,5},{8,12},{9,11},{10,... | collective-permute-start | bytes 2801672 | tf_op jit(solution)/shard_map/ppermute | solution.py:526
  43.2 19.5 %collective-permute-start.4 = (bf16[8,24,2432]{2,1,0:T(8,128)(2,1)S(1)}, bf16[8,24,2432]{2,1,0:T(8,128)(2,1)S(1)}, u32[]{:S(2)}, u32[]{:S(2)}) collective-permute-start(bf16[8,24,2432]{2,1,0:T(8,128)(2,1)S(1)} %pad_maximum_fusion.a_ref), channel_id=1, source_target_pairs={{0,1},{1,0},{2,3},{3,2},{4,5},{5,4},{6,7},{7,6},{8,9},{9,8},{10,11... | collective-permute-start | bytes 2801672 | tf_op jit(solution)/shard_map/ppermute | solution.py:526
  60.1 4.3 %copy-start.5 = (bf16[8,24,2432]{2,1,0:T(8,128)(2,1)}, bf16[8,24,2432]{2,1,0:T(8,128)(2,1)S(1)}, u32[]{:S(2)}) copy-start(bf16[8,24,2432]{2,1,0:T(8,128)(2,1)S(1)} %collective-permute-done.3.b_ref) | copy-start | bytes 2801668
  60.1 4.3 %collective-permute-start.5 = (bf16[8,24,2432]{2,1,0:T(8,128)(2,1)S(1)}, bf16[8,24,2432]{2,1,0:T(8,128)(2,1)}, u32[]{:S(2)}, u32[]{:S(2)}) collective-permute-start(bf16[8,24,2432]{2,1,0:T(8,128)(2,1)S(1)} %collective-permute-done.3.b_ref), channel_id=1, source_target_pairs={{0,1},{1,0},{2,3},{3,2},{4,5},{5,4},{6,7},{7,6},{8,9},{9,8},{10,11... | collective-permute-start | bytes 2801672 | tf_op jit(solution)/shard_map/ppermute | solution.py:526
  62.7 1.7 copy-start.6
  206.5 55.5 %copy-start = (bf16[768,768]{1,0:T(8,128)(2,1)S(1)}, bf16[768,768]{1,0:T(8,128)(2,1)}, u32[]{:S(2)}) copy-start(bf16[768,768]{1,0:T(8,128)(2,1)} %get-tuple-element.48.wo_ref) | copy-start | bytes 3538948
  262.0 0.8 copy-start.1
  275.7 4.7 %collective-permute-start.6 = (bf16[16,24,3200]{2,1,0:T(8,128)(2,1)S(1)}, bf16[16,24,3200]{2,1,0:T(8,128)(2,1)S(1)}, u32[]{:S(2)}, u32[]{:S(2)}) collective-permute-start(bf16[16,24,3200]{2,1,0:T(8,128)(2,1)S(1)} %get-tuple-element.51), channel_id=1, source_target_pairs={{0,1},{1,0},{2,3},{3,2},{4,5},{5,4},{6,7},{7,6},{8,9},{9,8},{10,11... | collective-permute-start | bytes 7372808 | tf_op jit(solution)/shard_map/ppermute | solution.py:526
  281.0 17.6 %collective-permute-start.7 = (bf16[8,24,3200]{2,1,0:T(8,128)(2,1)S(1)}, bf16[8,24,3200]{2,1,0:T(8,128)(2,1)S(1)}, u32[]{:S(2)}, u32[]{:S(2)}) collective-permute-start(bf16[8,24,3200]{2,1,0:T(8,128)(2,1)S(1)} %get-tuple-element.77), channel_id=1, source_target_pairs={{0,2},{1,5},{2,0},{3,7},{4,6},{5,1},{6,4},{7,3},{8,10},{9,13},{10,... | collective-permute-start | bytes 3686408 | tf_op jit(solution)/shard_map/ppermute | solution.py:526
  298.9 10.2 %collective-permute-start.8 = (bf16[4,24,3200]{2,1,0:T(8,128)(2,1)S(1)}, bf16[4,24,3200]{2,1,0:T(8,128)(2,1)S(1)}, u32[]{:S(2)}, u32[]{:S(2)}) collective-permute-start(bf16[4,24,3200]{2,1,0:T(8,128)(2,1)S(1)} %get-tuple-element.79), channel_id=1, source_target_pairs={{0,4},{1,3},{2,6},{3,1},{4,0},{5,7},{6,2},{7,5},{8,12},{9,11},{10,... | collective-permute-start | bytes 1843208 | tf_op jit(solution)/shard_map/ppermute | solution.py:526
  300.5 17.7 %copy-start.4 = (bf16[96,6144]{1,0:T(8,128)(2,1)S(1)}, bf16[96,6144]{1,0:T(8,128)(2,1)}, u32[]{:S(2)}) copy-start(bf16[96,6144]{1,0:T(8,128)(2,1)} %reduce-scatter.2.cloned.1.call-done) | copy-start | bytes 3538948
  301.7 16.5 %collective-permute-start.11 = (bf16[2,24,6144]{2,1,0:T(8,128)(2,1)S(1)}, bf16[2,24,6144]{2,1,0:T(8,128)(2,1)S(1)}, u32[]{:S(2)}, u32[]{:S(2)}) collective-permute-start(bf16[2,24,6144]{2,1,0:T(8,128)(2,1)S(1)} %bitcast.32), channel_id=1, source_target_pairs={{0,8},{8,0},{16,24},{24,16},{1,9},{9,1},{17,25},{25,17},{2,10},{10... | collective-permute-start | bytes 1769480 | tf_op jit(solution)/shard_map/ppermute | solution.py:526
  309.3 19.7 %collective-permute-start.9 = (bf16[2,24,3200]{2,1,0:T(8,128)(2,1)S(1)}, bf16[2,24,3200]{2,1,0:T(8,128)(2,1)S(1)}, u32[]{:S(2)}, u32[]{:S(2)}) collective-permute-start(bf16[2,24,3200]{2,1,0:T(8,128)(2,1)S(1)} %get-tuple-element.83), channel_id=1, source_target_pairs={{0,8},{8,0},{16,24},{24,16},{1,9},{9,1},{17,25},{25,17},{2,10},{10... | collective-permute-start | bytes 921608 | tf_op jit(solution)/shard_map/ppermute | solution.py:526
  319.0 26.5 %collective-permute-start.12 = (bf16[24,6144]{1,0:T(8,128)(2,1)S(1)}, bf16[24,6144]{1,0:T(8,128)(2,1)S(1)}, u32[]{:S(2)}, u32[]{:S(2)}) collective-permute-start(bf16[24,6144]{1,0:T(8,128)(2,1)S(1)} %get-tuple-element.80), channel_id=1, source_target_pairs={{0,16},{8,24},{16,0},{24,8},{1,17},{9,25},{17,1},{25,9},{2,18},{10... | collective-permute-start | bytes 884744 | tf_op jit(solution)/shard_map/ppermute | solution.py:526
  329.7 11.8 %collective-permute-start.10 = (bf16[1,24,3200]{2,1,0:T(8,128)(2,1)S(1)}, bf16[1,24,3200]{2,1,0:T(8,128)(2,1)S(1)}, u32[]{:S(2)}, u32[]{:S(2)}) collective-permute-start(bf16[1,24,3200]{2,1,0:T(8,128)(2,1)S(1)} %get-tuple-element.84), channel_id=1, source_target_pairs={{0,16},{8,24},{16,0},{24,8},{1,17},{9,25},{17,1},{25,9},{2,18},{10... | collective-permute-start | bytes 460808 | tf_op jit(solution)/shard_map/ppermute | solution.py:526
  341.5 0.7 copy-start.8
  345.4 0.7 copy-start.7
Sparse Core Ops, SparseCore 0:
  10.9 97.9 all-gather.1
  206.6 81.2 reduce-scatter.1

commit v4 on v3

--- a/solution.py
+++ b/solution.py
@@ -421,7 +421,7 @@
 
 def block_kernel(at_ref,x_ref,oT_ref,dy_ref,ga_ref,wo_ref,win_ref,wout_ref,
                  out_ref,dm_ref,doT_ref,dwo_ref,*rest,FC,SUB,nc,nt,legs):
-    dw_ref,b_s,bT_s,dyT,oacc,dacc,ain,aout,awo=rest
+    dw_ref,b_s,bT_s,oacc,dacc,ain,aout,awo,m_s=rest
     c=pl.program_id(0); t=pl.program_id(1)
     rows=pl.ds(t*BLOCK,BLOCK)
     def middle():
@@ -432,10 +432,11 @@
         b=(m*rms(m)*row_of(ga_ref[...],1)).astype(BF16)
         b_s[t]=b
         bT_s[t]=b.T
-        dyT[t]=dy_ref[rows,:].T
         oacc[rows,:]=m
+        m_s[rows,:]=m
         dacc[rows,:]=jnp.zeros((BLOCK,D),F32)
-    b=b_s[t]; dy=dy_ref[rows,:]
+    b=b_s[t]; dy=dy_ref[...]
+    dyt=dy.T
     G=[];DU=[]
     n=FC//SUB
     U=[dot(b,win_ref[:,s*SUB:(s+1)*SUB]) for s in range(n)]
@@ -448,7 +449,7 @@
         g=g.astype(BF16)
         du=(DG[s]*pull).astype(BF16)
         sl=slice(s*SUB,(s+1)*SUB)
-        aout[:,sl]+=dot(dyT[t],g)
+        aout[:,sl]+=dot(dyt,g)
         ain[:,sl]+=dot(bT_s[t],du)
         G.append(g);DU.append(du)
     g=jnp.concatenate(G,1);du=jnp.concatenate(DU,1)
@@ -471,7 +472,7 @@
     @pl.when(c==nc-1)
     def _():
         out_ref[...]=oacc[rows,:].astype(BF16)
-        m=middle()
+        m=m_s[rows,:]
         db=dacc[rows,:]
         r=rms(m); n2=m*r
         dn=db*row_of(ga_ref[...],1)
@@ -485,19 +486,20 @@
 def block_call(x,oT,dy,gains,wo,win,wout,core,legs,FC=768,SUB=256):
     T=x.shape[0]; nt=T//BLOCK; FF=3072; nc=FF//FC
     last=lambda c,t:jnp.where(c==nc-1,t,0)
+    first=lambda c,t:jnp.where(c==0,t,nt-1)
     ends=lambda c,t:jnp.where((c==0)|(c==nc-1),t,nt-1)
     one=pl.Buffered(1)
     sd=jax.ShapeDtypeStruct; BS=pl.BlockSpec; R=D//32
     return pl.pallas_call(functools.partial(block_kernel,FC=FC,SUB=SUB,nc=nc,nt=nt,legs=legs),
         grid_spec=pltpu.PrefetchScalarGridSpec(num_scalar_prefetch=1,grid=(nc,nt),
-        in_specs=[BS((BLOCK,D),lambda c,t,at:(ends(c,t),0)),BS((D,BLOCK),lambda c,t,at:(0,ends(c,t))),
-            BS((T,D),lambda c,t,at:(0,0),pipeline_mode=one),
+        in_specs=[BS((BLOCK,D),lambda c,t,at:(first(c,t),0)),BS((D,BLOCK),lambda c,t,at:(0,ends(c,t))),
+            BS((BLOCK,D),lambda c,t,at:(t,0)),
             BS((D,GA),lambda c,t,at:(0,gains[1]),pipeline_mode=one),BS((D,D),lambda c,t,at:(0,wo[1]),pipeline_mode=one),
             BS((D,FC),lambda c,t,at:(0,c+win[1]*D//FC)),BS((D,FC),lambda c,t,at:(0,c+wout[1]*D//FC))],
         out_specs=[BS((BLOCK,D),lambda c,t,at:(last(c,t),0)),BS((BLOCK,D),lambda c,t,at:(last(c,t),0)),BS((D,BLOCK),lambda c,t,at:(0,last(c,t))),
-            BS((D,D),lambda c,t,at:(0,0))]+([BS((32,R,2*FC),lambda c,t,at:(0,0,c))] if legs else [BS((D,2*FC),lambda c,t,at:(0,c))]),
-        scratch_shapes=[pltpu.VMEM((nt,BLOCK,D),BF16),pltpu.VMEM((nt,D,BLOCK),BF16),pltpu.VMEM((nt,D,BLOCK),BF16),
-            pltpu.VMEM((T,D),F32),pltpu.VMEM((T,D),F32),pltpu.VMEM((D,FC),F32),pltpu.VMEM((D,FC),F32),pltpu.VMEM((D,D),F32)]),
+            BS((D,D),lambda c,t,at:(0,0),pipeline_mode=one)]+([BS((32,R,2*FC),lambda c,t,at:(0,0,c))] if legs else [BS((D,2*FC),lambda c,t,at:(0,c))]),
+        scratch_shapes=[pltpu.VMEM((nt,BLOCK,D),BF16),pltpu.VMEM((nt,D,BLOCK),BF16),
+            pltpu.VMEM((T,D),F32),pltpu.VMEM((T,D),F32),pltpu.VMEM((D,FC),F32),pltpu.VMEM((D,FC),F32),pltpu.VMEM((D,D),F32),pltpu.VMEM((T,D),F32)]),
         out_shape=[sd((T,D),BF16),sd((T,D),F32),sd((D,T),BF16),sd((D,D),BF16)]+([sd((32,R,2*FF),BF16)] if legs else [sd((D,2*FF),BF16)]),
         name="feed_forward",
         compiler_params=pltpu.CompilerParams(vmem_limit_bytes=62*2**20+2**19))(core,x,oT,dy,gains[0],wo[0],win[0],wout[0])
@@ -628,14 +630,17 @@
         out_specs=[out,out],scratch_shapes=[pltpu.VMEM((D,D),F32)]),
         out_shape=[jax.ShapeDtypeStruct((16,R,GN),BF16)]*2,name="weight_grads",
         compiler_params=pltpu.CompilerParams(vmem_limit_bytes=48*2**20))(at,aT,gT,dwoT,tab)
-def scatter_sum(keep,send,beside):
+def scatter_sum(keep,send,beside,other,rest):
     r=swap(send,INNER,1)
     for half,axis,leg in ((8,INNER,first_leg),(4,INNER,second_leg),(2,"dp",1),(1,"dp",2)):
         out=add(keep[half:],r[half:])
         keep=add(keep[:half],r[:half])
         r=swap(out,axis,leg)
-        if half==8: r,beside=lax.optimization_barrier((r,beside))
-    return keep[0],r[0],beside
+        if half==8:
+            r,beside,other=lax.optimization_barrier((r,beside,other))
+            late=rest(other)
+    r,late=lax.optimization_barrier((r,late))
+    return keep[0],r[0],beside,late
 def finish_kernel(a_ref,b_ref,wq_ref,wk_ref,wv_ref,g_ref,q_ref,k_ref,v_ref,o_ref,tab_ref,dg_ref):
     R=a_ref.shape[0]
     tot=None
@@ -647,14 +652,13 @@
             y=jnp.sum(s*w[...].astype(BF16).astype(F32),axis=1,keepdims=True)
             tot=y if tot is None else tot+y
     t=a_ref[:,4*D:4*D+128].astype(F32)+b_ref[:,4*D:4*D+128].astype(F32)
-    t=jnp.concatenate([t,jnp.zeros((128-R,128),F32)],0).T
-    tab_ref[...]=t[:BUCKETS,:HEADS]
+    tab_ref[...]=t[:HEADS,:BUCKETS]
     rowv=jnp.broadcast_to(tot,(R,128))
     rowv=jnp.concatenate([rowv,jnp.zeros((128-R,128),F32)],0).T[:1,:R]
     dg_ref[...]=rowv/g_ref[...].astype(BF16).astype(F32)
 def finish_call(a,b,wq,wk,wv,g1):
     R=a.shape[0]; sd=jax.ShapeDtypeStruct
-    return pl.pallas_call(finish_kernel,out_shape=[sd((R,D),F32)]*4+[sd((BUCKETS,HEADS),F32),sd((1,R),F32)],name="finish_attention")(a,b,wq,wk,wv,g1[None])
+    return pl.pallas_call(finish_kernel,out_shape=[sd((R,D),F32)]*4+[sd((HEADS,BUCKETS),F32),sd((1,R),F32)],name="finish_attention")(a,b,wq,wk,wv,g1[None])
 def finish_ffn_kernel(s_ref,t_ref,w_ref,g_ref,i_ref,o_ref,dg_ref,*,FC):
     R=s_ref.shape[0]
     tot=None
@@ -696,7 +700,7 @@
         wa=lax.all_gather(pa,BOTH,axis=0,tiled=True)
         wb=lax.all_gather(pb,BOTH,axis=0,tiled=True)
         aT,qkvT=qkv_call(hidden,wa)
-    oT,lse=fwd2_call(long_flags,qkvT,bias,HP=4,mode="norm")
+    oT,lse=fwd2_call(long_flags,qkvT,bias,HP=4,mode="ones")
     GB=3*D//GA
     z=(lax.axis_index("dp") if legs else jnp.zeros((),jnp.int32)).reshape(1)
     out,dm,doT,dwoT,dffn=block_call(hidden,oT,out_grad,(wa,GB),(wb,0),(wb,1),(wb,5),z,legs,FC=FC)
@@ -705,13 +709,15 @@
     gT,tab=bwd2_call(long_flags,qkvT,doT,lse,bias,HP=4)
     if legs:
         keep,send=grads_call(slot_table(),aT,gT,dwoT,tab)
-        a,b2,dx=scatter_sum(keep,send,last_call(hidden,dm,gT,wa))
         h=fsum.reshape(4,rows,2*FF)
+        h,dm=lax.optimization_barrier((h,dm))
         r=swap(h[2:],"dp",1)
-        fa,fb=add(h[0],r[0]),swap(add(h[1],r[1]),"dp",2)
+        def rest(r):
+            fa,fb=add(h[0],r[0]),swap(add(h[1],r[1]),"dp",2)
+            return finish_ffn_call(fa,fb,ffn_in,norm2_gain,FC)
+        a,b2,dx,(di,du,dg2)=scatter_sum(keep,send,last_call(hidden,dm,gT,wa),r,rest)
         dq,dk,dv,do,table,dg1=finish_call(a,b2,query_w,key_w,value_w,norm1_gain)
-        di,du,dg2=finish_ffn_call(fa,fb,ffn_in,norm2_gain,FC)
-        dg1=dg1[0]; dg2=dg2[0]
+        dg1=dg1[0]; dg2=dg2[0]; table=table.T
     else:
         dx=last_call(hidden,dm,gT,wa)
         tabs=tab[:,0,:BUCKETS].reshape(-1)

time: 355 us -> 343 us (0.966)
  Pallas kernels: 242 us -> 235 us
  starting transfers between devices: 22.8 us -> 17.2 us
    ppermute x13, starting transfers between devices: 22.7 us -> 17.1 us  [swap(): return lax.ppermute(x, axis, [(i, i ^ f(i)) for i in range(n)])]
    reduce_scatter x1, waiting for transfers between devices: 0.01 us -> 5.03 us  [rs(): return lax.psum_scatter(x, axes, scatter_dimension=0, tiled=True)]
    ppermute x13, waiting for transfers between devices: 66.7 us -> 62 us  [swap(): return lax.ppermute(x, axis, [(i, i ^ f(i)) for i in range(n)])]
    pallas_call x1, Pallas kernels: 94.4 us -> 90.2 us  [block_call(): pl.pallas_call(functools.partial(block_kernel, FC=FC, SUB=SUB, nc=nc, nt=...]
  transfers between devices with their start and end apart: 15 -> 15, of which waited for: 11 -> 11; matrix products, arithmetic and copies ran while one was open for 2% -> 1% of each run, Pallas kernels for 41% -> 41%
where the time goes in v4:
time: 343 us; the launch traced here: 342 us
  Pallas kernels  235 us (69%)
  waiting for transfers between devices  67 us (20%)
  starting transfers between devices  17.2 us (5%)
  between operations  14.2 us (4%)
  other arithmetic  5.65 us (2%)
    pallas_call x1, Pallas kernels, block_call(): pl.pallas_call(functools.partial(block_kernel, FC=FC, SUB=SUB, nc=nc, nt=...  90.2 us
    ppermute x13, waiting for transfers between devices, swap(): return lax.ppermute(x, axis, [(i, i ^ f(i)) for i in range(n)])  62 us
    pallas_call x1, Pallas kernels, bwd2_call(): pl.pallas_call(functools.partial(bwd2_kernel, HP=HP, nb=n, tabmode=tabmod...  55.5 us
    pallas_call x1, Pallas kernels, fwd2_call(): pl.pallas_call(functools.partial(fwd2_kernel, HP=HP, mode=mode), grid_spe...  29.7 us
    ppermute x13, starting transfers between devices, swap(): return lax.ppermute(x, axis, [(i, i ^ f(i)) for i in range(n)])  17.1 us
    pallas_call x1, Pallas kernels, last_call(): pl.pallas_call(last_kernel, grid=(nt,), in_specs=[row, row, pl.BlockSpec(...  15.7 us
    pallas_call x1, Pallas kernels, project2_call(): pl.pallas_call(project2_kernel, grid_spec=pltpu.PrefetchScalarGridSpec(nu...  15.1 us
    pallas_call x1, Pallas kernels, grads_call(): pl.pallas_call(grads_kernel, grid_spec=pltpu.PrefetchScalarGridSpec(num_s...  12.9 us
  transfers between devices with their start and end apart: 15, of which 11 were waited for; matrix products, arithmetic and copies ran while one was open for 1% of the time, Pallas kernels for 41%

profile of v4, /device:TPU:0, one launch (start us, length us, event | category | flops | bytes accessed | tf_op | source)
XLA Modules:
  0.0 342.4 jit_solution(8046663654783513288)
XLA Ops:
  7.2 1.9 pack_feed_forward.1
  9.2 1.7 pack_attention.1
  10.9 4.0 %collective-permute-start = (bf16[1,24,2432]{2,1,0:T(8,128)(2,1)}, bf16[1,24,2432]{2,1,0:T(8,128)(2,1)S(1)}, u32[]{:S(2)}, u32[]{:S(2)}) collective-permute-start(bf16[1,24,2432]{2,1,0:T(8,128)(2,1)} %bitcast.23), channel_id=1, source_target_pairs={{0,16},{8,24},{16,0},{24,8},{1,17},{9,25},{17,1},{25,9},{2,18},{10... | collective-permute-start | bytes 350216 | tf_op jit(solution)/shard_map/ppermute | solution.py:528
  14.9 5.9 %collective-permute-done = bf16[1,24,2432]{2,1,0:T(8,128)(2,1)S(1)} collective-permute-done((bf16[1,24,2432]{2,1,0:T(8,128)(2,1)}, bf16[1,24,2432]{2,1,0:T(8,128)(2,1)S(1)}, u32[]{:S(2)}, u32[]{:S(2)}) %collective-permute-start) | collective-permute-done | bytes 116768 | tf_op jit(solution)/shard_map/ppermute | solution.py:528
  22.6 8.6 %bias.1.bias_ref = f32[12,512,512]{2,1,0:T(8,128)} custom-call(f32[12,32]{1,0:T(8,128)} %bitcast.32), custom_call_target="tpu_custom_call" | custom-call | tf_op jit(solution)/shard_map/bias/pallas_call | solution.py:49
  31.2 1.7 collective-permute-done.1
  34.4 7.2 %collective-permute-done.2 = bf16[4,24,2432]{2,1,0:T(8,128)(2,1)S(1)} collective-permute-done((bf16[4,24,2432]{2,1,0:T(8,128)(2,1)S(1)}, bf16[4,24,2432]{2,1,0:T(8,128)(2,1)S(1)}, u32[]{:S(2)}, u32[]{:S(2)}) %collective-permute-start.2) | collective-permute-done | bytes 466976 | tf_op jit(solution)/shard_map/ppermute | solution.py:528
  43.2 16.9 %collective-permute-done.3.b_ref = bf16[8,24,2432]{2,1,0:T(8,128)(2,1)S(1)} collective-permute-done((bf16[8,24,2432]{2,1,0:T(8,128)(2,1)S(1)}, bf16[8,24,2432]{2,1,0:T(8,128)(2,1)S(1)}, u32[]{:S(2)}, u32[]{:S(2)}) %collective-permute-start.3) | collective-permute-done | bytes 933920 | tf_op jit(solution)/shard_map/ppermute | solution.py:528
  60.1 2.0 collective-permute-start.5
  64.4 15.1 %project.1 = (bf16[768,2048]{1,0:T(8,128)(2,1)}, bf16[2304,2048]{1,0:T(8,128)(2,1)}, bf16[768,2432]{1,0:T(8,128)(2,1)}) custom-call(s32[2]{0:T(128)} %pad_add_fusion.1.at_ref, bf16[2048,768]{1,0:T(8,128)(2,1)} %x_ref.5, bf16[8,24,2432]{2,1,0:T(8,128)(2,1)} %copy-done.2, bf16[8,24,2432]{2,1,0:T(8,128)(2,1)} %copy-done.5, bf16[8,24,2432]{2,1,0:T(8,128)(2,1)} %copy-done.6, ...), custom_call_target="tpu_custom_call" | custom-call | tf_op jit(solution)/shard_map/project/pallas_call | solution.py:582
  79.5 29.7 %attend.1 = (bf16[768,2048]{1,0:T(8,128)(2,1)}, f32[12,1,2048]{2,1,0:T(1,128)}) custom-call(s32[4]{0:T(128)} %flags_ref.3, bf16[2304,2048]{1,0:T(8,128)(2,1)} %get-tuple-element.46.q_ref.k_ref.v_ref, bf16[2304,2048]{1,0:T(8,128)(2,1)} %get-tuple-element.46.q_ref.k_ref.v_ref, bf16[2304,2048]{1,0:T(8,128)(2,1)} %get-tuple-element.46.q_ref.k_ref.v_ref, ...), custom_call_target="tpu_custom_call" | custom-call | tf_op jit(solution)/shard_map/attend/pallas_call | solution.py:180
  109.2 90.2 %feed_forward.1 = (bf16[2048,768]{1,0:T(8,128)(2,1)}, f32[2048,768]{1,0:T(8,128)}, bf16[768,2048]{1,0:T(8,128)(2,1)}, bf16[768,768]{1,0:T(8,128)(2,1)}, bf16[32,24,6144]{2,1,0:T(8,128)(2,1)}) custom-call(s32[1]{0:T(128)} %bitcast.at_ref, bf16[2048,768]{1,0:T(8,128)(2,1)} %x_ref.5, bf16[768,2048]{1,0:T(8,128)(2,1)} %get-tuple-element.48.oT_ref, ...), custom_call_target="tpu_custom_call" | custom-call | tf_op jit(solution)/shard_map/feed_forward/pallas_call | solution.py:493
  199.5 55.5 %attend_back.1 = (bf16[3,768,2048]{2,1,0:T(8,128)(2,1)}, f32[12,8,128]{2,1,0:T(8,128)}) custom-call(s32[4]{0:T(128)} %flags_ref.3, bf16[2304,2048]{1,0:T(8,128)(2,1)} %get-tuple-element.46.q_ref.k_ref.v_ref, bf16[2304,2048]{1,0:T(8,128)(2,1)} %get-tuple-element.46.q_ref.k_ref.v_ref, bf16[2304,2048]{1,0:T(8,128)(2,1)} %get-tuple-element.46.q_ref.k_ref.v_ref, ...), custom_call_target="tpu_custom_call" | custom-call | tf_op jit(solution)/shard_map/attend_back/pallas_call | solution.py:268
  255.8 12.9 %weight_grads.1 = (bf16[16,24,3200]{2,1,0:T(8,128)(2,1)S(1)}, bf16[16,24,3200]{2,1,0:T(8,128)(2,1)S(1)}) custom-call(s32[2,16]{1,0:T(2,128)S(1)} %pad_add_fusion.at_ref, bf16[768,2048]{1,0:T(8,128)(2,1)} %get-tuple-element.51.aT_ref, bf16[3,768,2048]{2,1,0:T(8,128)(2,1)} %get-tuple-element.54.g_ref, bf16[768,768]{1,0:T(8,128)(2,1)S(1)} %copy-done, ...), custom_call_target="tpu_custom_call" | custom-call | tf_op jit(solution)/shard_map/weight_grads/pallas_call | solution.py:624
  269.2 4.3 %collective-permute-done.6 = bf16[16,24,3200]{2,1,0:T(8,128)(2,1)S(1)} collective-permute-done((bf16[16,24,3200]{2,1,0:T(8,128)(2,1)S(1)}, bf16[16,24,3200]{2,1,0:T(8,128)(2,1)S(1)}, u32[]{:S(2)}, u32[]{:S(2)}) %collective-permute-start.6) | collective-permute-done | bytes 2457632 | tf_op jit(solution)/shard_map/ppermute | solution.py:528
  275.2 5.0 %reduce-scatter.2.cloned.1.call-done = bf16[96,6144]{1,0:T(8,128)(2,1)} async-done(((bf16[768,6144]{1,0:T(8,128)(2,1)}), bf16[96,6144]{1,0:T(8,128)(2,1)}) %reduce-scatter.2.cloned.1.call-update) | async-done | bytes 1179664 | tf_op jit(solution)/shard_map/reduce_scatter | solution.py:707
  282.4 15.7 %project_back.1 = bf16[2048,768]{1,0:T(8,128)(2,1)} custom-call(bf16[2048,768]{1,0:T(8,128)(2,1)} %x_ref.5, f32[2048,768]{1,0:T(8,128)} %get-tuple-element.61.dm_ref, bf16[3,768,2048]{2,1,0:T(8,128)(2,1)} %get-tuple-element.54.g_ref, bf16[768,2432]{1,0:T(8,128)(2,1)} %get-tuple-element.49.ga_ref.w_ref), custom_call_target="tpu_custom_call" | custom-call | flops 7247757312 | bytes 31457280 | tf_op jit(solution)/shard_map/project_back/pallas_call | solution.py:416
  301.2 8.8 %collective-permute-done.9 = bf16[4,24,3200]{2,1,0:T(8,128)(2,1)S(1)} collective-permute-done((bf16[4,24,3200]{2,1,0:T(8,128)(2,1)S(1)}, bf16[4,24,3200]{2,1,0:T(8,128)(2,1)S(1)}, u32[]{:S(2)}, u32[]{:S(2)}) %collective-permute-start.9) | collective-permute-done | bytes 614432 | tf_op jit(solution)/shard_map/ppermute | solution.py:528
  312.1 1.9 collective-permute-start.12
  314.0 10.2 %collective-permute-done.10 = bf16[2,24,3200]{2,1,0:T(8,128)(2,1)S(1)} collective-permute-done((bf16[2,24,3200]{2,1,0:T(8,128)(2,1)S(1)}, bf16[2,24,3200]{2,1,0:T(8,128)(2,1)S(1)}, u32[]{:S(2)}, u32[]{:S(2)}) %collective-permute-start.10) | collective-permute-done | bytes 307232 | tf_op jit(solution)/shard_map/ppermute | solution.py:528
  325.0 3.2 collective-permute-done.12.t_ref
  328.9 2.0 finish_feed_forward.1
  330.9 2.1 collective-permute-done.11
  333.7 1.9 finish_attention.1
  (49 shorter events, 19.8 us)
Async XLA Ops:
  7.2 102.0 %all-gather.2.cloned.1.call-start = ((), (), s32[]{:S(2)}) async-start(), calls=%async_computation.1 | async-start | bytes 10948608 | tf_op jit(solution)/shard_map/all_gather | solution.py:691
  9.1 271.2 %reduce-scatter.2.cloned.1.call-start = ((), (), s32[]{:S(2)}) async-start(), calls=%async_computation.2 | async-start | bytes 10616832 | tf_op jit(solution)/shard_map/reduce_scatter | solution.py:707
  10.9 9.9 %collective-permute-start = (bf16[1,24,2432]{2,1,0:T(8,128)(2,1)}, bf16[1,24,2432]{2,1,0:T(8,128)(2,1)S(1)}, u32[]{:S(2)}, u32[]{:S(2)}) collective-permute-start(bf16[1,24,2432]{2,1,0:T(8,128)(2,1)} %bitcast.23), channel_id=1, source_target_pairs={{0,16},{8,24},{16,0},{24,8},{1,17},{9,25},{17,1},{25,9},{2,18},{10... | collective-permute-start | bytes 350216 | tf_op jit(solution)/shard_map/ppermute | solution.py:528
  21.7 11.2 %collective-permute-start.1 = (bf16[2,24,2432]{2,1,0:T(8,128)(2,1)S(1)}, bf16[2,24,2432]{2,1,0:T(8,128)(2,1)S(1)}, u32[]{:S(2)}, u32[]{:S(2)}) collective-permute-start(bf16[2,24,2432]{2,1,0:T(8,128)(2,1)S(1)} %pad_maximum_fusion.2), channel_id=1, source_target_pairs={{0,8},{8,0},{16,24},{24,16},{1,9},{9,1},{17,25},{25,17},{2,10},{10... | collective-permute-start | bytes 700424 | tf_op jit(solution)/shard_map/ppermute | solution.py:528
  22.6 10.3 %copy-start.3 = (bf16[24,2432]{1,0:T(8,128)(2,1)S(1)}, bf16[24,2432]{1,0:T(8,128)(2,1)}, u32[]{:S(2)}) copy-start(bf16[24,2432]{1,0:T(8,128)(2,1)} %pack_attention.1) | copy-start | bytes 350212
  32.9 8.6 %collective-permute-start.2 = (bf16[4,24,2432]{2,1,0:T(8,128)(2,1)S(1)}, bf16[4,24,2432]{2,1,0:T(8,128)(2,1)S(1)}, u32[]{:S(2)}, u32[]{:S(2)}) collective-permute-start(bf16[4,24,2432]{2,1,0:T(8,128)(2,1)S(1)} %pad_maximum_fusion.1), channel_id=1, source_target_pairs={{0,2},{1,5},{2,0},{3,7},{4,6},{5,1},{6,4},{7,3},{8,10},{9,13},{10,... | collective-permute-start | bytes 1400840 | tf_op jit(solution)/shard_map/ppermute | solution.py:528
  41.7 22.7 %copy-start.2 = (bf16[8,24,2432]{2,1,0:T(8,128)(2,1)}, bf16[8,24,2432]{2,1,0:T(8,128)(2,1)S(1)}, u32[]{:S(2)}) copy-start(bf16[8,24,2432]{2,1,0:T(8,128)(2,1)S(1)} %pad_maximum_fusion.a_ref) | copy-start | bytes 2801668
  41.7 18.4 %collective-permute-start.3 = (bf16[8,24,2432]{2,1,0:T(8,128)(2,1)S(1)}, bf16[8,24,2432]{2,1,0:T(8,128)(2,1)S(1)}, u32[]{:S(2)}, u32[]{:S(2)}) collective-permute-start(bf16[8,24,2432]{2,1,0:T(8,128)(2,1)S(1)} %pad_maximum_fusion.a_ref), channel_id=1, source_target_pairs={{0,4},{1,3},{2,6},{3,1},{4,0},{5,7},{6,2},{7,5},{8,12},{9,11},{10,... | collective-permute-start | bytes 2801672 | tf_op jit(solution)/shard_map/ppermute | solution.py:528
  43.2 19.5 %collective-permute-start.4 = (bf16[8,24,2432]{2,1,0:T(8,128)(2,1)S(1)}, bf16[8,24,2432]{2,1,0:T(8,128)(2,1)S(1)}, u32[]{:S(2)}, u32[]{:S(2)}) collective-permute-start(bf16[8,24,2432]{2,1,0:T(8,128)(2,1)S(1)} %pad_maximum_fusion.a_ref), channel_id=1, source_target_pairs={{0,1},{1,0},{2,3},{3,2},{4,5},{5,4},{6,7},{7,6},{8,9},{9,8},{10,11... | collective-permute-start | bytes 2801672 | tf_op jit(solution)/shard_map/ppermute | solution.py:528
  60.1 4.3 %copy-start.5 = (bf16[8,24,2432]{2,1,0:T(8,128)(2,1)}, bf16[8,24,2432]{2,1,0:T(8,128)(2,1)S(1)}, u32[]{:S(2)}) copy-start(bf16[8,24,2432]{2,1,0:T(8,128)(2,1)S(1)} %collective-permute-done.3.b_ref) | copy-start | bytes 2801668
  60.1 4.3 %collective-permute-start.5 = (bf16[8,24,2432]{2,1,0:T(8,128)(2,1)S(1)}, bf16[8,24,2432]{2,1,0:T(8,128)(2,1)}, u32[]{:S(2)}, u32[]{:S(2)}) collective-permute-start(bf16[8,24,2432]{2,1,0:T(8,128)(2,1)S(1)} %collective-permute-done.3.b_ref), channel_id=1, source_target_pairs={{0,1},{1,0},{2,3},{3,2},{4,5},{5,4},{6,7},{7,6},{8,9},{9,8},{10,11... | collective-permute-start | bytes 2801672 | tf_op jit(solution)/shard_map/ppermute | solution.py:528
  62.7 1.7 copy-start.6
  199.5 55.6 %copy-start = (bf16[768,768]{1,0:T(8,128)(2,1)S(1)}, bf16[768,768]{1,0:T(8,128)(2,1)}, u32[]{:S(2)}) copy-start(bf16[768,768]{1,0:T(8,128)(2,1)} %get-tuple-element.55.wo_ref) | copy-start | bytes 3538948
  255.0 0.8 copy-start.1
  268.7 4.8 %collective-permute-start.6 = (bf16[16,24,3200]{2,1,0:T(8,128)(2,1)S(1)}, bf16[16,24,3200]{2,1,0:T(8,128)(2,1)S(1)}, u32[]{:S(2)}, u32[]{:S(2)}) collective-permute-start(bf16[16,24,3200]{2,1,0:T(8,128)(2,1)S(1)} %get-tuple-element.58), channel_id=1, source_target_pairs={{0,1},{1,0},{2,3},{3,2},{4,5},{5,4},{6,7},{7,6},{8,9},{9,8},{10,11... | collective-permute-start | bytes 7372808 | tf_op jit(solution)/shard_map/ppermute | solution.py:528
  274.1 24.1 %collective-permute-start.7 = (bf16[8,24,3200]{2,1,0:T(8,128)(2,1)S(1)}, bf16[8,24,3200]{2,1,0:T(8,128)(2,1)}, u32[]{:S(2)}, u32[]{:S(2)}) collective-permute-start(bf16[8,24,3200]{2,1,0:T(8,128)(2,1)S(1)} %get-tuple-element.80), channel_id=1, source_target_pairs={{0,2},{1,5},{2,0},{3,7},{4,6},{5,1},{6,4},{7,3},{8,10},{9,13},{10,... | collective-permute-start | bytes 3686408 | tf_op jit(solution)/shard_map/ppermute | solution.py:528
  281.4 16.8 %collective-permute-start.8 = (bf16[2,24,6144]{2,1,0:T(8,128)(2,1)S(1)}, bf16[2,24,6144]{2,1,0:T(8,128)(2,1)S(1)}, u32[]{:S(2)}, u32[]{:S(2)}) collective-permute-start(bf16[2,24,6144]{2,1,0:T(8,128)(2,1)S(1)} %slice.65), channel_id=1, source_target_pairs={{0,8},{8,0},{16,24},{24,16},{1,9},{9,1},{17,25},{25,17},{2,10},{10... | collective-permute-start | bytes 1769480 | tf_op jit(solution)/shard_map/ppermute | solution.py:528
  298.1 13.1 %copy-start.4 = (bf16[96,6144]{1,0:T(8,128)(2,1)S(1)}, bf16[96,6144]{1,0:T(8,128)(2,1)}, u32[]{:S(2)}) copy-start(bf16[96,6144]{1,0:T(8,128)(2,1)} %reduce-scatter.2.cloned.1.call-done) | copy-start | bytes 3538948
  299.8 10.2 %collective-permute-start.9 = (bf16[4,24,3200]{2,1,0:T(8,128)(2,1)S(1)}, bf16[4,24,3200]{2,1,0:T(8,128)(2,1)S(1)}, u32[]{:S(2)}, u32[]{:S(2)}) collective-permute-start(bf16[4,24,3200]{2,1,0:T(8,128)(2,1)S(1)} %get-tuple-element.82), channel_id=1, source_target_pairs={{0,4},{1,3},{2,6},{3,1},{4,0},{5,7},{6,2},{7,5},{8,12},{9,11},{10,... | collective-permute-start | bytes 1843208 | tf_op jit(solution)/shard_map/ppermute | solution.py:528
  310.2 14.1 %collective-permute-start.10 = (bf16[2,24,3200]{2,1,0:T(8,128)(2,1)S(1)}, bf16[2,24,3200]{2,1,0:T(8,128)(2,1)S(1)}, u32[]{:S(2)}, u32[]{:S(2)}) collective-permute-start(bf16[2,24,3200]{2,1,0:T(8,128)(2,1)S(1)} %get-tuple-element.86), channel_id=1, source_target_pairs={{0,8},{8,0},{16,24},{24,16},{1,9},{9,1},{17,25},{25,17},{2,10},{10... | collective-permute-start | bytes 921608 | tf_op jit(solution)/shard_map/ppermute | solution.py:528
  312.1 16.1 %collective-permute-start.12 = (bf16[24,6144]{1,0:T(8,128)(2,1)S(1)}, bf16[24,6144]{1,0:T(8,128)(2,1)S(1)}, u32[]{:S(2)}, u32[]{:S(2)}) collective-permute-start(bf16[24,6144]{1,0:T(8,128)(2,1)S(1)} %get-tuple-element.83), channel_id=1, source_target_pairs={{0,16},{8,24},{16,0},{24,8},{1,17},{9,25},{17,1},{25,9},{2,18},{10... | collective-permute-start | bytes 884744 | tf_op jit(solution)/shard_map/ppermute | solution.py:528
  325.0 8.1 %collective-permute-start.11 = (bf16[1,24,3200]{2,1,0:T(8,128)(2,1)S(1)}, bf16[1,24,3200]{2,1,0:T(8,128)(2,1)S(1)}, u32[]{:S(2)}, u32[]{:S(2)}) collective-permute-start(bf16[1,24,3200]{2,1,0:T(8,128)(2,1)S(1)} %get-tuple-element.87), channel_id=1, source_target_pairs={{0,16},{8,24},{16,0},{24,8},{1,17},{9,25},{17,1},{25,9},{2,18},{10... | collective-permute-start | bytes 460808 | tf_op jit(solution)/shard_map/ppermute | solution.py:528
  328.2 0.7 copy-start.7
  333.1 0.7 copy-start.8
Sparse Core Ops, SparseCore 0:
  10.9 98.0 all-gather.1
  199.5 80.6 reduce-scatter.1

commit v5 on v4

--- a/solution.py
+++ b/solution.py
@@ -421,40 +421,70 @@
 
 def block_kernel(at_ref,x_ref,oT_ref,dy_ref,ga_ref,wo_ref,win_ref,wout_ref,
                  out_ref,dm_ref,doT_ref,dwo_ref,*rest,FC,SUB,nc,nt,legs):
-    dw_ref,b_s,bT_s,oacc,dacc,ain,aout,awo,m_s=rest
+    dw_ref,b_s,oacc,dacc,ain,aout,awo,m_s=rest
     c=pl.program_id(0); t=pl.program_id(1)
     rows=pl.ds(t*BLOCK,BLOCK)
     def middle():
         return x_ref[...].astype(F32)+dot(oT_ref[...].T,wo_ref[...],NT)
+    @pl.when(t==0)
+    def _():
+        ain[...]=jnp.zeros_like(ain); aout[...]=jnp.zeros_like(aout)
+    @pl.when((c==nc-1)&(t==0))
+    def _(): awo[...]=jnp.zeros_like(awo)
+    n=FC//SUB
+    def inner(dy):
+        return [dot(dy,wout_ref[:,s*SUB:(s+1)*SUB]) for s in range(n)]
+    def gates(b,DG):
+        U=[dot(b,win_ref[:,s*SUB:(s+1)*SUB]) for s in range(n)]
+        G=[];DU=[]
+        for s in range(n):
+            g,pull=gate(U[s],"erf")
+            G.append(g.astype(BF16)); DU.append((DG[s]*pull).astype(BF16))
+        return G,DU
+    def sums(bt,dyt,G,DU):
+        for s in range(n):
+            sl=slice(s*SUB,(s+1)*SUB)
+            aout[:,sl]+=dot(dyt,G[s])
+            ain[:,sl]+=dot(bt,DU[s])
+    def outer(G,DU):
+        return dot(jnp.concatenate(G,1),wout_ref[...],NT),dot(jnp.concatenate(DU,1),win_ref[...],NT)
     @pl.when(c==0)
     def _():
+        dy=dy_ref[...]
+        DG=inner(dy)
         m=middle()
         b=(m*rms(m)*row_of(ga_ref[...],1)).astype(BF16)
         b_s[t]=b
-        bT_s[t]=b.T
-        oacc[rows,:]=m
         m_s[rows,:]=m
-        dacc[rows,:]=jnp.zeros((BLOCK,D),F32)
-    b=b_s[t]; dy=dy_ref[...]
-    dyt=dy.T
-    G=[];DU=[]
-    n=FC//SUB
-    U=[dot(b,win_ref[:,s*SUB:(s+1)*SUB]) for s in range(n)]
-    DG=[dot(dy,wout_ref[:,s*SUB:(s+1)*SUB]) for s in range(n)]
-    @pl.when(t==0)
-    def _():
-        ain[...]=jnp.zeros_like(ain); aout[...]=jnp.zeros_like(aout)
-    for s in range(n):
-        g,pull=gate(U[s],"erf")
-        g=g.astype(BF16)
-        du=(DG[s]*pull).astype(BF16)
-        sl=slice(s*SUB,(s+1)*SUB)
-        aout[:,sl]+=dot(dyt,g)
-        ain[:,sl]+=dot(bT_s[t],du)
-        G.append(g);DU.append(du)
-    g=jnp.concatenate(G,1);du=jnp.concatenate(DU,1)
-    oacc[rows,:]+=dot(g,wout_ref[...],NT)
-    dacc[rows,:]+=dot(du,win_ref[...],NT)
+        G,DU=gates(b,DG)
+        o,d=outer(G,DU)
+        sums(b.T,dy.T,G,DU)
+        oacc[rows,:]=m+o
+        dacc[rows,:]=d
+    @pl.when((c>0)&(c<nc-1))
+    def _():
+        dy=dy_ref[...]; b=b_s[t]
+        G,DU=gates(b,inner(dy))
+        sums(b.T,dy.T,G,DU)
+        o,d=outer(G,DU)
+        oacc[rows,:]+=o
+        dacc[rows,:]+=d
+    @pl.when(c==nc-1)
+    def _():
+        dy=dy_ref[...]; b=b_s[t]
+        G,DU=gates(b,inner(dy))
+        o,d=outer(G,DU)
+        db=dacc[rows,:]+d
+        out_ref[...]=(oacc[rows,:]+o).astype(BF16)
+        sums(b.T,dy.T,G,DU)
+        m=m_s[rows,:]
+        r=rms(m); n2=m*r
+        dn=db*row_of(ga_ref[...],1)
+        dm=dy.astype(F32)+r*(dn-n2*jnp.mean(dn*n2,axis=-1,keepdims=True))
+        dm_ref[...]=dm
+        dmb=dm.astype(BF16)
+        awo[...]+=dot(dmb.T,oT_ref[...],NT)
+        doT_ref[...]=dot(dmb,wo_ref[...]).astype(BF16).T
     @pl.when(t==nt-1)
     def _():
         if legs:
@@ -467,20 +497,6 @@
         else:
             dw_ref[:,:FC]=ain[...].astype(BF16)
             dw_ref[:,FC:]=aout[...].astype(BF16)
-    @pl.when((c==nc-1)&(t==0))
-    def _(): awo[...]=jnp.zeros_like(awo)
-    @pl.when(c==nc-1)
-    def _():
-        out_ref[...]=oacc[rows,:].astype(BF16)
-        m=m_s[rows,:]
-        db=dacc[rows,:]
-        r=rms(m); n2=m*r
-        dn=db*row_of(ga_ref[...],1)
-        dm=dy.astype(F32)+r*(dn-n2*jnp.mean(dn*n2,axis=-1,keepdims=True))
-        dm_ref[...]=dm
-        dmb=dm.astype(BF16)
-        awo[...]+=dot(dmb.T,oT_ref[...],NT)
-        doT_ref[...]=dot(dmb,wo_ref[...]).astype(BF16).T
     @pl.when((c==nc-1)&(t==nt-1))
     def _(): dwo_ref[...]=awo[...].astype(BF16)
 def block_call(x,oT,dy,gains,wo,win,wout,core,legs,FC=768,SUB=256):
@@ -495,10 +511,10 @@
         in_specs=[BS((BLOCK,D),lambda c,t,at:(first(c,t),0)),BS((D,BLOCK),lambda c,t,at:(0,ends(c,t))),
             BS((BLOCK,D),lambda c,t,at:(t,0)),
             BS((D,GA),lambda c,t,at:(0,gains[1]),pipeline_mode=one),BS((D,D),lambda c,t,at:(0,wo[1]),pipeline_mode=one),
-            BS((D,FC),lambda c,t,at:(0,c+win[1]*D//FC)),BS((D,FC),lambda c,t,at:(0,c+wout[1]*D//FC))],
+            BS((D,FC),lambda c,t,at:(0,c+win[1])),BS((D,FC),lambda c,t,at:(0,c+wout[1]))],
         out_specs=[BS((BLOCK,D),lambda c,t,at:(last(c,t),0)),BS((BLOCK,D),lambda c,t,at:(last(c,t),0)),BS((D,BLOCK),lambda c,t,at:(0,last(c,t))),
             BS((D,D),lambda c,t,at:(0,0),pipeline_mode=one)]+([BS((32,R,2*FC),lambda c,t,at:(0,0,c))] if legs else [BS((D,2*FC),lambda c,t,at:(0,c))]),
-        scratch_shapes=[pltpu.VMEM((nt,BLOCK,D),BF16),pltpu.VMEM((nt,D,BLOCK),BF16),
+        scratch_shapes=[pltpu.VMEM((nt,BLOCK,D),BF16),
             pltpu.VMEM((T,D),F32),pltpu.VMEM((T,D),F32),pltpu.VMEM((D,FC),F32),pltpu.VMEM((D,FC),F32),pltpu.VMEM((D,D),F32),pltpu.VMEM((T,D),F32)]),
         out_shape=[sd((T,D),BF16),sd((T,D),F32),sd((D,T),BF16),sd((D,D),BF16)]+([sd((32,R,2*FF),BF16)] if legs else [sd((D,2*FF),BF16)]),
         name="feed_forward",
@@ -516,9 +532,9 @@
     return pl.pallas_call(pack_a_kernel,out_shape=jax.ShapeDtypeStruct((q.shape[0],GW),BF16),name="pack_attention")(q,k,v,g1[None],g2[None])
 def pack_b_kernel(wo_ref,wi_ref,wu_ref,o_ref):
     F=wi_ref.shape[1]
-    o_ref[:,:D]=wo_ref[...].astype(BF16)
-    o_ref[:,D:D+F]=wi_ref[...].astype(BF16)
-    o_ref[:,D+F:]=wu_ref[...].astype(BF16)
+    o_ref[:,:F]=wi_ref[...].astype(BF16)
+    o_ref[:,F:2*F]=wu_ref[...].astype(BF16)
+    o_ref[:,2*F:]=wo_ref[...].astype(BF16)
 def pack_b(wo,wi,wu):
     return pl.pallas_call(pack_b_kernel,out_shape=jax.ShapeDtypeStruct((wi.shape[0],D+2*wi.shape[1]),BF16),name="pack_feed_forward")(wo.T,wi,wu.T)
 
@@ -638,7 +654,10 @@
         r=swap(out,axis,leg)
         if half==8:
             r,beside,other=lax.optimization_barrier((r,beside,other))
-            late=rest(other)
+            late=rest[0](other)
+        if half==2:
+            r,late=lax.optimization_barrier((r,late))
+            late=rest[1](late)
     r,late=lax.optimization_barrier((r,late))
     return keep[0],r[0],beside,late
 def finish_kernel(a_ref,b_ref,wq_ref,wk_ref,wv_ref,g_ref,q_ref,k_ref,v_ref,o_ref,tab_ref,dg_ref):
@@ -696,14 +715,14 @@
         bias=bias_call(bias_table)
         gains=jnp.concatenate([norm1_gain[:,None],norm2_gain[:,None],jnp.zeros((rows,GA-2),F32)],1)
         pa=jnp.concatenate([query_w,key_w,value_w,gains],1).astype(BF16)
-        pb=jnp.concatenate([out_w.T,ffn_in,ffn_out.T],1).astype(BF16)
+        pb=jnp.concatenate([ffn_in,ffn_out.T,out_w.T],1).astype(BF16)
         wa=lax.all_gather(pa,BOTH,axis=0,tiled=True)
         wb=lax.all_gather(pb,BOTH,axis=0,tiled=True)
         aT,qkvT=qkv_call(hidden,wa)
     oT,lse=fwd2_call(long_flags,qkvT,bias,HP=4,mode="ones")
     GB=3*D//GA
     z=(lax.axis_index("dp") if legs else jnp.zeros((),jnp.int32)).reshape(1)
-    out,dm,doT,dwoT,dffn=block_call(hidden,oT,out_grad,(wa,GB),(wb,0),(wb,1),(wb,5),z,legs,FC=FC)
+    out,dm,doT,dwoT,dffn=block_call(hidden,oT,out_grad,(wa,GB),(wb,2*FF//D),(wb,0),(wb,FF//FC),z,legs,FC=FC)
     def rs(x,axes=BOTH): return lax.psum_scatter(x,axes,scatter_dimension=0,tiled=True)
     fsum=rs(dffn.reshape(D,2*FF),INNER if legs else BOTH)
     gT,tab=bwd2_call(long_flags,qkvT,doT,lse,bias,HP=4)
@@ -712,9 +731,7 @@
         h=fsum.reshape(4,rows,2*FF)
         h,dm=lax.optimization_barrier((h,dm))
         r=swap(h[2:],"dp",1)
-        def rest(r):
-            fa,fb=add(h[0],r[0]),swap(add(h[1],r[1]),"dp",2)
-            return finish_ffn_call(fa,fb,ffn_in,norm2_gain,FC)
+        rest=(lambda r:(add(h[0],r[0]),swap(add(h[1],r[1]),"dp",2)),lambda z:finish_ffn_call(*z,ffn_in,norm2_gain,FC))
         a,b2,dx,(di,du,dg2)=scatter_sum(keep,send,last_call(hidden,dm,gT,wa),r,rest)
         dq,dk,dv,do,table,dg1=finish_call(a,b2,query_w,key_w,value_w,norm1_gain)
         dg1=dg1[0]; dg2=dg2[0]; table=table.T

time: 343 us -> 339 us (0.988)
  Pallas kernels: 235 us -> 230 us
    pallas_call x1, Pallas kernels: 90.2 us -> 85.5 us  [block_call(): pl.pallas_call(functools.partial(block_kernel, FC=FC, SUB=SUB, nc=nc, nt=...]
  transfers between devices with their start and end apart: 15 -> 15, of which waited for: 11 -> 10; matrix products, arithmetic and copies ran while one was open for 1% -> 1% of each run, Pallas kernels for 41% -> 42%
where the time goes in v5:
time: 339 us; the launch traced here: 338 us
  Pallas kernels  230 us (68%)
  waiting for transfers between devices  68.4 us (20%)
  starting transfers between devices  17.1 us (5%)
  between operations  14.2 us (4%)
  other arithmetic  5.69 us (2%)
    pallas_call x1, Pallas kernels, block_call(): pl.pallas_call(functools.partial(block_kernel, FC=FC, SUB=SUB, nc=nc, nt=...  85.5 us
    ppermute x13, waiting for transfers between devices, swap(): return lax.ppermute(x, axis, [(i, i ^ f(i)) for i in range(n)])  63.2 us
    pallas_call x1, Pallas kernels, bwd2_call(): pl.pallas_call(functools.partial(bwd2_kernel, HP=HP, nb=n, tabmode=tabmod...  55.4 us
    pallas_call x1, Pallas kernels, fwd2_call(): pl.pallas_call(functools.partial(fwd2_kernel, HP=HP, mode=mode), grid_spe...  29.7 us
    ppermute x13, starting transfers between devices, swap(): return lax.ppermute(x, axis, [(i, i ^ f(i)) for i in range(n)])  17 us
    pallas_call x1, Pallas kernels, last_call(): pl.pallas_call(last_kernel, grid=(nt,), in_specs=[row, row, pl.BlockSpec(...  15.7 us
    pallas_call x1, Pallas kernels, project2_call(): pl.pallas_call(project2_kernel, grid_spec=pltpu.PrefetchScalarGridSpec(nu...  15.1 us
    pallas_call x1, Pallas kernels, grads_call(): pl.pallas_call(grads_kernel, grid_spec=pltpu.PrefetchScalarGridSpec(num_s...  12.9 us
  transfers between devices with their start and end apart: 15, of which 10 were waited for; matrix products, arithmetic and copies ran while one was open for 1% of the time, Pallas kernels for 42%

profile of v5, /device:TPU:0, one launch (start us, length us, event | category | flops | bytes accessed | tf_op | source)
XLA Modules:
  0.0 338.2 jit_solution(10307850744856857545)
XLA Ops:
  7.2 1.9 pack_feed_forward.1
  9.2 1.7 pack_attention.1
  10.9 4.0 %collective-permute-start = (bf16[1,24,2432]{2,1,0:T(8,128)(2,1)}, bf16[1,24,2432]{2,1,0:T(8,128)(2,1)S(1)}, u32[]{:S(2)}, u32[]{:S(2)}) collective-permute-start(bf16[1,24,2432]{2,1,0:T(8,128)(2,1)} %bitcast.23), channel_id=1, source_target_pairs={{0,16},{8,24},{16,0},{24,8},{1,17},{9,25},{17,1},{25,9},{2,18},{10... | collective-permute-start | bytes 350216 | tf_op jit(solution)/shard_map/ppermute | solution.py:544
  14.9 5.9 %collective-permute-done = bf16[1,24,2432]{2,1,0:T(8,128)(2,1)S(1)} collective-permute-done((bf16[1,24,2432]{2,1,0:T(8,128)(2,1)}, bf16[1,24,2432]{2,1,0:T(8,128)(2,1)S(1)}, u32[]{:S(2)}, u32[]{:S(2)}) %collective-permute-start) | collective-permute-done | bytes 116768 | tf_op jit(solution)/shard_map/ppermute | solution.py:544
  22.6 8.6 %bias.1.bias_ref = f32[12,512,512]{2,1,0:T(8,128)} custom-call(f32[12,32]{1,0:T(8,128)} %bitcast.32), custom_call_target="tpu_custom_call" | custom-call | tf_op jit(solution)/shard_map/bias/pallas_call | solution.py:49
  31.2 1.7 collective-permute-done.1
  34.4 7.2 %collective-permute-done.2 = bf16[4,24,2432]{2,1,0:T(8,128)(2,1)S(1)} collective-permute-done((bf16[4,24,2432]{2,1,0:T(8,128)(2,1)S(1)}, bf16[4,24,2432]{2,1,0:T(8,128)(2,1)S(1)}, u32[]{:S(2)}, u32[]{:S(2)}) %collective-permute-start.2) | collective-permute-done | bytes 466976 | tf_op jit(solution)/shard_map/ppermute | solution.py:544
  43.2 16.9 %collective-permute-done.3.b_ref = bf16[8,24,2432]{2,1,0:T(8,128)(2,1)S(1)} collective-permute-done((bf16[8,24,2432]{2,1,0:T(8,128)(2,1)S(1)}, bf16[8,24,2432]{2,1,0:T(8,128)(2,1)S(1)}, u32[]{:S(2)}, u32[]{:S(2)}) %collective-permute-start.3) | collective-permute-done | bytes 933920 | tf_op jit(solution)/shard_map/ppermute | solution.py:544
  60.1 2.0 collective-permute-start.5
  62.7 1.7 collective-permute-done.5.d_ref
  64.4 15.1 %project.1 = (bf16[768,2048]{1,0:T(8,128)(2,1)}, bf16[2304,2048]{1,0:T(8,128)(2,1)}, bf16[768,2432]{1,0:T(8,128)(2,1)}) custom-call(s32[2]{0:T(128)} %pad_add_fusion.1.at_ref, bf16[2048,768]{1,0:T(8,128)(2,1)} %x_ref.5, bf16[8,24,2432]{2,1,0:T(8,128)(2,1)} %copy-done.2, bf16[8,24,2432]{2,1,0:T(8,128)(2,1)} %copy-done.5, bf16[8,24,2432]{2,1,0:T(8,128)(2,1)} %copy-done.6, ...), custom_call_target="tpu_custom_call" | custom-call | tf_op jit(solution)/shard_map/project/pallas_call | solution.py:598
  79.5 29.7 %attend.1 = (bf16[768,2048]{1,0:T(8,128)(2,1)}, f32[12,1,2048]{2,1,0:T(1,128)}) custom-call(s32[4]{0:T(128)} %flags_ref.3, bf16[2304,2048]{1,0:T(8,128)(2,1)} %get-tuple-element.49.q_ref.k_ref.v_ref, bf16[2304,2048]{1,0:T(8,128)(2,1)} %get-tuple-element.49.q_ref.k_ref.v_ref, bf16[2304,2048]{1,0:T(8,128)(2,1)} %get-tuple-element.49.q_ref.k_ref.v_ref, ...), custom_call_target="tpu_custom_call" | custom-call | tf_op jit(solution)/shard_map/attend/pallas_call | solution.py:180
  109.2 85.5 %feed_forward.1 = (bf16[2048,768]{1,0:T(8,128)(2,1)}, f32[2048,768]{1,0:T(8,128)}, bf16[768,2048]{1,0:T(8,128)(2,1)}, bf16[768,768]{1,0:T(8,128)(2,1)}, bf16[32,24,6144]{2,1,0:T(8,128)(2,1)}) custom-call(s32[1]{0:T(128)} %bitcast.at_ref, bf16[2048,768]{1,0:T(8,128)(2,1)} %x_ref.5, bf16[768,2048]{1,0:T(8,128)(2,1)} %get-tuple-element.51.oT_ref, ...), custom_call_target="tpu_custom_call" | custom-call | tf_op jit(solution)/shard_map/feed_forward/pallas_call | solution.py:509
  194.8 55.4 %attend_back.1 = (bf16[3,768,2048]{2,1,0:T(8,128)(2,1)}, f32[12,8,128]{2,1,0:T(8,128)}) custom-call(s32[4]{0:T(128)} %flags_ref.3, bf16[2304,2048]{1,0:T(8,128)(2,1)} %get-tuple-element.49.q_ref.k_ref.v_ref, bf16[2304,2048]{1,0:T(8,128)(2,1)} %get-tuple-element.49.q_ref.k_ref.v_ref, bf16[2304,2048]{1,0:T(8,128)(2,1)} %get-tuple-element.49.q_ref.k_ref.v_ref, ...), custom_call_target="tpu_custom_call" | custom-call | tf_op jit(solution)/shard_map/attend_back/pallas_call | solution.py:268
  250.9 12.9 %weight_grads.1 = (bf16[16,24,3200]{2,1,0:T(8,128)(2,1)S(1)}, bf16[16,24,3200]{2,1,0:T(8,128)(2,1)S(1)}) custom-call(s32[2,16]{1,0:T(2,128)S(1)} %pad_add_fusion.at_ref, bf16[768,2048]{1,0:T(8,128)(2,1)} %get-tuple-element.54.aT_ref, bf16[3,768,2048]{2,1,0:T(8,128)(2,1)} %get-tuple-element.57.g_ref, bf16[768,768]{1,0:T(8,128)(2,1)S(1)} %copy-done, ...), custom_call_target="tpu_custom_call" | custom-call | tf_op jit(solution)/shard_map/weight_grads/pallas_call | solution.py:640
  264.4 4.3 %collective-permute-done.6 = bf16[16,24,3200]{2,1,0:T(8,128)(2,1)S(1)} collective-permute-done((bf16[16,24,3200]{2,1,0:T(8,128)(2,1)S(1)}, bf16[16,24,3200]{2,1,0:T(8,128)(2,1)S(1)}, u32[]{:S(2)}, u32[]{:S(2)}) %collective-permute-start.6) | collective-permute-done | bytes 2457632 | tf_op jit(solution)/shard_map/ppermute | solution.py:544
  270.3 5.2 %reduce-scatter.2.cloned.1.call-done = bf16[96,6144]{1,0:T(8,128)(2,1)} async-done(((bf16[768,6144]{1,0:T(8,128)(2,1)}), bf16[96,6144]{1,0:T(8,128)(2,1)}) %reduce-scatter.2.cloned.1.call-update) | async-done | bytes 1179664 | tf_op jit(solution)/shard_map/reduce_scatter | solution.py:726
  277.7 15.7 %project_back.1 = bf16[2048,768]{1,0:T(8,128)(2,1)} custom-call(bf16[2048,768]{1,0:T(8,128)(2,1)} %x_ref.5, f32[2048,768]{1,0:T(8,128)} %get-tuple-element.64.dm_ref, bf16[3,768,2048]{2,1,0:T(8,128)(2,1)} %get-tuple-element.57.g_ref, bf16[768,2432]{1,0:T(8,128)(2,1)} %get-tuple-element.52.ga_ref.w_ref), custom_call_target="tpu_custom_call" | custom-call | flops 7247757312 | bytes 31457280 | tf_op jit(solution)/shard_map/project_back/pallas_call | solution.py:416
  296.5 8.8 %collective-permute-done.9 = bf16[4,24,3200]{2,1,0:T(8,128)(2,1)S(1)} collective-permute-done((bf16[4,24,3200]{2,1,0:T(8,128)(2,1)S(1)}, bf16[4,24,3200]{2,1,0:T(8,128)(2,1)S(1)}, u32[]{:S(2)}, u32[]{:S(2)}) %collective-permute-start.9) | collective-permute-done | bytes 614432 | tf_op jit(solution)/shard_map/ppermute | solution.py:544
  307.5 1.8 collective-permute-start.11
  309.3 12.7 %collective-permute-done.11.t_ref = bf16[24,6144]{1,0:T(8,128)(2,1)S(1)} collective-permute-done((bf16[24,6144]{1,0:T(8,128)(2,1)S(1)}, bf16[24,6144]{1,0:T(8,128)(2,1)S(1)}, u32[]{:S(2)}, u32[]{:S(2)}) %collective-permute-start.11) | collective-permute-done | bytes 294944 | tf_op jit(solution)/shard_map/ppermute | solution.py:544
  322.7 2.0 finish_feed_forward.1
  324.8 4.1 %collective-permute-done.12 = bf16[1,24,3200]{2,1,0:T(8,128)(2,1)S(1)} collective-permute-done((bf16[1,24,3200]{2,1,0:T(8,128)(2,1)S(1)}, bf16[1,24,3200]{2,1,0:T(8,128)(2,1)S(1)}, u32[]{:S(2)}, u32[]{:S(2)}) %collective-permute-start.12) | collective-permute-done | bytes 153632 | tf_op jit(solution)/shard_map/ppermute | solution.py:544
  329.5 1.9 finish_attention.1
  (49 shorter events, 17.5 us)
Async XLA Ops:
  7.2 102.0 %all-gather.2.cloned.1.call-start = ((), (), s32[]{:S(2)}) async-start(), calls=%async_computation.1 | async-start | bytes 10948608 | tf_op jit(solution)/shard_map/all_gather | solution.py:710
  9.1 266.5 %reduce-scatter.2.cloned.1.call-start = ((), (), s32[]{:S(2)}) async-start(), calls=%async_computation.2 | async-start | bytes 10616832 | tf_op jit(solution)/shard_map/reduce_scatter | solution.py:726
  10.9 9.9 %collective-permute-start = (bf16[1,24,2432]{2,1,0:T(8,128)(2,1)}, bf16[1,24,2432]{2,1,0:T(8,128)(2,1)S(1)}, u32[]{:S(2)}, u32[]{:S(2)}) collective-permute-start(bf16[1,24,2432]{2,1,0:T(8,128)(2,1)} %bitcast.23), channel_id=1, source_target_pairs={{0,16},{8,24},{16,0},{24,8},{1,17},{9,25},{17,1},{25,9},{2,18},{10... | collective-permute-start | bytes 350216 | tf_op jit(solution)/shard_map/ppermute | solution.py:544
  21.7 11.2 %collective-permute-start.1 = (bf16[2,24,2432]{2,1,0:T(8,128)(2,1)S(1)}, bf16[2,24,2432]{2,1,0:T(8,128)(2,1)S(1)}, u32[]{:S(2)}, u32[]{:S(2)}) collective-permute-start(bf16[2,24,2432]{2,1,0:T(8,128)(2,1)S(1)} %pad_maximum_fusion.2), channel_id=1, source_target_pairs={{0,8},{8,0},{16,24},{24,16},{1,9},{9,1},{17,25},{25,17},{2,10},{10... | collective-permute-start | bytes 700424 | tf_op jit(solution)/shard_map/ppermute | solution.py:544
  22.6 10.3 %copy-start.3 = (bf16[24,2432]{1,0:T(8,128)(2,1)S(1)}, bf16[24,2432]{1,0:T(8,128)(2,1)}, u32[]{:S(2)}) copy-start(bf16[24,2432]{1,0:T(8,128)(2,1)} %pack_attention.1) | copy-start | bytes 350212
  32.9 8.6 %collective-permute-start.2 = (bf16[4,24,2432]{2,1,0:T(8,128)(2,1)S(1)}, bf16[4,24,2432]{2,1,0:T(8,128)(2,1)S(1)}, u32[]{:S(2)}, u32[]{:S(2)}) collective-permute-start(bf16[4,24,2432]{2,1,0:T(8,128)(2,1)S(1)} %pad_maximum_fusion.1), channel_id=1, source_target_pairs={{0,2},{1,5},{2,0},{3,7},{4,6},{5,1},{6,4},{7,3},{8,10},{9,13},{10,... | collective-permute-start | bytes 1400840 | tf_op jit(solution)/shard_map/ppermute | solution.py:544
  41.7 22.7 %copy-start.2 = (bf16[8,24,2432]{2,1,0:T(8,128)(2,1)}, bf16[8,24,2432]{2,1,0:T(8,128)(2,1)S(1)}, u32[]{:S(2)}) copy-start(bf16[8,24,2432]{2,1,0:T(8,128)(2,1)S(1)} %pad_maximum_fusion.a_ref) | copy-start | bytes 2801668
  41.7 18.4 %collective-permute-start.3 = (bf16[8,24,2432]{2,1,0:T(8,128)(2,1)S(1)}, bf16[8,24,2432]{2,1,0:T(8,128)(2,1)S(1)}, u32[]{:S(2)}, u32[]{:S(2)}) collective-permute-start(bf16[8,24,2432]{2,1,0:T(8,128)(2,1)S(1)} %pad_maximum_fusion.a_ref), channel_id=1, source_target_pairs={{0,4},{1,3},{2,6},{3,1},{4,0},{5,7},{6,2},{7,5},{8,12},{9,11},{10,... | collective-permute-start | bytes 2801672 | tf_op jit(solution)/shard_map/ppermute | solution.py:544
  43.2 19.5 %collective-permute-start.4 = (bf16[8,24,2432]{2,1,0:T(8,128)(2,1)S(1)}, bf16[8,24,2432]{2,1,0:T(8,128)(2,1)S(1)}, u32[]{:S(2)}, u32[]{:S(2)}) collective-permute-start(bf16[8,24,2432]{2,1,0:T(8,128)(2,1)S(1)} %pad_maximum_fusion.a_ref), channel_id=1, source_target_pairs={{0,1},{1,0},{2,3},{3,2},{4,5},{5,4},{6,7},{7,6},{8,9},{9,8},{10,11... | collective-permute-start | bytes 2801672 | tf_op jit(solution)/shard_map/ppermute | solution.py:544
  60.1 4.3 %copy-start.5 = (bf16[8,24,2432]{2,1,0:T(8,128)(2,1)}, bf16[8,24,2432]{2,1,0:T(8,128)(2,1)S(1)}, u32[]{:S(2)}) copy-start(bf16[8,24,2432]{2,1,0:T(8,128)(2,1)S(1)} %collective-permute-done.3.b_ref) | copy-start | bytes 2801668
  60.1 4.3 %collective-permute-start.5 = (bf16[8,24,2432]{2,1,0:T(8,128)(2,1)S(1)}, bf16[8,24,2432]{2,1,0:T(8,128)(2,1)}, u32[]{:S(2)}, u32[]{:S(2)}) collective-permute-start(bf16[8,24,2432]{2,1,0:T(8,128)(2,1)S(1)} %collective-permute-done.3.b_ref), channel_id=1, source_target_pairs={{0,1},{1,0},{2,3},{3,2},{4,5},{5,4},{6,7},{7,6},{8,9},{9,8},{10,11... | collective-permute-start | bytes 2801672 | tf_op jit(solution)/shard_map/ppermute | solution.py:544
  62.7 1.7 copy-start.6
  194.8 55.4 %copy-start = (bf16[768,768]{1,0:T(8,128)(2,1)S(1)}, bf16[768,768]{1,0:T(8,128)(2,1)}, u32[]{:S(2)}) copy-start(bf16[768,768]{1,0:T(8,128)(2,1)} %get-tuple-element.58.wo_ref) | copy-start | bytes 3538948
  250.1 0.8 copy-start.1
  263.8 4.9 %collective-permute-start.6 = (bf16[16,24,3200]{2,1,0:T(8,128)(2,1)S(1)}, bf16[16,24,3200]{2,1,0:T(8,128)(2,1)S(1)}, u32[]{:S(2)}, u32[]{:S(2)}) collective-permute-start(bf16[16,24,3200]{2,1,0:T(8,128)(2,1)S(1)} %get-tuple-element.61), channel_id=1, source_target_pairs={{0,1},{1,0},{2,3},{3,2},{4,5},{5,4},{6,7},{7,6},{8,9},{9,8},{10,11... | collective-permute-start | bytes 7372808 | tf_op jit(solution)/shard_map/ppermute | solution.py:544
  269.2 24.2 %collective-permute-start.7 = (bf16[8,24,3200]{2,1,0:T(8,128)(2,1)S(1)}, bf16[8,24,3200]{2,1,0:T(8,128)(2,1)}, u32[]{:S(2)}, u32[]{:S(2)}) collective-permute-start(bf16[8,24,3200]{2,1,0:T(8,128)(2,1)S(1)} %get-tuple-element.86), channel_id=1, source_target_pairs={{0,2},{1,5},{2,0},{3,7},{4,6},{5,1},{6,4},{7,3},{8,10},{9,13},{10,... | collective-permute-start | bytes 3686408 | tf_op jit(solution)/shard_map/ppermute | solution.py:544
  276.7 16.7 %collective-permute-start.8 = (bf16[2,24,6144]{2,1,0:T(8,128)(2,1)S(1)}, bf16[2,24,6144]{2,1,0:T(8,128)(2,1)S(1)}, u32[]{:S(2)}, u32[]{:S(2)}) collective-permute-start(bf16[2,24,6144]{2,1,0:T(8,128)(2,1)S(1)} %slice.65), channel_id=1, source_target_pairs={{0,8},{8,0},{16,24},{24,16},{1,9},{9,1},{17,25},{25,17},{2,10},{10... | collective-permute-start | bytes 1769480 | tf_op jit(solution)/shard_map/ppermute | solution.py:544
  293.4 13.2 %copy-start.4 = (bf16[96,6144]{1,0:T(8,128)(2,1)S(1)}, bf16[96,6144]{1,0:T(8,128)(2,1)}, u32[]{:S(2)}) copy-start(bf16[96,6144]{1,0:T(8,128)(2,1)} %reduce-scatter.2.cloned.1.call-done) | copy-start | bytes 3538948
  295.1 10.2 %collective-permute-start.9 = (bf16[4,24,3200]{2,1,0:T(8,128)(2,1)S(1)}, bf16[4,24,3200]{2,1,0:T(8,128)(2,1)S(1)}, u32[]{:S(2)}, u32[]{:S(2)}) collective-permute-start(bf16[4,24,3200]{2,1,0:T(8,128)(2,1)S(1)} %get-tuple-element.88), channel_id=1, source_target_pairs={{0,4},{1,3},{2,6},{3,1},{4,0},{5,7},{6,2},{7,5},{8,12},{9,11},{10,... | collective-permute-start | bytes 1843208 | tf_op jit(solution)/shard_map/ppermute | solution.py:544
  305.4 16.5 %collective-permute-start.10 = (bf16[2,24,3200]{2,1,0:T(8,128)(2,1)S(1)}, bf16[2,24,3200]{2,1,0:T(8,128)(2,1)S(1)}, u32[]{:S(2)}, u32[]{:S(2)}) collective-permute-start(bf16[2,24,3200]{2,1,0:T(8,128)(2,1)S(1)} %get-tuple-element.91), channel_id=1, source_target_pairs={{0,8},{8,0},{16,24},{24,16},{1,9},{9,1},{17,25},{25,17},{2,10},{10... | collective-permute-start | bytes 921608 | tf_op jit(solution)/shard_map/ppermute | solution.py:544
  307.5 14.5 %collective-permute-start.11 = (bf16[24,6144]{1,0:T(8,128)(2,1)S(1)}, bf16[24,6144]{1,0:T(8,128)(2,1)S(1)}, u32[]{:S(2)}, u32[]{:S(2)}) collective-permute-start(bf16[24,6144]{1,0:T(8,128)(2,1)S(1)} %get-tuple-element.89), channel_id=1, source_target_pairs={{0,16},{8,24},{16,0},{24,8},{1,17},{9,25},{17,1},{25,9},{2,18},{10... | collective-permute-start | bytes 884744 | tf_op jit(solution)/shard_map/ppermute | solution.py:544
  322.0 0.8 copy-start.7
  322.7 6.1 %collective-permute-start.12 = (bf16[1,24,3200]{2,1,0:T(8,128)(2,1)S(1)}, bf16[1,24,3200]{2,1,0:T(8,128)(2,1)S(1)}, u32[]{:S(2)}, u32[]{:S(2)}) collective-permute-start(bf16[1,24,3200]{2,1,0:T(8,128)(2,1)S(1)} %get-tuple-element.93), channel_id=1, source_target_pairs={{0,16},{8,24},{16,0},{24,8},{1,17},{9,25},{17,1},{25,9},{2,18},{10... | collective-permute-start | bytes 460808 | tf_op jit(solution)/shard_map/ppermute | solution.py:544
  328.9 0.7 copy-start.8
Sparse Core Ops, SparseCore 0:
  10.9 98.0 all-gather.1
  194.8 80.6 reduce-scatter.1

commit v6 on v5

--- a/solution.py
+++ b/solution.py
@@ -646,20 +646,23 @@
         out_specs=[out,out],scratch_shapes=[pltpu.VMEM((D,D),F32)]),
         out_shape=[jax.ShapeDtypeStruct((16,R,GN),BF16)]*2,name="weight_grads",
         compiler_params=pltpu.CompilerParams(vmem_limit_bytes=48*2**20))(at,aT,gT,dwoT,tab)
-def scatter_sum(keep,send,beside,other,rest):
+def scatter_sum(keep,send,dm,beside,other,rest):
     r=swap(send,INNER,1)
     for half,axis,leg in ((8,INNER,first_leg),(4,INNER,second_leg),(2,"dp",1),(1,"dp",2)):
         out=add(keep[half:],r[half:])
         keep=add(keep[:half],r[:half])
+        if half==4:
+            out,dm=lax.optimization_barrier((out,dm))
+            dx=beside(dm)
         r=swap(out,axis,leg)
-        if half==8:
-            r,beside,other=lax.optimization_barrier((r,beside,other))
+        if half==4:
+            r,dx,other=lax.optimization_barrier((r,dx,other))
             late=rest[0](other)
         if half==2:
             r,late=lax.optimization_barrier((r,late))
             late=rest[1](late)
     r,late=lax.optimization_barrier((r,late))
-    return keep[0],r[0],beside,late
+    return keep[0],r[0],dx,late
 def finish_kernel(a_ref,b_ref,wq_ref,wk_ref,wv_ref,g_ref,q_ref,k_ref,v_ref,o_ref,tab_ref,dg_ref):
     R=a_ref.shape[0]
     tot=None
@@ -732,7 +735,7 @@
         h,dm=lax.optimization_barrier((h,dm))
         r=swap(h[2:],"dp",1)
         rest=(lambda r:(add(h[0],r[0]),swap(add(h[1],r[1]),"dp",2)),lambda z:finish_ffn_call(*z,ffn_in,norm2_gain,FC))
-        a,b2,dx,(di,du,dg2)=scatter_sum(keep,send,last_call(hidden,dm,gT,wa),r,rest)
+        a,b2,dx,(di,du,dg2)=scatter_sum(keep,send,dm,lambda dm:last_call(hidden,dm,gT,wa),r,rest)
         dq,dk,dv,do,table,dg1=finish_call(a,b2,query_w,key_w,value_w,norm1_gain)
         dg1=dg1[0]; dg2=dg2[0]; table=table.T
     else:

time: 339 us -> 344 us (1.015)
  starting transfers between devices: 17.1 us -> 21.6 us
    reduce_scatter x1, waiting for transfers between devices: 5.24 us -> 0.02 us  [rs(): return lax.psum_scatter(x, axes, scatter_dimension=0, tiled=True)]
    ppermute x13, starting transfers between devices: 17 us -> 21.5 us  [swap(): return lax.ppermute(x, axis, [(i, i ^ f(i)) for i in range(n)])]
    ppermute x13, waiting for transfers between devices: 63.2 us -> 66.8 us  [swap(): return lax.ppermute(x, axis, [(i, i ^ f(i)) for i in range(n)])]
where the time goes in v6:
time: 344 us; the launch traced here: 340 us
  Pallas kernels  230 us (67%)
  waiting for transfers between devices  66.9 us (19%)
  starting transfers between devices  21.6 us (6%)
  between operations  14.2 us (4%)
  other arithmetic  4.36 us (1%)
    pallas_call x1, Pallas kernels, block_call(): pl.pallas_call(functools.partial(block_kernel, FC=FC, SUB=SUB, nc=nc, nt=...  85.5 us
    ppermute x13, waiting for transfers between devices, swap(): return lax.ppermute(x, axis, [(i, i ^ f(i)) for i in range(n)])  66.8 us
    pallas_call x1, Pallas kernels, bwd2_call(): pl.pallas_call(functools.partial(bwd2_kernel, HP=HP, nb=n, tabmode=tabmod...  55.4 us
    pallas_call x1, Pallas kernels, fwd2_call(): pl.pallas_call(functools.partial(fwd2_kernel, HP=HP, mode=mode), grid_spe...  29.7 us
    ppermute x13, starting transfers between devices, swap(): return lax.ppermute(x, axis, [(i, i ^ f(i)) for i in range(n)])  21.5 us
    pallas_call x1, Pallas kernels, last_call(): pl.pallas_call(last_kernel, grid=(nt,), in_specs=[row, row, pl.BlockSpec(...  15.7 us
    pallas_call x1, Pallas kernels, project2_call(): pl.pallas_call(project2_kernel, grid_spec=pltpu.PrefetchScalarGridSpec(nu...  15.1 us
    pallas_call x1, Pallas kernels, grads_call(): pl.pallas_call(grads_kernel, grid_spec=pltpu.PrefetchScalarGridSpec(num_s...  12.9 us
  transfers between devices with their start and end apart: 15, of which 10 were waited for; matrix products, arithmetic and copies ran while one was open for 1% of the time, Pallas kernels for 42%

profile of v6, /device:TPU:0, one launch (start us, length us, event | category | flops | bytes accessed | tf_op | source)
XLA Modules:
  0.0 339.8 jit_solution(7736878807492575865)
XLA Ops:
  7.2 1.9 pack_feed_forward.1
  9.2 1.7 pack_attention.1
  10.9 4.0 %collective-permute-start = (bf16[1,24,2432]{2,1,0:T(8,128)(2,1)}, bf16[1,24,2432]{2,1,0:T(8,128)(2,1)S(1)}, u32[]{:S(2)}, u32[]{:S(2)}) collective-permute-start(bf16[1,24,2432]{2,1,0:T(8,128)(2,1)} %bitcast.23), channel_id=1, source_target_pairs={{0,16},{8,24},{16,0},{24,8},{1,17},{9,25},{17,1},{25,9},{2,18},{10... | collective-permute-start | bytes 350216 | tf_op jit(solution)/shard_map/ppermute | solution.py:544
  14.9 5.9 %collective-permute-done = bf16[1,24,2432]{2,1,0:T(8,128)(2,1)S(1)} collective-permute-done((bf16[1,24,2432]{2,1,0:T(8,128)(2,1)}, bf16[1,24,2432]{2,1,0:T(8,128)(2,1)S(1)}, u32[]{:S(2)}, u32[]{:S(2)}) %collective-permute-start) | collective-permute-done | bytes 116768 | tf_op jit(solution)/shard_map/ppermute | solution.py:544
  22.6 8.6 %bias.1.bias_ref = f32[12,512,512]{2,1,0:T(8,128)} custom-call(f32[12,32]{1,0:T(8,128)} %bitcast.32), custom_call_target="tpu_custom_call" | custom-call | tf_op jit(solution)/shard_map/bias/pallas_call | solution.py:49
  31.2 1.7 collective-permute-done.1
  34.4 7.2 %collective-permute-done.2 = bf16[4,24,2432]{2,1,0:T(8,128)(2,1)S(1)} collective-permute-done((bf16[4,24,2432]{2,1,0:T(8,128)(2,1)S(1)}, bf16[4,24,2432]{2,1,0:T(8,128)(2,1)S(1)}, u32[]{:S(2)}, u32[]{:S(2)}) %collective-permute-start.2) | collective-permute-done | bytes 466976 | tf_op jit(solution)/shard_map/ppermute | solution.py:544
  43.2 16.9 %collective-permute-done.3.b_ref = bf16[8,24,2432]{2,1,0:T(8,128)(2,1)S(1)} collective-permute-done((bf16[8,24,2432]{2,1,0:T(8,128)(2,1)S(1)}, bf16[8,24,2432]{2,1,0:T(8,128)(2,1)S(1)}, u32[]{:S(2)}, u32[]{:S(2)}) %collective-permute-start.3) | collective-permute-done | bytes 933920 | tf_op jit(solution)/shard_map/ppermute | solution.py:544
  60.1 2.0 collective-permute-start.5
  62.7 1.7 collective-permute-done.5.d_ref
  64.4 15.1 %project.1 = (bf16[768,2048]{1,0:T(8,128)(2,1)}, bf16[2304,2048]{1,0:T(8,128)(2,1)}, bf16[768,2432]{1,0:T(8,128)(2,1)}) custom-call(s32[2]{0:T(128)} %pad_add_fusion.1.at_ref, bf16[2048,768]{1,0:T(8,128)(2,1)} %x_ref.5, bf16[8,24,2432]{2,1,0:T(8,128)(2,1)} %copy-done.2, bf16[8,24,2432]{2,1,0:T(8,128)(2,1)} %copy-done.5, bf16[8,24,2432]{2,1,0:T(8,128)(2,1)} %copy-done.6, ...), custom_call_target="tpu_custom_call" | custom-call | tf_op jit(solution)/shard_map/project/pallas_call | solution.py:598
  79.5 29.7 %attend.1 = (bf16[768,2048]{1,0:T(8,128)(2,1)}, f32[12,1,2048]{2,1,0:T(1,128)}) custom-call(s32[4]{0:T(128)} %flags_ref.3, bf16[2304,2048]{1,0:T(8,128)(2,1)} %get-tuple-element.51.q_ref.k_ref.v_ref, bf16[2304,2048]{1,0:T(8,128)(2,1)} %get-tuple-element.51.q_ref.k_ref.v_ref, bf16[2304,2048]{1,0:T(8,128)(2,1)} %get-tuple-element.51.q_ref.k_ref.v_ref, ...), custom_call_target="tpu_custom_call" | custom-call | tf_op jit(solution)/shard_map/attend/pallas_call | solution.py:180
  109.2 85.5 %feed_forward.1 = (bf16[2048,768]{1,0:T(8,128)(2,1)}, f32[2048,768]{1,0:T(8,128)}, bf16[768,2048]{1,0:T(8,128)(2,1)}, bf16[768,768]{1,0:T(8,128)(2,1)}, bf16[32,24,6144]{2,1,0:T(8,128)(2,1)}) custom-call(s32[1]{0:T(128)} %bitcast.at_ref, bf16[2048,768]{1,0:T(8,128)(2,1)} %x_ref.5, bf16[768,2048]{1,0:T(8,128)(2,1)} %get-tuple-element.53.oT_ref, ...), custom_call_target="tpu_custom_call" | custom-call | tf_op jit(solution)/shard_map/feed_forward/pallas_call | solution.py:509
  194.8 55.4 %attend_back.1 = (bf16[3,768,2048]{2,1,0:T(8,128)(2,1)}, f32[12,8,128]{2,1,0:T(8,128)}) custom-call(s32[4]{0:T(128)} %flags_ref.3, bf16[2304,2048]{1,0:T(8,128)(2,1)} %get-tuple-element.51.q_ref.k_ref.v_ref, bf16[2304,2048]{1,0:T(8,128)(2,1)} %get-tuple-element.51.q_ref.k_ref.v_ref, bf16[2304,2048]{1,0:T(8,128)(2,1)} %get-tuple-element.51.q_ref.k_ref.v_ref, ...), custom_call_target="tpu_custom_call" | custom-call | tf_op jit(solution)/shard_map/attend_back/pallas_call | solution.py:268
  250.9 12.9 %weight_grads.1 = (bf16[16,24,3200]{2,1,0:T(8,128)(2,1)S(1)}, bf16[16,24,3200]{2,1,0:T(8,128)(2,1)S(1)}) custom-call(s32[2,16]{1,0:T(2,128)S(1)} %pad_add_fusion.at_ref, bf16[768,2048]{1,0:T(8,128)(2,1)} %get-tuple-element.56.aT_ref, bf16[3,768,2048]{2,1,0:T(8,128)(2,1)} %get-tuple-element.59.g_ref, bf16[768,768]{1,0:T(8,128)(2,1)S(1)} %copy-done, ...), custom_call_target="tpu_custom_call" | custom-call | tf_op jit(solution)/shard_map/weight_grads/pallas_call | solution.py:640
  264.4 4.3 %collective-permute-done.6 = bf16[16,24,3200]{2,1,0:T(8,128)(2,1)S(1)} collective-permute-done((bf16[16,24,3200]{2,1,0:T(8,128)(2,1)S(1)}, bf16[16,24,3200]{2,1,0:T(8,128)(2,1)S(1)}, u32[]{:S(2)}, u32[]{:S(2)}) %collective-permute-start.6) | collective-permute-done | bytes 2457632 | tf_op jit(solution)/shard_map/ppermute | solution.py:544
  270.4 16.1 %collective-permute-done.7 = bf16[8,24,3200]{2,1,0:T(8,128)(2,1)S(1)} collective-permute-done((bf16[8,24,3200]{2,1,0:T(8,128)(2,1)S(1)}, bf16[8,24,3200]{2,1,0:T(8,128)(2,1)S(1)}, u32[]{:S(2)}, u32[]{:S(2)}) %collective-permute-start.7) | collective-permute-done | bytes 1228832 | tf_op jit(solution)/shard_map/ppermute | solution.py:544
  288.0 2.4 collective-permute-start.9
  291.2 15.7 %project_back.1 = bf16[2048,768]{1,0:T(8,128)(2,1)} custom-call(bf16[2048,768]{1,0:T(8,128)(2,1)} %x_ref.5, f32[2048,768]{1,0:T(8,128)} %get-tuple-element.68.dm_ref, bf16[3,768,2048]{2,1,0:T(8,128)(2,1)} %get-tuple-element.59.g_ref, bf16[768,2432]{1,0:T(8,128)(2,1)} %get-tuple-element.54.ga_ref.w_ref), custom_call_target="tpu_custom_call" | custom-call | flops 7247757312 | bytes 31457280 | tf_op jit(solution)/shard_map/project_back/pallas_call | solution.py:416
  308.3 4.9 %collective-permute-start.11 = (bf16[24,6144]{1,0:T(8,128)(2,1)S(1)}, bf16[24,6144]{1,0:T(8,128)(2,1)S(1)}, u32[]{:S(2)}, u32[]{:S(2)}) collective-permute-start(bf16[24,6144]{1,0:T(8,128)(2,1)S(1)} %get-tuple-element.93), channel_id=1, source_target_pairs={{0,16},{8,24},{16,0},{24,8},{1,17},{9,25},{17,1},{25,9},{2,18},{10... | collective-permute-start | bytes 884744 | tf_op jit(solution)/shard_map/ppermute | solution.py:544
  313.2 7.8 %collective-permute-done.11.t_ref = bf16[24,6144]{1,0:T(8,128)(2,1)S(1)} collective-permute-done((bf16[24,6144]{1,0:T(8,128)(2,1)S(1)}, bf16[24,6144]{1,0:T(8,128)(2,1)S(1)}, u32[]{:S(2)}, u32[]{:S(2)}) %collective-permute-start.11) | collective-permute-done | bytes 294944 | tf_op jit(solution)/shard_map/ppermute | solution.py:544
  324.1 2.0 finish_feed_forward.1
  326.2 4.3 %collective-permute-done.12 = bf16[1,24,3200]{2,1,0:T(8,128)(2,1)S(1)} collective-permute-done((bf16[1,24,3200]{2,1,0:T(8,128)(2,1)S(1)}, bf16[1,24,3200]{2,1,0:T(8,128)(2,1)S(1)}, u32[]{:S(2)}, u32[]{:S(2)}) %collective-permute-start.12) | collective-permute-done | bytes 153632 | tf_op jit(solution)/shard_map/ppermute | solution.py:544
  331.1 1.9 finish_attention.1
  (49 shorter events, 16.3 us)
Async XLA Ops:
  7.2 102.0 %all-gather.2.cloned.1.call-start = ((), (), s32[]{:S(2)}) async-start(), calls=%async_computation.1 | async-start | bytes 10948608 | tf_op jit(solution)/shard_map/all_gather | solution.py:713
  9.1 277.7 %reduce-scatter.2.cloned.1.call-start = ((), (), s32[]{:S(2)}) async-start(), calls=%async_computation.2 | async-start | bytes 10616832 | tf_op jit(solution)/shard_map/reduce_scatter | solution.py:729
  10.9 9.9 %collective-permute-start = (bf16[1,24,2432]{2,1,0:T(8,128)(2,1)}, bf16[1,24,2432]{2,1,0:T(8,128)(2,1)S(1)}, u32[]{:S(2)}, u32[]{:S(2)}) collective-permute-start(bf16[1,24,2432]{2,1,0:T(8,128)(2,1)} %bitcast.23), channel_id=1, source_target_pairs={{0,16},{8,24},{16,0},{24,8},{1,17},{9,25},{17,1},{25,9},{2,18},{10... | collective-permute-start | bytes 350216 | tf_op jit(solution)/shard_map/ppermute | solution.py:544
  21.7 11.2 %collective-permute-start.1 = (bf16[2,24,2432]{2,1,0:T(8,128)(2,1)S(1)}, bf16[2,24,2432]{2,1,0:T(8,128)(2,1)S(1)}, u32[]{:S(2)}, u32[]{:S(2)}) collective-permute-start(bf16[2,24,2432]{2,1,0:T(8,128)(2,1)S(1)} %pad_maximum_fusion.2), channel_id=1, source_target_pairs={{0,8},{8,0},{16,24},{24,16},{1,9},{9,1},{17,25},{25,17},{2,10},{10... | collective-permute-start | bytes 700424 | tf_op jit(solution)/shard_map/ppermute | solution.py:544
  22.6 10.3 %copy-start.3 = (bf16[24,2432]{1,0:T(8,128)(2,1)S(1)}, bf16[24,2432]{1,0:T(8,128)(2,1)}, u32[]{:S(2)}) copy-start(bf16[24,2432]{1,0:T(8,128)(2,1)} %pack_attention.1) | copy-start | bytes 350212
  32.9 8.6 %collective-permute-start.2 = (bf16[4,24,2432]{2,1,0:T(8,128)(2,1)S(1)}, bf16[4,24,2432]{2,1,0:T(8,128)(2,1)S(1)}, u32[]{:S(2)}, u32[]{:S(2)}) collective-permute-start(bf16[4,24,2432]{2,1,0:T(8,128)(2,1)S(1)} %pad_maximum_fusion.1), channel_id=1, source_target_pairs={{0,2},{1,5},{2,0},{3,7},{4,6},{5,1},{6,4},{7,3},{8,10},{9,13},{10,... | collective-permute-start | bytes 1400840 | tf_op jit(solution)/shard_map/ppermute | solution.py:544
  41.7 22.7 %copy-start.2 = (bf16[8,24,2432]{2,1,0:T(8,128)(2,1)}, bf16[8,24,2432]{2,1,0:T(8,128)(2,1)S(1)}, u32[]{:S(2)}) copy-start(bf16[8,24,2432]{2,1,0:T(8,128)(2,1)S(1)} %pad_maximum_fusion.a_ref) | copy-start | bytes 2801668
  41.7 18.4 %collective-permute-start.3 = (bf16[8,24,2432]{2,1,0:T(8,128)(2,1)S(1)}, bf16[8,24,2432]{2,1,0:T(8,128)(2,1)S(1)}, u32[]{:S(2)}, u32[]{:S(2)}) collective-permute-start(bf16[8,24,2432]{2,1,0:T(8,128)(2,1)S(1)} %pad_maximum_fusion.a_ref), channel_id=1, source_target_pairs={{0,4},{1,3},{2,6},{3,1},{4,0},{5,7},{6,2},{7,5},{8,12},{9,11},{10,... | collective-permute-start | bytes 2801672 | tf_op jit(solution)/shard_map/ppermute | solution.py:544
  43.2 19.5 %collective-permute-start.4 = (bf16[8,24,2432]{2,1,0:T(8,128)(2,1)S(1)}, bf16[8,24,2432]{2,1,0:T(8,128)(2,1)S(1)}, u32[]{:S(2)}, u32[]{:S(2)}) collective-permute-start(bf16[8,24,2432]{2,1,0:T(8,128)(2,1)S(1)} %pad_maximum_fusion.a_ref), channel_id=1, source_target_pairs={{0,1},{1,0},{2,3},{3,2},{4,5},{5,4},{6,7},{7,6},{8,9},{9,8},{10,11... | collective-permute-start | bytes 2801672 | tf_op jit(solution)/shard_map/ppermute | solution.py:544
  60.1 4.3 %copy-start.5 = (bf16[8,24,2432]{2,1,0:T(8,128)(2,1)}, bf16[8,24,2432]{2,1,0:T(8,128)(2,1)S(1)}, u32[]{:S(2)}) copy-start(bf16[8,24,2432]{2,1,0:T(8,128)(2,1)S(1)} %collective-permute-done.3.b_ref) | copy-start | bytes 2801668
  60.1 4.3 %collective-permute-start.5 = (bf16[8,24,2432]{2,1,0:T(8,128)(2,1)S(1)}, bf16[8,24,2432]{2,1,0:T(8,128)(2,1)}, u32[]{:S(2)}, u32[]{:S(2)}) collective-permute-start(bf16[8,24,2432]{2,1,0:T(8,128)(2,1)S(1)} %collective-permute-done.3.b_ref), channel_id=1, source_target_pairs={{0,1},{1,0},{2,3},{3,2},{4,5},{5,4},{6,7},{7,6},{8,9},{9,8},{10,11... | collective-permute-start | bytes 2801672 | tf_op jit(solution)/shard_map/ppermute | solution.py:544
  62.7 1.7 copy-start.6
  194.8 55.4 %copy-start = (bf16[768,768]{1,0:T(8,128)(2,1)S(1)}, bf16[768,768]{1,0:T(8,128)(2,1)}, u32[]{:S(2)}) copy-start(bf16[768,768]{1,0:T(8,128)(2,1)} %get-tuple-element.60.wo_ref) | copy-start | bytes 3538948
  250.1 0.8 copy-start.1
  263.8 4.9 %collective-permute-start.6 = (bf16[16,24,3200]{2,1,0:T(8,128)(2,1)S(1)}, bf16[16,24,3200]{2,1,0:T(8,128)(2,1)S(1)}, u32[]{:S(2)}, u32[]{:S(2)}) collective-permute-start(bf16[16,24,3200]{2,1,0:T(8,128)(2,1)S(1)} %get-tuple-element.63), channel_id=1, source_target_pairs={{0,1},{1,0},{2,3},{3,2},{4,5},{5,4},{6,7},{7,6},{8,9},{9,8},{10,11... | collective-permute-start | bytes 7372808 | tf_op jit(solution)/shard_map/ppermute | solution.py:544
  269.3 17.2 %collective-permute-start.7 = (bf16[8,24,3200]{2,1,0:T(8,128)(2,1)S(1)}, bf16[8,24,3200]{2,1,0:T(8,128)(2,1)S(1)}, u32[]{:S(2)}, u32[]{:S(2)}) collective-permute-start(bf16[8,24,3200]{2,1,0:T(8,128)(2,1)S(1)} %get-tuple-element.90), channel_id=1, source_target_pairs={{0,2},{1,5},{2,0},{3,7},{4,6},{5,1},{6,4},{7,3},{8,10},{9,13},{10,... | collective-permute-start | bytes 3686408 | tf_op jit(solution)/shard_map/ppermute | solution.py:544
  288.0 19.5 %copy-start.4 = (bf16[96,6144]{1,0:T(8,128)(2,1)S(1)}, bf16[96,6144]{1,0:T(8,128)(2,1)}, u32[]{:S(2)}) copy-start(bf16[96,6144]{1,0:T(8,128)(2,1)} %reduce-scatter.2.cloned.1.call-done) | copy-start | bytes 3538948
  288.0 19.0 %collective-permute-start.9 = (bf16[2,24,6144]{2,1,0:T(8,128)(2,1)S(1)}, bf16[2,24,6144]{2,1,0:T(8,128)(2,1)S(1)}, u32[]{:S(2)}, u32[]{:S(2)}) collective-permute-start(bf16[2,24,6144]{2,1,0:T(8,128)(2,1)S(1)} %slice.69), channel_id=1, source_target_pairs={{0,8},{8,0},{16,24},{24,16},{1,9},{9,1},{17,25},{25,17},{2,10},{10... | collective-permute-start | bytes 1769480 | tf_op jit(solution)/shard_map/ppermute | solution.py:544
  290.4 16.6 %collective-permute-start.8 = (bf16[4,24,3200]{2,1,0:T(8,128)(2,1)S(1)}, bf16[4,24,3200]{2,1,0:T(8,128)(2,1)S(1)}, u32[]{:S(2)}, u32[]{:S(2)}) collective-permute-start(bf16[4,24,3200]{2,1,0:T(8,128)(2,1)S(1)} %get-tuple-element.67), channel_id=1, source_target_pairs={{0,4},{1,3},{2,6},{3,1},{4,0},{5,7},{6,2},{7,5},{8,12},{9,11},{10,... | collective-permute-start | bytes 1843208 | tf_op jit(solution)/shard_map/ppermute | solution.py:544
  307.1 14.9 %collective-permute-start.10 = (bf16[2,24,3200]{2,1,0:T(8,128)(2,1)S(1)}, bf16[2,24,3200]{2,1,0:T(8,128)(2,1)S(1)}, u32[]{:S(2)}, u32[]{:S(2)}) collective-permute-start(bf16[2,24,3200]{2,1,0:T(8,128)(2,1)S(1)} %get-tuple-element.95), channel_id=1, source_target_pairs={{0,8},{8,0},{16,24},{24,16},{1,9},{9,1},{17,25},{25,17},{2,10},{10... | collective-permute-start | bytes 921608 | tf_op jit(solution)/shard_map/ppermute | solution.py:544
  308.3 12.7 %collective-permute-start.11 = (bf16[24,6144]{1,0:T(8,128)(2,1)S(1)}, bf16[24,6144]{1,0:T(8,128)(2,1)S(1)}, u32[]{:S(2)}, u32[]{:S(2)}) collective-permute-start(bf16[24,6144]{1,0:T(8,128)(2,1)S(1)} %get-tuple-element.93), channel_id=1, source_target_pairs={{0,16},{8,24},{16,0},{24,8},{1,17},{9,25},{17,1},{25,9},{2,18},{10... | collective-permute-start | bytes 884744 | tf_op jit(solution)/shard_map/ppermute | solution.py:544
  321.0 3.1 copy-start.7
  322.7 7.8 %collective-permute-start.12 = (bf16[1,24,3200]{2,1,0:T(8,128)(2,1)S(1)}, bf16[1,24,3200]{2,1,0:T(8,128)(2,1)S(1)}, u32[]{:S(2)}, u32[]{:S(2)}) collective-permute-start(bf16[1,24,3200]{2,1,0:T(8,128)(2,1)S(1)} %get-tuple-element.97), channel_id=1, source_target_pairs={{0,16},{8,24},{16,0},{24,8},{1,17},{9,25},{17,1},{25,9},{2,18},{10... | collective-permute-start | bytes 460808 | tf_op jit(solution)/shard_map/ppermute | solution.py:544
  330.5 0.7 copy-start.8
Sparse Core Ops, SparseCore 0:
  10.9 98.0 all-gather.1
  194.8 80.6 reduce-scatter.1
